TPU v7x, 32 devices: a whole 2x2x4 slice. The times are simulated.
32 devices in a mesh: dp: 16 (over z, y, core), tensor: 2 (over x).
Axes of the slice: x: 2, y: 2, z: 4, core: 2. Of those that a mesh axis runs over, the one named last changes fastest.
Arguments:
- features: bfloat16 [32, 1024, 768], P(('dp', 'tensor')), may hold values from -6 to 6
- lengths: int32 [32], P(('dp', 'tensor')), may hold values from 512 to 1024, as said below
- span_starts: int32 [32, 8], P(('dp', 'tensor')), may hold values from 0 to 1014, as said below
- buckets: int32 [2047], replicated, may hold values from 0 to 319
- cotangent: bfloat16 [32, 1024, 768], P(('dp', 'tensor')), may hold values from -6 to 6
- qkv_w: float32 [3, 768, 768], P(None, 'dp'), may hold values from -0.21875 to 0.21875
- qkv_m: float32 [3, 768, 768], P(None, 'dp'), may hold values from -0.00061035156 to 0.00061035156
- qkv_v: float32 [3, 768, 768], P(None, 'dp'), may hold values from 1.409991e-09 to 2.2559856e-08
- out_w: float32 [768, 768], P('dp'), may hold values from -3 to 3
- out_m: float32 [768, 768], P('dp'), may hold values from -7.6293945e-05 to 7.6293945e-05
- out_v: float32 [768, 768], P('dp'), may hold values from 2.819982e-11 to 4.229973e-10
- ffn_in: float32 [769, 3072], P(None, ('dp', 'tensor')), may hold values from -0.21875 to 0.21875
- ffn_in_m: float32 [769, 3072], P(None, ('dp', 'tensor')), may hold values from -0.00061035156 to 0.00061035156
- ffn_in_v: float32 [769, 3072], P(None, ('dp', 'tensor')), may hold values from 1.409991e-09 to 2.2559856e-08
- ffn_out: float32 [3072, 768], P(('dp', 'tensor')), may hold values from -0.109375 to 0.109375
- ffn_out_m: float32 [3072, 768], P(('dp', 'tensor')), may hold values from -0.00061035156 to 0.00061035156
- ffn_out_v: float32 [3072, 768], P(('dp', 'tensor')), may hold values from 1.409991e-09 to 2.2559856e-08
- small_params: float32 [9, 768], replicated, may hold values from -4 to 4, as said below
- small_m: float32 [9, 768], replicated, may hold values from -0.0012207031 to 0.0012207031
- small_v: float32 [9, 768], replicated, may hold values from 5.639964e-09 to 9.0239425e-08
- pos_table: float32 [321, 12], replicated, may hold values from -4 to 4
- pos_m: float32 [321, 12], replicated, may hold values from -0.0012207031 to 0.0012207031
- pos_v: float32 [321, 12], replicated, may hold values from 5.639964e-09 to 9.0239425e-08
- gate_proj: float32 [65, 8], replicated, may hold values from -0.75 to 0.75
- gate_m: float32 [65, 8], replicated, may hold values from -0.0012207031 to 0.0012207031
- gate_v: float32 [65, 8], replicated, may hold values from 5.639964e-09 to 9.0239425e-08
- step_count: int32 [1], replicated, may hold values from 1 to 4
Outputs:
- layer_out: float32 [32, 1024, 768], P(('dp', 'tensor'))
- feature_grad: float32 [32, 1024, 768], P(('dp', 'tensor'))
- grad_norm: float32 [1], replicated
- qkv_new: float32 [3, 768, 768], P(None, 'dp')
- qkv_moment: float32 [3, 768, 768], P(None, 'dp')
- qkv_second: float32 [3, 768, 768], P(None, 'dp')
- qkv_copy: bfloat16 [3, 768, 768], P(None, 'dp')
- out_new: float32 [768, 768], P('dp')
- out_moment: float32 [768, 768], P('dp')
- out_second: float32 [768, 768], P('dp')
- out_copy: bfloat16 [768, 768], P('dp')
- ffn_in_new: float32 [769, 3072], P(None, ('dp', 'tensor'))
- ffn_in_moment: float32 [769, 3072], P(None, ('dp', 'tensor'))
- ffn_in_second: float32 [769, 3072], P(None, ('dp', 'tensor'))
- ffn_in_copy: bfloat16 [769, 3072], P(None, ('dp', 'tensor'))
- ffn_out_new: float32 [3072, 768], P(('dp', 'tensor'))
- ffn_out_moment: float32 [3072, 768], P(('dp', 'tensor'))
- ffn_out_second: float32 [3072, 768], P(('dp', 'tensor'))
- ffn_out_copy: bfloat16 [3072, 768], P(('dp', 'tensor'))
- small_grad: float32 [9, 768], replicated
- small_new: float32 [9, 768], replicated
- small_moment: float32 [9, 768], replicated
- small_second: float32 [9, 768], replicated
- pos_new: float32 [321, 12], replicated
- pos_moment: float32 [321, 12], replicated
- pos_second: float32 [321, 12], replicated
- gate_new: float32 [65, 8], replicated
- gate_moment: float32 [65, 8], replicated
- gate_second: float32 [65, 8], replicated
Inputs may be any that keep to these rules, and one draw needn't show every extreme that they name: `lengths`: every length is at least half of 1024; the first utterance is full in every draw. `span_starts`: each start is at most its utterance's length minus 10; spans may intersect. buckets[o] is the bucket of relative offset o - 1023. `small_params`: gains (rows 3 and 5) lie between 0.7 and 1.3.
All inputs are finite; a program needn't handle non-finite values.
Results may differ from a plain program's by a relative error of at most 0.02.
Values may be sent and summed in bfloat16 or wider, within the bound.
No kernel may reach another device: no remote copies, remote signals or barrier semaphores. Data moves between devices by JAX's collectives and lax.ppermute only.
A program may use at most 320 MiB of HBM per device.

v0:
```python
import jax
import jax.numpy as jnp
from jax import lax
from jax.sharding import PartitionSpec as P

D = 768
H = 12
HD = 64
FF = 3072
NB = 320
SPAN = 10


PRECISE = lax.Precision.HIGHEST
CLIP_NORM = 1.0
BETA_ONE = 0.9
BETA_TWO = 0.98
ADAM_EPS = 1e-08
DECAY_RATE = 0.01
NORM_EPS = 1e-05
NEG_BIG = -1e30


def layer_norm(rows_in, gain_row, shift_row):
    row_mean = jnp.mean(rows_in, axis=-1, keepdims=True)
    centred = rows_in - row_mean
    inv_std = lax.rsqrt(jnp.mean(centred * centred, axis=-1, keepdims=True) + NORM_EPS)
    return centred * inv_std * gain_row + shift_row


def gelu_exact(values_in):
    return jax.nn.gelu(values_in, approximate=False)


def gate_of(heads_in, gate_proj, gate_const):
    logits = jnp.einsum("lhd,de->lhe", heads_in, gate_proj[:-1], precision=PRECISE) + gate_proj[-1]
    gate_one = jax.nn.sigmoid(jnp.sum(logits[..., :4], axis=-1))
    gate_two = jax.nn.sigmoid(jnp.sum(logits[..., 4:], axis=-1))
    return gate_one * (gate_two * gate_const - 1.0) + 2.0


def toeplitz_rows(window, row_count, col_count):
    head_count, wide = window.shape
    tiled = jnp.tile(window, (1, row_count + 1))
    skewed = tiled[:, row_count - 1 : row_count - 1 + row_count * (wide - 1)]
    return skewed.reshape(head_count, row_count, wide - 1)[:, :, :col_count]


def diagonal_sums(block_in):
    head_count, row_count, col_count = block_in.shape
    width = col_count + row_count
    padded = jnp.pad(block_in, ((0, 0), (0, 0), (0, row_count)))
    flat = jnp.pad(padded.reshape(head_count, row_count * width), ((0, 0), (row_count - 1, 1)))
    skewed = flat.reshape(head_count, row_count, width + 1)
    return jnp.sum(skewed, axis=1)[:, : col_count + row_count - 1]


def contract_rows(left, right):
    return lax.dot_general(
        left, right, (((0,), (0,)), ((), ())), preferred_element_type=jnp.float32
    )


def times_trans(left, right):
    return lax.dot_general(
        left, right, (((1,), (1,)), ((), ())), preferred_element_type=jnp.float32
    )


def adam_step(weight, grad_in, moment, second, clip_factor, rate_in, count_in):
    scaled = grad_in * clip_factor
    new_moment = BETA_ONE * moment + (1.0 - BETA_ONE) * scaled
    new_second = BETA_TWO * second + (1.0 - BETA_TWO) * scaled * scaled
    first_fix = 1.0 - BETA_ONE**count_in
    second_fix = 1.0 - BETA_TWO**count_in
    update = new_moment / first_fix / (jnp.sqrt(new_second / second_fix) + ADAM_EPS)
    return (weight - rate_in * (update + DECAY_RATE * weight), new_moment, new_second)


def local(
    features,
    lengths,
    span_starts,
    buckets,
    cotangent,
    qkv_w,
    qkv_m,
    qkv_v,
    out_w,
    out_m,
    out_v,
    ffn_in,
    ffn_in_m,
    ffn_in_v,
    ffn_out,
    ffn_out_m,
    ffn_out_v,
    small_params,
    small_m,
    small_v,
    pos_table,
    pos_m,
    pos_v,
    gate_proj,
    gate_m,
    gate_v,
    step_count,
):
    utt_count = features.shape[0]
    seq_len = features.shape[1]
    frames = utt_count * seq_len
    query_rows = min(512, seq_len)
    blocks = seq_len // query_rows
    window_len = seq_len + query_rows - 1
    query_scale = HD ** (-0.5)
    positions = jnp.arange(seq_len, dtype=jnp.int32)
    inside = (positions[None, :, None] >= span_starts[:, None, :]) & (
        positions[None, :, None] < span_starts[:, None, :] + SPAN
    )
    masked = jnp.any(inside, axis=2)
    masked_rows = masked.reshape(frames, 1)
    mixed_in = jnp.where(masked[:, :, None], small_params[8], features.astype(jnp.float32)).reshape(
        frames, D
    )
    rounded = mixed_in.astype(jnp.bfloat16)
    qkv_all, out_all = (
        lax.all_gather(qkv_w.astype(jnp.bfloat16), "dp", axis=1, tiled=True),
        lax.all_gather(out_w.astype(jnp.bfloat16), "dp", axis=0, tiled=True),
    )
    w_in, w_out = (
        lax.all_gather(ffn_in.astype(jnp.bfloat16), "dp", axis=1, tiled=True),
        lax.all_gather(ffn_out.astype(jnp.bfloat16), "dp", axis=0, tiled=True),
    )
    projected = jnp.einsum("fi,kio->kfo", rounded, qkv_all, preferred_element_type=jnp.float32)
    queries = (
        ((projected[0] + small_params[0]) * query_scale)
        .astype(jnp.bfloat16)
        .reshape(utt_count, seq_len, H, HD)
    )
    keys_all = projected[1].astype(jnp.bfloat16).reshape(utt_count, seq_len, H, HD)
    values_all = (
        (projected[2] + small_params[1]).astype(jnp.bfloat16).reshape(utt_count, seq_len, H, HD)
    )
    heads_in = rounded.astype(jnp.float32).reshape(frames, H, HD)
    gate_vals, gate_back = jax.vjp(gate_of, heads_in, gate_proj, pos_table[NB])
    gates_utt = gate_vals.reshape(utt_count, seq_len, H)
    onehot_t = (jnp.arange(NB, dtype=jnp.int32)[:, None] == buckets[None, :]).astype(jnp.float32)
    offsets_t = lax.dot_general(
        pos_table[:NB], onehot_t, (((0,), (0,)), ((), ())), precision=PRECISE
    )

    def pieces(item_id):
        utt_index = item_id // blocks
        row_start = item_id % blocks * query_rows
        query_block = lax.dynamic_slice_in_dim(
            lax.dynamic_index_in_dim(queries, utt_index, 0, False), row_start, query_rows, 0
        )
        keys_utt = lax.dynamic_index_in_dim(keys_all, utt_index, 0, False)
        values_utt = lax.dynamic_index_in_dim(values_all, utt_index, 0, False)
        gate_block = lax.dynamic_slice_in_dim(
            lax.dynamic_index_in_dim(gates_utt, utt_index, 0, False), row_start, query_rows, 0
        )
        window_start = seq_len - query_rows - row_start
        window = lax.dynamic_slice_in_dim(offsets_t, window_start, window_len, 1)
        relative = toeplitz_rows(window, query_rows, seq_len)
        product = jnp.einsum(
            "ihd,jhd->hij", query_block, keys_utt, preferred_element_type=jnp.float32
        )
        scores = product + jnp.transpose(gate_block)[:, :, None] * relative
        valid_cols = positions < lax.dynamic_index_in_dim(lengths, utt_index, 0, False)
        scores = jnp.where(valid_cols[None, None, :], scores, NEG_BIG)
        return (
            utt_index,
            row_start,
            window_start,
            query_block,
            keys_utt,
            values_utt,
            gate_block,
            relative,
            scores,
        )

    def attend(item_id):
        block_parts = pieces(item_id)
        scores = block_parts[8]
        row_max = jnp.max(scores, axis=-1, keepdims=True)
        exp_scores = jnp.exp(scores - row_max)
        row_total = jnp.sum(exp_scores, axis=-1, keepdims=True)
        prob_vals = (exp_scores / row_total).astype(jnp.bfloat16)
        context_block = jnp.einsum(
            "hij,jhd->ihd", prob_vals, block_parts[5], preferred_element_type=jnp.float32
        ).astype(jnp.bfloat16)
        return (context_block, (row_max + jnp.log(row_total))[:, :, 0])

    item_ids = jnp.arange(utt_count * blocks, dtype=jnp.int32)
    contexts, lse_all = lax.map(attend, item_ids)
    context = contexts.reshape(frames, D)
    attention = jnp.dot(context, out_all, preferred_element_type=jnp.float32) + small_params[2]
    first_out, norm_one_back = jax.vjp(
        layer_norm, mixed_in + attention, small_params[3], small_params[4]
    )
    first_low = first_out.astype(jnp.bfloat16)
    gathered = lax.all_gather(first_low, "tensor", axis=0, tiled=True)
    hidden = jnp.dot(gathered, w_in[:D], preferred_element_type=jnp.float32) + w_in[D]
    active_f, gelu_back = jax.vjp(gelu_exact, hidden)
    active = active_f.astype(jnp.bfloat16)
    branch = (
        lax.psum_scatter(
            jnp.dot(active, w_out, preferred_element_type=jnp.float32).astype(jnp.bfloat16),
            "tensor",
            scatter_dimension=0,
            tiled=True,
        ).astype(jnp.float32)
        + small_params[7]
    )
    second_out, norm_two_back = jax.vjp(
        layer_norm, first_out + branch, small_params[5], small_params[6]
    )
    layer_out = second_out.reshape(utt_count, seq_len, D)
    valid_rows = (positions[None, :] < lengths[:, None]).astype(jnp.float32)
    cot_rows = (cotangent.astype(jnp.float32) * valid_rows[:, :, None]).reshape(frames, D)
    d_res2, d_gain2, d_shift2 = norm_two_back(cot_rows)
    d_branch = d_res2.astype(jnp.bfloat16)
    d_bias_out = jnp.sum(d_branch.astype(jnp.float32), axis=0)
    d_gathered = lax.all_gather(d_branch, "tensor", axis=0, tiled=True)
    d_active = times_trans(d_gathered, w_out)
    d_hidden = gelu_back(d_active)[0].astype(jnp.bfloat16)
    d_first = d_res2 + lax.psum_scatter(
        times_trans(d_hidden, w_in[:D]).astype(jnp.bfloat16),
        "tensor",
        scatter_dimension=0,
        tiled=True,
    ).astype(jnp.float32)
    g_outw_local = contract_rows(active, d_gathered)
    g_in_local = jnp.concatenate(
        [contract_rows(gathered, d_hidden), jnp.sum(d_hidden.astype(jnp.float32), axis=0)[None, :]],
        axis=0,
    )
    d_res1, d_gain1, d_shift1 = norm_one_back(d_first)
    d_attention = d_res1.astype(jnp.bfloat16)
    d_bias_attn = jnp.sum(d_attention.astype(jnp.float32), axis=0)
    g_out_local = contract_rows(context, d_attention)
    d_context = (
        times_trans(d_attention, out_all).astype(jnp.bfloat16).reshape(utt_count, seq_len, H, HD)
    )

    def attend_back(carry, item_id):
        key_acc, value_acc, offset_acc = carry
        (
            utt_index,
            row_start,
            window_start,
            query_block,
            keys_utt,
            values_utt,
            gate_block,
            relative,
            scores,
        ) = pieces(item_id)
        lse_block = lax.dynamic_index_in_dim(lse_all, item_id, 0, False)
        dctx_block = lax.dynamic_slice_in_dim(
            lax.dynamic_index_in_dim(d_context, utt_index, 0, False), row_start, query_rows, 0
        )
        prob_vals = jnp.exp(scores - lse_block[:, :, None])
        d_probs = jnp.einsum(
            "ihd,jhd->hij", dctx_block, values_utt, preferred_element_type=jnp.float32
        )
        row_delta = jnp.sum(d_probs * prob_vals, axis=-1, keepdims=True)
        d_scores = (prob_vals * (d_probs - row_delta)).astype(jnp.bfloat16)
        d_query = jnp.einsum(
            "hij,jhd->ihd", d_scores, keys_utt, preferred_element_type=jnp.float32
        ).astype(jnp.bfloat16)
        d_key = jnp.einsum(
            "hij,ihd->jhd", d_scores, query_block, preferred_element_type=jnp.float32
        )
        d_value = jnp.einsum(
            "hij,ihd->jhd",
            prob_vals.astype(jnp.bfloat16),
            dctx_block,
            preferred_element_type=jnp.float32,
        )
        d_scores_f = d_scores.astype(jnp.float32)
        d_gate = jnp.transpose(jnp.sum(d_scores_f * relative, axis=-1))
        d_window = diagonal_sums(d_scores_f * jnp.transpose(gate_block)[:, :, None])
        key_acc = lax.dynamic_update_index_in_dim(
            key_acc, lax.dynamic_index_in_dim(key_acc, utt_index, 0, False) + d_key, utt_index, 0
        )
        value_acc = lax.dynamic_update_index_in_dim(
            value_acc,
            lax.dynamic_index_in_dim(value_acc, utt_index, 0, False) + d_value,
            utt_index,
            0,
        )
        offset_acc = lax.dynamic_update_slice_in_dim(
            offset_acc,
            lax.dynamic_slice_in_dim(offset_acc, window_start, window_len, 1) + d_window,
            window_start,
            1,
        )
        return ((key_acc, value_acc, offset_acc), (d_query, d_gate))

    carry_init = (
        jnp.zeros((utt_count, seq_len, H, HD), jnp.float32),
        jnp.zeros((utt_count, seq_len, H, HD), jnp.float32),
        jnp.zeros((H, 2 * seq_len - 1), jnp.float32),
    )
    (key_grad, value_grad, offset_grad), (query_grads, gate_grads) = lax.scan(
        attend_back, carry_init, item_ids
    )
    d_queries = query_grads.reshape(frames, D) * query_scale
    d_keys = key_grad.astype(jnp.bfloat16).reshape(frames, D)
    d_values = value_grad.astype(jnp.bfloat16).reshape(frames, D)
    stacked = jnp.stack([d_queries, d_keys, d_values])
    g_qkv_local = jnp.einsum("fi,kfo->kio", rounded, stacked, preferred_element_type=jnp.float32)
    d_heads, g_gate_local, d_const = gate_back(gate_grads.reshape(frames, H))
    d_mixed = (
        d_res1
        + jnp.einsum("kfo,kio->fi", stacked, qkv_all, preferred_element_type=jnp.float32)
        + d_heads.reshape(frames, D)
    )
    feature_grad = jnp.where(masked_rows, 0.0, d_mixed).reshape(utt_count, seq_len, D)
    d_mask_vec = jnp.sum(jnp.where(masked_rows, d_mixed, 0.0), axis=0)
    d_bias_query = jnp.sum(d_queries.astype(jnp.float32), axis=0)
    d_bias_value = jnp.sum(d_values.astype(jnp.float32), axis=0)
    small_local = jnp.stack(
        [
            d_bias_query,
            d_bias_value,
            d_bias_attn,
            d_gain1,
            d_shift1,
            d_gain2,
            d_shift2,
            d_bias_out,
            d_mask_vec,
        ]
    )
    pos_main = lax.dot_general(onehot_t, offset_grad, (((1,), (1,)), ((), ())), precision=PRECISE)
    pos_local = jnp.concatenate([pos_main, d_const[None, :]], axis=0)
    g_qkv, g_out, g_in, g_outw = (
        lax.psum_scatter(
            g_qkv_local.astype(jnp.bfloat16), "dp", scatter_dimension=1, tiled=True
        ).astype(jnp.float32),
        lax.psum_scatter(
            g_out_local.astype(jnp.bfloat16), "dp", scatter_dimension=0, tiled=True
        ).astype(jnp.float32),
        lax.psum_scatter(
            g_in_local.astype(jnp.bfloat16), "dp", scatter_dimension=1, tiled=True
        ).astype(jnp.float32),
        lax.psum_scatter(
            g_outw_local.astype(jnp.bfloat16), "dp", scatter_dimension=0, tiled=True
        ).astype(jnp.float32),
    )
    g_qkv, g_out = (
        lax.psum(g_qkv.astype(jnp.bfloat16), "tensor").astype(jnp.float32),
        lax.psum(g_out.astype(jnp.bfloat16), "tensor").astype(jnp.float32),
    )
    g_small, g_pos, g_gate = lax.psum((small_local, pos_local, g_gate_local), ("dp", "tensor"))
    own_attn = jnp.sum(g_qkv * g_qkv) + jnp.sum(g_out * g_out)
    own_sum = (
        jnp.where(lax.axis_index("tensor") == 0, own_attn, 0.0)
        + jnp.sum(g_in * g_in)
        + jnp.sum(g_outw * g_outw)
    )
    shared = jnp.sum(g_small * g_small) + jnp.sum(g_pos * g_pos) + jnp.sum(g_gate * g_gate)
    grad_norm = jnp.sqrt(lax.psum(own_sum, ("dp", "tensor")) + shared)
    clip_factor = jnp.minimum(1.0, CLIP_NORM / (grad_norm + 1e-06))
    count_in = step_count[0].astype(jnp.float32)
    qkv_new, qkv_moment, qkv_second = adam_step(
        qkv_w, g_qkv, qkv_m, qkv_v, clip_factor, 2.0 * D ** (-0.5), count_in
    )
    out_new, out_moment, out_second = adam_step(
        out_w, g_out, out_m, out_v, clip_factor, 1.0, count_in
    )
    ffn_in_new, ffn_in_moment, ffn_in_second = adam_step(
        ffn_in, g_in, ffn_in_m, ffn_in_v, clip_factor, 2.0 * D ** (-0.5), count_in
    )
    ffn_out_new, ffn_out_moment, ffn_out_second = adam_step(
        ffn_out, g_outw, ffn_out_m, ffn_out_v, clip_factor, 2.0 * FF ** (-0.5), count_in
    )
    small_new, small_moment, small_second = adam_step(
        small_params, g_small, small_m, small_v, clip_factor, 0.5, count_in
    )
    pos_new, pos_moment, pos_second = adam_step(
        pos_table, g_pos, pos_m, pos_v, clip_factor, 1.0, count_in
    )
    gate_new, gate_moment, gate_second = adam_step(
        gate_proj, g_gate, gate_m, gate_v, clip_factor, 2.0 * HD ** (-0.5), count_in
    )
    return (
        layer_out,
        feature_grad,
        grad_norm.reshape(1),
        qkv_new,
        qkv_moment,
        qkv_second,
        qkv_new.astype(jnp.bfloat16),
        out_new,
        out_moment,
        out_second,
        out_new.astype(jnp.bfloat16),
        ffn_in_new,
        ffn_in_moment,
        ffn_in_second,
        ffn_in_new.astype(jnp.bfloat16),
        ffn_out_new,
        ffn_out_moment,
        ffn_out_second,
        ffn_out_new.astype(jnp.bfloat16),
        g_small,
        small_new,
        small_moment,
        small_second,
        pos_new,
        pos_moment,
        pos_second,
        gate_new,
        gate_moment,
        gate_second,
    )


def solution(mesh):
    in_specs = (
        P(("dp", "tensor"), None, None),
        P(("dp", "tensor")),
        P(("dp", "tensor"), None),
        P(),
        P(("dp", "tensor"), None, None),
        P(None, "dp", None),
        P(None, "dp", None),
        P(None, "dp", None),
        P("dp", None),
        P("dp", None),
        P("dp", None),
        P(None, ("dp", "tensor")),
        P(None, ("dp", "tensor")),
        P(None, ("dp", "tensor")),
        P(("dp", "tensor"), None),
        P(("dp", "tensor"), None),
        P(("dp", "tensor"), None),
        P(),
        P(),
        P(),
        P(),
        P(),
        P(),
        P(),
        P(),
        P(),
        P(),
    )
    out_specs = (
        P(("dp", "tensor"), None, None),
        P(("dp", "tensor"), None, None),
        P(),
        P(None, "dp", None),
        P(None, "dp", None),
        P(None, "dp", None),
        P(None, "dp", None),
        P("dp", None),
        P("dp", None),
        P("dp", None),
        P("dp", None),
        P(None, ("dp", "tensor")),
        P(None, ("dp", "tensor")),
        P(None, ("dp", "tensor")),
        P(None, ("dp", "tensor")),
        P(("dp", "tensor"), None),
        P(("dp", "tensor"), None),
        P(("dp", "tensor"), None),
        P(("dp", "tensor"), None),
        P(),
        P(),
        P(),
        P(),
        P(),
        P(),
        P(),
        P(),
        P(),
        P(),
    )
    return jax.shard_map(local, mesh=mesh, in_specs=in_specs, out_specs=out_specs, check_vma=False)
```

profile of v0, /device:TPU:0, one launch (start us, length us, event | category | flops | bytes accessed | tf_op | source)
XLA Modules:
  0.0 2321.4 jit_solution(8115044679986107699)
XLA Ops:
  24.1 36.8 %all-gather.7.cloned.1.call-done = bf16[3,768,768]{2,1,0:T(8,128)(2,1)} async-done(((bf16[3,48,768]{2,1,0:T(8,128)(2,1)}), bf16[3,768,768]{2,1,0:T(8,128)(2,1)}) %all-gather.7.cloned.1.call-update) | async-done | bytes 3538960 | tf_op jit(solution)/shard_map/all_gather | solution.py:127
  71.4 493.8 %while.36 = (s32[]{:T(128)}, bf16[2,512,12,64]{1,3,2,0:T(8,128)(2,1)}, f32[2,12,512]{2,1,0:T(8,128)}, s32[1]{0:T(128)}, s32[2]{0:T(128)S(1)}, /*index=5*/bf16[1,...) while((s32[]{:T(128)}, ...), condition=%wide.region_6.7_spmd.clone, body=%wide.region_3.6_spmd.clone.sunk | while | flops 1667623936 | bytes 388974720 | solution.py:197
  101.8 61.9 %tile.33 = f32[12,787455]{1,0:T(8,128)} reshape(f32[12,513,1535]{2,1,0:T(8,128)} %tile.32) | data formatting | bytes 75595680 | tf_op jit(solution)/shard_map/while/body/eval_jaxpr/tile | solution.py:44
  163.7 38.2 %slice.176 = f32[12,785408]{1,0:T(8,128)} slice(f32[12,787455]{1,0:T(8,128)} %tile.33), slice={[0:12], [511:785919]} | slice | bytes 75399168 | tf_op jit(solution)/shard_map/while/body/eval_jaxpr/slice | solution.py:45
  202.0 78.3 %reshape.584 = f32[12,512,1534]{2,1,0:T(8,128)} reshape(f32[12,785408]{1,0:T(8,128)} %slice.176) | data formatting | bytes 75399168 | tf_op jit(solution)/shard_map/while/body/eval_jaxpr/reshape | solution.py:46
  340.7 61.4 %tile.33 = f32[12,787455]{1,0:T(8,128)} reshape(f32[12,513,1535]{2,1,0:T(8,128)} %tile.32) | data formatting | bytes 75595680 | tf_op jit(solution)/shard_map/while/body/eval_jaxpr/tile | solution.py:44
  402.0 38.2 %slice.176 = f32[12,785408]{1,0:T(8,128)} slice(f32[12,787455]{1,0:T(8,128)} %tile.33), slice={[0:12], [511:785919]} | slice | bytes 75399168 | tf_op jit(solution)/shard_map/while/body/eval_jaxpr/slice | solution.py:45
  440.3 78.3 %reshape.584 = f32[12,512,1534]{2,1,0:T(8,128)} reshape(f32[12,785408]{1,0:T(8,128)} %slice.176) | data formatting | bytes 75399168 | tf_op jit(solution)/shard_map/while/body/eval_jaxpr/reshape | solution.py:46
  579.7 42.0 %all-gather.11.cloned.1.call-done = bf16[2048,768]{0,1:T(8,128)(2,1)} async-done(((bf16[1024,768]{0,1:T(8,128)(2,1)}), bf16[2048,768]{0,1:T(8,128)(2,1)}) %all-gather.11.cloned.1.call-update) | async-done | bytes 3145744 | tf_op jit(solution)/shard_map/all_gather | solution.py:204
  621.7 35.9 %multiply_convert_fusion.1 = (bf16[2048,1536]{1,0:T(8,128)(2,1)}, f32[2048,1536]{1,0:T(8,128)}, f32[2048,1536]{1,0:T(8,128)}) fusion(f32[1536]{0:T(1024)S(1)} %convert_reduce_fusion.4, bf16[2048,768]{0,1:T(8,128)(2,1)} %all-gather.11.cloned.1.call-done, bf16[769,1536]{0,1:T(8,128)(2,1)} %all-gather.13.cloned.1.call-done), kind=kOutput, calls=%fused_computation.61 | convolution fusion | flops 5039456256 | bytes 36968448 | tf_op jit(solution)/shard_map/dot_general | solution.py:205
  679.2 38.8 %reduce-scatter.8.cloned.1.call-done = bf16[1024,768]{0,1:T(8,128)(2,1)} async-done(((bf16[2048,768]{0,1:T(8,128)(2,1)}), bf16[1024,768]{0,1:T(8,128)(2,1)}) %reduce-scatter.8.cloned.1.call-update) | async-done | bytes 1572880 | tf_op jit(solution)/shard_map/reduce_scatter | solution.py:209
  730.2 45.0 %all-gather.17.cloned.1.call-done = bf16[2048,768]{0,1:T(8,128)(2,1)} async-done(((bf16[1024,768]{0,1:T(8,128)(2,1)}), bf16[2048,768]{0,1:T(8,128)(2,1)}) %all-gather.17.cloned.1.call-update) | async-done | bytes 3145744 | tf_op jit(solution)/shard_map/all_gather | solution.py:226
  864.1 1143.6 %while.37 = (s32[]{:T(128)}, f32[1,1024,12,64]{1,3,2,0:T(8,128)}, f32[1,1024,12,64]{1,3,2,0:T(8,128)}, f32[12,2047]{1,0:T(8,128)}, bf16[2,512,12,64]{1,3,2,0:T(8...) while((s32[]{:T(128)}, f32[1,1024,12,64]{1,3,2,0:T(8,128)}, ...), condition=%wide.region_21.22_spmd.clone, body=%wide.region_17.21_spmd.clone.sunk | while | flops 4132301824 | bytes 1098917632 | solution.py:308
  884.9 62.0 %tile.35 = f32[12,787455]{1,0:T(8,128)} reshape(f32[12,513,1535]{2,1,0:T(8,128)} %tile.34) | data formatting | bytes 75595680 | tf_op jit(solution)/shard_map/while/body/eval_jaxpr/tile | solution.py:44
  946.9 38.5 %slice.180 = f32[12,785408]{1,0:T(8,128)} slice(f32[12,787455]{1,0:T(8,128)} %tile.35), slice={[0:12], [511:785919]} | slice | bytes 75399168 | tf_op jit(solution)/shard_map/while/body/eval_jaxpr/slice | solution.py:45
  985.4 86.4 %reshape.585 = f32[12,512,1534]{2,1,0:T(8,128)} reshape(f32[12,785408]{1,0:T(8,128)} %slice.180) | data formatting | bytes 75399168 | tf_op jit(solution)/shard_map/while/body/eval_jaxpr/reshape | solution.py:46
  1122.0 28.6 %fusion.192 = (f32[12,512]{1,0:T(8,128)S(1)}, bf16[12,512,1024]{2,1,0:T(8,128)(2,1)}) fusion(f32[12,512,1534]{2,1,0:T(8,128)} %reshape.585, f32[12,512,1024]{2,1,0:T(8,128)} %subtract_exponential_fusion.3, f32[12,512,1024]{2,1,0:T(8,128)} %get-tuple-element.901, f32[12,512]{1,0:T(8,128)S(1)} %get-tuple-element.902), kind=kLoop, calls=%fused_computation.23.clone.1 | loop fusion | flops 37742592 | bytes 88129536 | tf_op jit(solution)/shard_map/while/body/eval_jaxpr/reduce_sum | solution.py:284
  1202.7 29.9 %pad.82 = f32[16,512,1536]{2,1,0:T(8,128)} pad(f32[12,512,1536]{2,1,0:T(8,128)} %pad.81, f32[]{:T(128)} %constant.311.clone.1..sunk), padding=0_4x0_0x0_0 | pad | bytes 88080384 | tf_op jit(solution)/shard_map/while
  1232.7 46.1 %copy.307 = f32[2,8,512,1536]{3,1,2,0:T(8,128)} copy(f32[2,8,512,1536]{3,2,1,0:T(8,128)} %bitcast.276) | data formatting | bytes 100663296 | tf_op jit(solution)/shard_map/while
  1278.8 37.8 %pad.83 = f32[12,786944]{1,0:T(8,128)} pad(f32[12,786432]{1,0:T(8,128)} %bitcast.277, f32[]{:T(128)} %constant.311.clone.1..sunk), padding=0_0x511_1 | pad | bytes 75522048 | tf_op jit(solution)/shard_map/while/body/eval_jaxpr/jit(_pad)/pad | solution.py:53
  1316.6 92.1 %reshape.586 = f32[12,512,1537]{2,1,0:T(8,128)} reshape(f32[12,786944]{1,0:T(8,128)} %pad.83) | data formatting | bytes 75546624 | tf_op jit(solution)/shard_map/while/body/eval_jaxpr/reshape | solution.py:54
  1459.0 61.4 %tile.35 = f32[12,787455]{1,0:T(8,128)} reshape(f32[12,513,1535]{2,1,0:T(8,128)} %tile.34) | data formatting | bytes 75595680 | tf_op jit(solution)/shard_map/while/body/eval_jaxpr/tile | solution.py:44
  1520.3 38.2 %slice.180 = f32[12,785408]{1,0:T(8,128)} slice(f32[12,787455]{1,0:T(8,128)} %tile.35), slice={[0:12], [511:785919]} | slice | bytes 75399168 | tf_op jit(solution)/shard_map/while/body/eval_jaxpr/slice | solution.py:45
  1558.6 86.4 %reshape.585 = f32[12,512,1534]{2,1,0:T(8,128)} reshape(f32[12,785408]{1,0:T(8,128)} %slice.180) | data formatting | bytes 75399168 | tf_op jit(solution)/shard_map/while/body/eval_jaxpr/reshape | solution.py:46
  1695.2 28.6 %fusion.192 = (f32[12,512]{1,0:T(8,128)S(1)}, bf16[12,512,1024]{2,1,0:T(8,128)(2,1)}) fusion(f32[12,512,1534]{2,1,0:T(8,128)} %reshape.585, f32[12,512,1024]{2,1,0:T(8,128)} %subtract_exponential_fusion.3, f32[12,512,1024]{2,1,0:T(8,128)} %get-tuple-element.901, f32[12,512]{1,0:T(8,128)S(1)} %get-tuple-element.902), kind=kLoop, calls=%fused_computation.23.clone.1 | loop fusion | flops 37742592 | bytes 88129536 | tf_op jit(solution)/shard_map/while/body/eval_jaxpr/reduce_sum | solution.py:284
  1776.0 29.9 %pad.82 = f32[16,512,1536]{2,1,0:T(8,128)} pad(f32[12,512,1536]{2,1,0:T(8,128)} %pad.81, f32[]{:T(128)} %constant.311.clone.1..sunk), padding=0_4x0_0x0_0 | pad | bytes 88080384 | tf_op jit(solution)/shard_map/while
  1805.9 46.1 %copy.307 = f32[2,8,512,1536]{3,1,2,0:T(8,128)} copy(f32[2,8,512,1536]{3,2,1,0:T(8,128)} %bitcast.276) | data formatting | bytes 100663296 | tf_op jit(solution)/shard_map/while
  1852.0 37.8 %pad.83 = f32[12,786944]{1,0:T(8,128)} pad(f32[12,786432]{1,0:T(8,128)} %bitcast.277, f32[]{:T(128)} %constant.311.clone.1..sunk), padding=0_0x511_1 | pad | bytes 75522048 | tf_op jit(solution)/shard_map/while/body/eval_jaxpr/jit(_pad)/pad | solution.py:53
  1889.9 92.1 %reshape.586 = f32[12,512,1537]{2,1,0:T(8,128)} reshape(f32[12,786944]{1,0:T(8,128)} %pad.83) | data formatting | bytes 75546624 | tf_op jit(solution)/shard_map/while/body/eval_jaxpr/reshape | solution.py:54
  2081.3 77.0 %all-reduce.12.cloned.1.call-done = bf16[3,768,768]{2,0,1:T(4,128)(2,1)} async-done(((bf16[3,768,768]{2,0,1:T(4,128)(2,1)}), bf16[3,768,768]{2,0,1:T(4,128)(2,1)}) %all-reduce.12.cloned.1.call-update) | async-done | bytes 3538960
  2160.1 60.4 %reduce-scatter.12.cloned.1.call-done = bf16[48,768]{1,0:T(8,128)(2,1)} async-done(((bf16[768,768]{1,0:T(8,128)(2,1)}), bf16[48,768]{1,0:T(8,128)(2,1)}) %reduce-scatter.12.cloned.1.call-update) | async-done | bytes 73744 | tf_op jit(solution)/shard_map/reduce_scatter | solution.py:345
  2255.8 40.4 %all-reduce.7 = (f32[]{:T(128)}, f32[9,768]{1,0:T(8,128)S(1)}, f32[321,12]{0,1:T(8,128)S(1)}, f32[65,8]{0,1:T(8,128)S(1)}) all-reduce(f32[]{:T(128)S(6)} %add.519, f32[9,768]{1,0:T(8,128)S(1)} %stack.32, f32[321,12]{0,1:T(8,128)S(1)} %pad_maximum_fusion.6, ...), channel_id=1, replica_groups=mesh['dp'=16,'tensor'=2] {'dp','tensor'}, use_global_device_ids=true, to_apply=%region_33.34 | all-reduce | flops 11285 | bytes 90280 | tf_op jit(solution)/shard_map/psum | solution.py:367
  (405 shorter events, 674.1 us)
Async XLA Ops:
  7.2 12.8 copy-start.79
  7.2 12.0 copy-start.30
  7.2 53.7 %all-gather.7.cloned.1.call-start = ((), (), s32[]{:S(2)}) async-start(), calls=%async_computation.5 | async-start | bytes 3760128 | tf_op jit(solution)/shard_map/all_gather | solution.py:127
  9.1 561.9 %all-gather.9.cloned.1.call-start = ((), (), s32[]{:S(2)}) async-start(), calls=%async_computation.6 | async-start | bytes 1253376 | tf_op jit(solution)/shard_map/all_gather | solution.py:128
  10.8 567.8 %all-gather.13.cloned.1.call-start = ((), (), s32[]{:S(2)}) async-start(), calls=%async_computation.8 | async-start | bytes 2924544 | tf_op jit(solution)/shard_map/all_gather | solution.py:131
  12.5 609.2 %all-gather.11.cloned.1.call-start = ((), (), s32[]{:S(2)}) async-start(), calls=%async_computation.7 | async-start | bytes 4718592 | tf_op jit(solution)/shard_map/all_gather | solution.py:204
  16.7 44.2 %copy-start.60 = (f32[768]{0:T(1024)}, f32[768]{0:T(1024)S(1)}, u32[]{:S(2)}) copy-start(f32[768]{0:T(1024)S(1)} %get-tuple-element.622) | copy-start | bytes 9220
  19.9 40.9 %copy-start.21 = (bf16[1,1024,768]{1,2,0:T(8,128)(2,1)}, bf16[1,1024,768]{1,2,0:T(8,128)(2,1)S(1)}, u32[]{:S(2)}) copy-start(bf16[1,1024,768]{1,2,0:T(8,128)(2,1)S(1)} %copy.227) | copy-start | bytes 4718596
  20.1 47.0 %copy-start.75 = (pred[1024]{0:T(1024)(128)(4,1)}, pred[1024]{0:T(1024)(128)(4,1)S(1)}, u32[]{:S(2)}) copy-start(pred[1024]{0:T(1024)(128)(4,1)S(1)} %fusion.102) | copy-start | bytes 3076
  577.7 89.0 %all-gather.15.cloned.1.call-start = ((), (), s32[]{:S(2)}) async-start(), calls=%async_computation.9 | async-start | bytes 2506752 | tf_op jit(solution)/shard_map/all_gather | solution.py:132
  578.5 139.6 %reduce-scatter.8.cloned.1.call-start = ((), (), s32[]{:S(2)}) async-start(), calls=%async_computation.10 | async-start | bytes 4718592 | tf_op jit(solution)/shard_map/reduce_scatter | solution.py:209
  675.7 42.3 %copy-start.64 = (f32[768]{0:T(1024)S(1)}, f32[768]{0:T(1024)}, u32[]{:S(2)}) copy-start(f32[768]{0:T(1024)} %get-tuple-element.616) | copy-start | bytes 9220
  675.8 99.4 %all-gather.17.cloned.1.call-start = ((), (), s32[]{:S(2)}) async-start(), calls=%async_computation.11 | async-start | bytes 4718592 | tf_op jit(solution)/shard_map/all_gather | solution.py:226
  679.2 44.2 %copy-start.51 = (f32[1024]{0:T(1024)}, f32[1024]{0:T(1024)S(1)}, u32[]{:S(2)}) copy-start(f32[1024]{0:T(1024)S(1)} %fusion.108) | copy-start | bytes 12292
  730.1 117.0 %reduce-scatter.10.cloned.1.call-start = ((), (), s32[]{:S(2)}) async-start(), calls=%async_computation.12 | async-start | bytes 4718592 | tf_op jit(solution)/shard_map/reduce_scatter | solution.py:229
  775.2 19.1 copy-start.55
  803.6 1247.2 %reduce-scatter.14.cloned.1.call-start = ((), (), s32[]{:S(2)}) async-start(), calls=%async_computation.14 | async-start | bytes 2506752 | tf_op jit(solution)/shard_map/reduce_scatter | solution.py:351
  813.4 1239.0 %reduce-scatter.16.cloned.1.call-start = ((), (), s32[]{:S(2)}) async-start(), calls=%async_computation.15 | async-start | bytes 2924544
  827.6 24.0 %copy-start.59 = (f32[1024]{0:T(1024)S(1)}, f32[1024]{0:T(1024)}, u32[]{:S(2)}) copy-start(f32[1024]{0:T(1024)} %copy-done.58) | copy-start | bytes 12292
  827.6 1330.7 %all-reduce.12.cloned.1.call-start = ((), (), s32[]{:S(2)}) async-start(), calls=%async_computation.16 | async-start | bytes 9437184
  1092.2 13.4 copy-start.13
  1408.7 15.7 copy-start.26
  1408.7 17.1 copy-start.5
  1408.7 17.1 copy-start.10
  1665.5 13.4 copy-start.13
  1982.0 15.7 copy-start.26
  1982.0 17.2 copy-start.5
  1982.0 17.2 copy-start.10
  2041.1 179.4 %reduce-scatter.12.cloned.1.call-start = ((), (), s32[]{:S(2)}) async-start(), calls=%async_computation.13 | async-start | bytes 1253376 | tf_op jit(solution)/shard_map/reduce_scatter | solution.py:345
  2064.7 181.8 %all-reduce.14.cloned.1.call-start = ((), (), s32[]{:S(2)}) async-start(), calls=%async_computation.17 | async-start | bytes 589824 | tf_op jit(solution)/shard_map/psum | solution.py:356
  2068.5 11.4 copy-start.17
  2077.8 142.8 %copy-start.28 = (f32[12,2047]{1,0:T(8,128)S(1)}, f32[12,2047]{1,0:T(8,128)}, u32[]{:S(2)}) copy-start(f32[12,2047]{1,0:T(8,128)} %get-tuple-element.1064) | copy-start | bytes 294772
  (75 other events, 412.2 us)
Sparse Core Ops, SparseCore 0:
  10.9 49.9 all-gather.6
  63.7 37.3 all-gather.8
  104.0 42.5 all-gather.12
  577.8 43.8 all-gather.10
  624.4 42.2 all-gather.14
  675.9 42.1 reduce-scatter.7
  730.2 44.9 all-gather.16
  803.8 43.3 reduce-scatter.9
  850.9 62.9 reduce-scatter.13
  918.0 63.4 reduce-scatter.15
  2041.2 117.0 all-reduce.11
  2162.8 57.6 reduce-scatter.11
  2223.6 22.8 all-reduce.13
where the time goes:
time: 2330 us; the launch traced here: 2320 us
  local copies, waits for them, and re-layouts  1340 us (58%)
  waiting for transfers between devices  353 us (15%)
  matrix products  331 us (14%)
  other arithmetic  186 us (8%)
  loops' own time  49.1 us (2%)
  blocking collectives  40.4 us (2%)
  between operations  23.5 us (1%)
    reshape x4, local copies, waits for them, and re-layouts, toeplitz_rows(): return skewed.reshape(head_count, row_count, wide - 1)[:, :, :col_count]  329 us
    another operation x8, local copies, waits for them, and re-layouts, toeplitz_rows(): tiled = jnp.tile(window, (1, row_count + 1))  298 us
    reshape x2, local copies, waits for them, and re-layouts, diagonal_sums(): skewed = flat.reshape(head_count, row_count, width + 1)  184 us
    while x48, local copies, waits for them, and re-layouts  156 us
    slice x4, local copies, waits for them, and re-layouts, toeplitz_rows(): skewed = tiled[:, row_count - 1:row_count - 1 + row_count * (wide - 1)]  153 us
    dot_general x4, matrix products, pieces(): jnp.einsum('ihd,jhd->hij', query_block, keys_utt, preferred_element_type=...  80.2 us
    unnamed x15, waiting for transfers between devices  77.2 us
    pad x2, local copies, waits for them, and re-layouts, diagonal_sums(): jnp.pad(padded.reshape(head_count, row_count * width), ((0, 0), (row_coun...  75.7 us
  transfers between devices with their start and end apart: 13, of which 9 were waited for; matrix products, arithmetic and copies ran while one was open for 76% of the time, Pallas kernels for 0%

commit v1 on v0

v1 whole, which is shorter than its diff:
```python
import functools

import jax
import jax.numpy as jnp
from jax import lax
from jax.experimental import pallas as pl
from jax.experimental.pallas import tpu as pltpu
from jax.sharding import PartitionSpec as P

D = 768
H = 12
HD = 64
FF = 3072
NB = 320
SPAN = 10
CLIP_NORM = 1.0
BETA_ONE = 0.9
BETA_TWO = 0.98
ADAM_EPS = 1e-08
DECAY_RATE = 0.01
NORM_EPS = 1e-05
NEG_BIG = -1e30


def adam_step(weight, grad_in, moment, second, clip_factor, rate_in, count_in):
    scaled = grad_in * clip_factor
    new_moment = BETA_ONE * moment + (1.0 - BETA_ONE) * scaled
    new_second = BETA_TWO * second + (1.0 - BETA_TWO) * scaled * scaled
    first_fix = 1.0 - BETA_ONE**count_in
    second_fix = 1.0 - BETA_TWO**count_in
    update = new_moment / first_fix / (jnp.sqrt(new_second / second_fix) + ADAM_EPS)
    return (weight - rate_in * (update + DECAY_RATE * weight), new_moment, new_second)


NT=(((1,),(1,)),((),()))
TN=(((0,),(0,)),((),()))
def dot(a,b,dims=(((1,),(0,)),((),()))):
    return lax.dot_general(a,b,dims,preferred_element_type=jnp.float32)

def toep_kernel(off_ref, out_ref):
    row=jnp.broadcast_to(off_ref[0], out_ref.shape[1:])
    out_ref[0]=pltpu.roll(row, 0, 1, stride=1, stride_axis=0)

def toep(offr):
    n,w=offr.shape[0],offr.shape[-1]
    return pl.pallas_call(toep_kernel, grid=(n,),
        in_specs=[pl.BlockSpec((1,1,w),lambda h:(h,0,0))],
        out_specs=pl.BlockSpec((1,128,w),lambda h:(h,0,0)),
        out_shape=jax.ShapeDtypeStruct((n,128,w),jnp.float32))(offr.reshape(n,1,w))

def fwd_kernel(len_ref, q_ref,k_ref,v_ref,t_ref,g_ref,p_ref,o_ref,rl_ref,s_ref, *, seq, ib):
    h=pl.program_id(0)
    par=lax.rem(h,2)
    lane=lax.broadcasted_iota(jnp.int32,(seq,128),1)
    rowi=lax.broadcasted_iota(jnp.int32,(seq,128),0)
    inh=(lane//64)==par
    flag=lane==(64*(1-par))
    one=jnp.bfloat16(1.0); zero=jnp.bfloat16(0.0)
    bias=jnp.where(rowi<len_ref[0],0.0,NEG_BIG).astype(jnp.bfloat16)
    qm=jnp.where(flag,one,jnp.where(inh,q_ref[0],zero))
    km=jnp.where(flag,bias,k_ref[0])
    vm=jnp.where(flag,one,v_ref[0])
    vt=vm.T
    nb=seq//128
    base=seq-128
    for i0 in range(0,seq,ib):
        gate=g_ref[0,:,i0:i0+ib]
        qb=qm[i0:i0+ib]
        m=None
        for jb in range(nb):
            j0=jb*128
            c0=i0-j0+base
            s=dot(km[j0:j0+128],qb,NT)+t_ref[0,:,c0:c0+ib]*gate
            s_ref[j0:j0+128,:]=s
            mm=jnp.max(s.reshape(16,8,ib),axis=0)
            m=mm if m is None else jnp.maximum(m,mm)
        m=jnp.max(m,axis=0,keepdims=True)
        for jb in range(nb):
            j0=jb*128
            e=jnp.exp(s_ref[j0:j0+128,:]-m).astype(jnp.bfloat16)
            p_ref[0,j0:j0+128,i0:i0+ib]=e
        ct=dot(vt,p_ref[0,:,i0:i0+ib])
        l=jnp.where(par==0,ct[64:65],ct[0:1])
        rl=1.0/l
        oc=(ct*rl).T
        rc=jnp.broadcast_to(rl,(128,ib)).T
        ih=inh[i0:i0+ib]
        o_ref[i0:i0+ib,:]=jnp.where(ih,oc.astype(jnp.bfloat16),o_ref[i0:i0+ib,:])
        rl_ref[i0:i0+ib,:]=jnp.where(ih,rc,rl_ref[i0:i0+ib,:])

def attn_fwd(length,qkv,t2,gates,ib=256):
    seq=qkv.shape[1]; w=t2.shape[-1]
    return pl.pallas_call(functools.partial(fwd_kernel,seq=seq,ib=ib),
        grid_spec=pltpu.PrefetchScalarGridSpec(num_scalar_prefetch=1,grid=(H,),
        in_specs=[pl.BlockSpec((1,seq,128),lambda h,l:(0,0,h//2)),
                  pl.BlockSpec((1,seq,128),lambda h,l:(1,0,h//2)),
                  pl.BlockSpec((1,seq,128),lambda h,l:(2,0,h//2)),
                  pl.BlockSpec((1,128,w),lambda h,l:(h,0,0)),
                  pl.BlockSpec((1,1,seq),lambda h,l:(h,0,0))],
        out_specs=[pl.BlockSpec((1,seq,seq),lambda h,l:(h,0,0)),
                   pl.BlockSpec((seq,128),lambda h,l:(0,h//2)),
                   pl.BlockSpec((seq,128),lambda h,l:(0,h//2))],
        scratch_shapes=[pltpu.VMEM((seq,ib),jnp.float32)]),
        out_shape=[jax.ShapeDtypeStruct((H,seq,seq),jnp.bfloat16),
                   jax.ShapeDtypeStruct((seq,D),jnp.bfloat16),
                   jax.ShapeDtypeStruct((seq,D),jnp.float32)],
        compiler_params=pltpu.CompilerParams(vmem_limit_bytes=50<<20),
        )(length,qkv,qkv,qkv,t2,gates)

def bwd_kernel(q_ref,k_ref,v_ref,dc_ref,c_ref,p_ref,t_ref,g_ref,dq_ref,dk_ref,dv_ref,dg_ref,do_ref,a_ref,ds_ref,*,seq,ib):
    h=pl.program_id(0)
    par=lax.rem(h,2)
    lane=lax.broadcasted_iota(jnp.int32,(seq,128),1)
    inh=(lane//64)==par
    f0=lane==(64*(1-par))
    f1=lane==(64*(1-par)+1)
    one=jnp.bfloat16(1.0)
    dc=dc_ref[...]
    dcf=jnp.where(inh,dc.astype(jnp.float32),0.0)
    delta=-jnp.sum(dcf*c_ref[...].astype(jnp.float32),axis=1,keepdims=True)
    hi=delta.astype(jnp.bfloat16).astype(jnp.float32)
    lo=delta-hi
    dca=jnp.where(f0,hi,jnp.where(f1,lo,dcf)).astype(jnp.bfloat16)
    va=jnp.where(f0|f1,one,v_ref[0])
    kt=k_ref[0].T
    q=q_ref[0]
    nb=seq//128
    base=seq-128
    a_ref[...]=jnp.zeros_like(a_ref)
    for i0 in range(0,seq,ib):
        gate=g_ref[0,:,i0:i0+ib]
        dcb=dca[i0:i0+ib]
        dg=jnp.zeros((8,ib),jnp.float32)
        for jb in range(nb):
            j0=jb*128
            c0=i0-j0+base
            ds=dot(va[j0:j0+128],dcb,NT)*p_ref[0,j0:j0+128,i0:i0+ib].astype(jnp.float32)
            ds_ref[j0:j0+128,i0:i0+ib]=ds.astype(jnp.bfloat16)
            dg=dg+jnp.sum((ds*t_ref[0,:,c0:c0+ib]).reshape(16,8,ib),axis=0)
            a_ref[:,c0:c0+ib]+=ds*gate
        dg_ref[0,:,i0:i0+ib]=jnp.sum(dg,axis=0,keepdims=True)
        dqt=dot(kt,ds_ref[:,i0:i0+ib])
        dq_ref[i0:i0+ib,:]=jnp.where(inh[i0:i0+ib],dqt.T.astype(jnp.bfloat16),dq_ref[i0:i0+ib,:])
    dk=dot(ds_ref[...],q)
    dk_ref[...]=jnp.where(inh,dk.astype(jnp.bfloat16),dk_ref[...])
    dv=dot(p_ref[0],dc)
    dv_ref[...]=jnp.where(inh,dv.astype(jnp.bfloat16),dv_ref[...])
    a=a_ref[...]
    w=a.shape[1]
    r=64
    while r>=8:
        a=a[:r]+pltpu.roll(a[r:],w-r,1)
        r//=2
    acc=a[0:1]
    for r in range(1,8):
        acc=acc+pltpu.roll(a[r:r+1],w-r,1)
    do_ref[0]=acc

def attn_bwd(qkv,dctx,ctx,p,t2,gates,ib=256):
    seq=qkv.shape[1]; w=t2.shape[-1]
    pairb=pl.BlockSpec((seq,128),lambda h:(0,h//2))
    return pl.pallas_call(functools.partial(bwd_kernel,seq=seq,ib=ib),
        grid=(H,),
        in_specs=[pl.BlockSpec((1,seq,128),lambda h:(0,0,h//2)),
                  pl.BlockSpec((1,seq,128),lambda h:(1,0,h//2)),
                  pl.BlockSpec((1,seq,128),lambda h:(2,0,h//2)),
                  pairb,pairb,
                  pl.BlockSpec((1,seq,seq),lambda h:(h,0,0)),
                  pl.BlockSpec((1,128,w),lambda h:(h,0,0)),
                  pl.BlockSpec((1,1,seq),lambda h:(h,0,0))],
        out_specs=[pairb,pairb,pairb,
                   pl.BlockSpec((1,1,seq),lambda h:(h,0,0)),
                   pl.BlockSpec((1,1,w),lambda h:(h,0,0))],
        scratch_shapes=[pltpu.VMEM((128,w),jnp.float32),pltpu.VMEM((seq,seq),jnp.bfloat16)],
        out_shape=[jax.ShapeDtypeStruct((seq,D),jnp.bfloat16)]*3+[
                   jax.ShapeDtypeStruct((H,1,seq),jnp.float32),
                   jax.ShapeDtypeStruct((H,1,w),jnp.float32)],
        compiler_params=pltpu.CompilerParams(vmem_limit_bytes=50<<20),
        )(qkv,qkv,qkv,dctx,ctx,p,t2,gates)


def gelu_both(x):
    half = 0.5 * (1.0 + lax.erf(x * 0.7071067811865476))
    dens = jnp.exp(-0.5 * x * x) * 0.3989422804014327
    return x * half, half + x * dens


def split3(x):
    hi = x.astype(jnp.bfloat16)
    rest = x - hi.astype(jnp.float32)
    mid = rest.astype(jnp.bfloat16)
    low = (rest - mid.astype(jnp.float32)).astype(jnp.bfloat16)
    return hi, mid, low


def tree_sum(parts):
    while len(parts) > 1:
        half = len(parts) // 2
        parts = [parts[i] + parts[i + half] for i in range(half)]
    return parts[0]


def norm_rows(r):
    mean = jnp.mean(r, axis=-1, keepdims=True)
    cen = r - mean
    inv = lax.rsqrt(jnp.mean(cen * cen, axis=-1, keepdims=True) + NORM_EPS)
    return cen * inv, inv


def norm_back(cot, n, inv, gain):
    e = cot * gain
    return inv * (
        e - jnp.mean(e, axis=-1, keepdims=True) - n * jnp.mean(e * n, axis=-1, keepdims=True)
    )


class Net:
    def __init__(self, dp_size, t_size):
        self.t = t_size
        self.sizes = {"z": dp_size // 4, "y": 2, "c": 2, "x": t_size}
        d = lax.axis_index("dp")
        self.at = {"z": d // 4, "y": d // 2 % 2, "c": d % 2, "x": lax.axis_index("tensor")}

    def shift(self, v, axis, k):
        pairs = []
        sz = self.sizes
        for z in range(sz["z"]):
            for y in range(2):
                for c in range(2):
                    for x in range(sz["x"]):
                        src = {"z": z, "y": y, "c": c, "x": x}
                        dst = dict(src)
                        dst[axis] = (src[axis] - k) % sz[axis]
                        flat = [((q["z"] * 2 + q["y"]) * 2 + q["c"]) * sz["x"] + q["x"] for q in (src, dst)]
                        pairs.append(tuple(flat))
        return lax.ppermute(v, ("dp", "tensor"), pairs)

    def gather(self, v, axis, dim):
        return jnp.concatenate([v] + [self.shift(v, axis, k) for k in range(1, self.sizes[axis])], axis=dim)

    def scatter(self, v, axis, dim):
        n = self.sizes[axis]
        total = lax.index_in_dim(v, 0, dim, False).astype(jnp.float32)
        for k in range(1, n):
            total += self.shift(lax.index_in_dim(v, k, dim, False), axis, n - k).astype(jnp.float32)
        return total.astype(jnp.bfloat16)

    def scatter_own(self, v, axis, dim):
        n = self.sizes[axis]
        at = self.at[axis]
        total = lax.dynamic_index_in_dim(v, at, dim, False).astype(jnp.float32)
        for k in range(1, n):
            part = lax.dynamic_index_in_dim(v, (at + k) % n, dim, False)
            total += self.shift(part, axis, n - k).astype(jnp.float32)
        return total.astype(jnp.bfloat16)

    def gather_own(self, v, axis, dim):
        n = self.sizes[axis]
        at = self.at[axis]
        out = jnp.zeros(v.shape[:dim] + (n,) + v.shape[dim:], v.dtype)
        for k in range(n):
            part = v if k == 0 else self.shift(v, axis, k)
            out = lax.dynamic_update_index_in_dim(out, part, (at + k) % n, dim)
        return out

    def total(self, v):
        for axis in ("c", "x", "y", "z"):
            v = tree_sum([v] + [self.shift(v, axis, k) for k in range(1, self.sizes[axis])])
        return v


def local(dp_size, t_size, features, lengths, span_starts, buckets, cotangent,
          qkv_w, qkv_m, qkv_v, out_w, out_m, out_v, ffn_in, ffn_in_m, ffn_in_v,
          ffn_out, ffn_out_m, ffn_out_v, small_params, small_m, small_v,
          pos_table, pos_m, pos_v, gate_proj, gate_m, gate_v, step_count):
    f32, b16 = jnp.float32, jnp.bfloat16
    net = Net(dp_size, t_size)
    zs = net.sizes["z"]
    seq = features.shape[1]
    own = ffn_out.shape[0]
    rows = qkv_w.shape[1]
    scale = HD**-0.5

    attn_own = jnp.concatenate([qkv_w, out_w[None]], axis=0).astype(b16)
    attn_z = net.gather_own(attn_own, "z", 0)
    attn_y = net.gather_own(attn_z, "y", 1)
    attn_c = net.gather_own(attn_y, "c", 2)
    attn_all = attn_c.transpose(3, 0, 1, 2, 4, 5).reshape(4, D, D)
    qkv_all, out_all = attn_all[:3], attn_all[3]

    w_in_own = ffn_in[:D].T.astype(b16)
    w_out_own = ffn_out.astype(b16)
    b_in_own = ffn_in[D:].astype(b16).astype(f32)
    w_in_half = net.gather(net.gather(net.gather(w_in_own[None, None, None], "z", 2), "y", 1), "x", 0)
    w_out_half = net.gather(net.gather(net.gather(w_out_own[None, None, None], "z", 2), "x", 0), "y", 1)
    b_in_half = net.gather(net.gather(net.gather(b_in_own[None, None], "z", 2), "y", 1), "x", 0)
    w_in = [w_in_half.reshape(-1, D), net.shift(w_in_half, "c", 1).reshape(-1, D)]
    w_out = [w_out_half.reshape(-1, D), net.shift(w_out_half, "c", 1).reshape(-1, D)]
    b_in = [b_in_half.reshape(-1), net.shift(b_in_half, "c", 1).reshape(-1)]

    positions = jnp.arange(seq, dtype=jnp.int32)
    starts = span_starts[0]
    masked = jnp.any((positions[:, None] >= starts[None, :]) & (positions[:, None] < starts[None, :] + SPAN), axis=1)[:, None]
    mixed = jnp.where(masked, small_params[8][None, :], features[0].astype(f32))
    rounded = mixed.astype(b16)

    ga = jnp.sum(gate_proj[:HD, :4], axis=1)
    gb = jnp.sum(gate_proj[:HD, 4:], axis=1)
    za = jnp.sum(gate_proj[HD, :4])
    zb = jnp.sum(gate_proj[HD, 4:])
    eye = jnp.eye(H, dtype=f32)[:, :, None]
    wg = jnp.concatenate([(eye * ga).reshape(H, D), (eye * gb).reshape(H, D)], axis=0)
    wg3 = split3(wg)
    z3 = dot(jnp.concatenate(wg3, axis=0), rounded, NT).reshape(3, 2 * H, seq)
    z_all = z3[0] + z3[1] + z3[2]
    gate_a = jax.nn.sigmoid(z_all[:H] + za)
    gate_b = jax.nn.sigmoid(z_all[H:] + zb)
    const = pos_table[NB][:, None]
    gates = (gate_a * (gate_b * const - 1.0) + 2.0).reshape(H, 1, seq)

    rev = jnp.flip(buckets)
    order = jnp.concatenate([rev[127:], jnp.full((1,), -1, jnp.int32), rev[:127]])
    onehot = (jnp.arange(NB, dtype=jnp.int32)[:, None] == order[None, :]).astype(b16)
    off3 = dot(jnp.concatenate(split3(pos_table[:NB].T), axis=0), onehot).reshape(3, H, 2 * seq)
    table = toep(off3[0] + off3[1] + off3[2])

    proj = jnp.einsum("fi,kio->kfo", rounded, qkv_all, preferred_element_type=f32)
    bias3 = jnp.stack([small_params[0], jnp.zeros((D,), f32), small_params[1]])[:, None, :]
    scale3 = jnp.array([scale, 1.0, 1.0], f32)[:, None, None]
    qkv = ((proj + bias3) * scale3).astype(b16)
    probs, context, inv_sum = attn_fwd(lengths, qkv, table, gates)
    attention = dot(context, out_all) + small_params[2]
    n1, inv1 = norm_rows(mixed + attention)
    first = n1 * small_params[3] + small_params[4]
    first_low = first.astype(b16)

    active, slope = [], []
    for half in range(2):
        hid = dot(first_low, w_in[half], NT) + b_in[half]
        act, slo = gelu_both(hid)
        active.append(act.astype(b16))
        slope.append(slo.astype(b16))
    branch = dot(active[0], w_out[0]) + dot(active[1], w_out[1]) + small_params[7]
    n2, inv2 = norm_rows(first + branch)
    layer_out = n2 * small_params[5] + small_params[6]

    cot = jnp.where((positions < lengths[0])[:, None], cotangent[0].astype(f32), 0.0)
    d_gain2 = jnp.sum(cot * n2, axis=0)
    d_shift2 = jnp.sum(cot, axis=0)
    d_res2 = norm_back(cot, n2, inv2, small_params[5])
    d_branch = d_res2.astype(b16)
    d_bias_out = jnp.sum(d_branch.astype(f32), axis=0)
    shape_rel = (t_size, 2, zs, own, D)
    g_outw_peer = dot(active[1], d_branch, TN).astype(b16)
    g_outw_mine = dot(active[0], d_branch, TN).astype(b16)
    g_outw = (g_outw_mine.astype(f32) + net.shift(g_outw_peer, "c", 1).astype(f32)).astype(b16).reshape(shape_rel)
    g_outw = net.scatter(net.scatter(net.scatter(g_outw, "y", 1), "x", 0), "z", 0).astype(f32)
    d_hidden = [(dot(d_branch, w_out[h], NT) * slope[h].astype(f32)).astype(b16) for h in range(2)]
    d_first = d_res2 + (dot(d_hidden[0], w_in[0]) + dot(d_hidden[1], w_in[1]))
    g_in_peer = dot(d_hidden[1], first_low, TN).astype(b16)
    g_in_mine = dot(d_hidden[0], first_low, TN).astype(b16)
    g_in = (g_in_mine.astype(f32) + net.shift(g_in_peer, "c", 1).astype(f32)).astype(b16).reshape(shape_rel)
    g_in = net.scatter(net.scatter(net.scatter(g_in, "x", 0), "y", 0), "z", 0).astype(f32)
    g_bias_in = jnp.stack([jnp.sum(d.astype(f32), axis=0) for d in d_hidden]).reshape(2, t_size, 2, zs, own)
    for dim, axis in enumerate(("c", "x", "y", "z")):
        g_bias_in = jnp.roll(g_bias_in, net.at[axis], dim)
    g_bias_in = g_bias_in.transpose(3, 2, 0, 1, 4).reshape(-1, own)

    d_gain1 = jnp.sum(d_first * n1, axis=0)
    d_shift1 = jnp.sum(d_first, axis=0)
    d_res1 = norm_back(d_first, n1, inv1, small_params[3])
    d_attention = d_res1.astype(b16)
    d_bias_attn = jnp.sum(d_attention.astype(f32), axis=0)
    g_out_local = dot(context, d_attention, TN).astype(b16)
    d_context = (dot(d_attention, out_all, NT) * inv_sum).astype(b16)

    dq, dk, dv, dgate, doff = attn_bwd(qkv, d_context, context, probs, table, gates)
    dq = dq * scale
    g_qkv_local = [dot(rounded, d, TN).astype(b16) for d in (dq, dk, dv)]
    dgate = dgate.reshape(H, seq)
    d_a = dgate * (gate_b * const - 1.0) * gate_a * (1.0 - gate_a)
    d_b = dgate * gate_a * const * gate_b * (1.0 - gate_b)
    d_const = jnp.sum(dgate * gate_a * gate_b, axis=1)
    dz = jnp.concatenate([d_a, d_b], axis=0)
    dz_hi = dz.astype(b16)
    dz_lo = (dz - dz_hi.astype(f32)).astype(b16)
    d_heads = dot(jnp.concatenate([dz_hi, dz_lo, dz_hi], axis=0),
                  jnp.concatenate([wg3[0], wg3[0], wg3[1]], axis=0), TN)
    d_mixed = (d_res1 + dot(dq, qkv_all[0], NT) + dot(dk, qkv_all[1], NT) + dot(dv, qkv_all[2], NT) + d_heads)
    feature_grad = jnp.where(masked, 0.0, d_mixed)
    d_mask = jnp.sum(jnp.where(masked, d_mixed, 0.0), axis=0)
    g_z2 = dot(jnp.concatenate([dz_hi, dz_lo], axis=0), rounded).reshape(2, 2, H, H, HD)
    g_z = jnp.sum((g_z2[0] + g_z2[1]) * eye, axis=(1, 2))
    g_zb = jnp.sum(dz.reshape(2, H * seq), axis=1)
    g_gate_local = jnp.repeat(jnp.concatenate([g_z, g_zb[:, None]], axis=1).T, 4, axis=1)
    pos3 = dot(onehot, jnp.concatenate(split3(doff.reshape(H, 2 * seq)), axis=0), NT).reshape(NB, 3, H)
    pos_local = jnp.concatenate([jnp.sum(pos3, axis=1), d_const[None, :]], axis=0)
    small_local = jnp.stack([
        jnp.sum(dq.astype(f32), axis=0), jnp.sum(dv.astype(f32), axis=0), d_bias_attn,
        d_gain1, d_shift1, d_gain2, d_shift2, d_bias_out, d_mask])

    g_attn = jnp.stack(g_qkv_local + [g_out_local])
    if t_size <= 4:
        g_attn = g_attn.reshape(t_size, 4 // t_size, zs, 2, 2, rows, D)
        g_attn = net.scatter_own(g_attn, "c", 4)
        g_attn = net.scatter_own(g_attn, "x", 0)
        g_attn = net.scatter_own(g_attn, "y", 2)
        g_attn = net.scatter_own(g_attn, "z", 1)
    else:
        g_attn = g_attn.reshape(4, zs, 2, 2, rows, D).transpose(1, 2, 3, 0, 4, 5)
        g_attn = g_attn.reshape(zs, 2, 2, t_size, -1, D)
        g_attn = net.scatter_own(g_attn, "c", 2)
        g_attn = net.scatter_own(g_attn, "x", 2)
        g_attn = net.scatter_own(g_attn, "y", 1)
        g_attn = net.scatter_own(g_attn, "z", 0)
    attn_sq = jnp.sum(jnp.square(g_attn.astype(f32)))
    g_attn = net.gather_own(g_attn, "x", 0).reshape(4, rows, D).astype(f32)
    g_qkv, g_out = g_attn[:3], g_attn[3]

    parts = [small_local, pos_local, g_gate_local, g_bias_in]
    counts = [p.size for p in parts]
    pad = -sum(counts) % 1024
    flat = jnp.concatenate([p.reshape(-1) for p in parts] + [jnp.zeros((pad,), f32)])
    flat = net.total(flat.reshape(-1, 128)).reshape(-1)
    pieces, at = [], 0
    for p, count in zip(parts, counts):
        pieces.append(flat[at : at + count].reshape(p.shape))
        at += count
    g_small, g_pos, g_gate, g_bias = pieces
    shared = sum(jnp.sum(jnp.square(p)) for p in pieces)
    own_sum = attn_sq + jnp.sum(jnp.square(g_in)) + jnp.sum(jnp.square(g_outw))
    own_sum = net.total(jnp.broadcast_to(own_sum, (8, 128)))[0, 0]
    grad_norm = jnp.sqrt(own_sum + shared)
    clip = jnp.minimum(1.0, CLIP_NORM / (grad_norm + 1e-06))
    count = step_count[0].astype(f32)
    me = lax.axis_index("dp") * t_size + lax.axis_index("tensor")
    g_ffn_in = jnp.concatenate([g_in.T, lax.dynamic_slice_in_dim(g_bias, me, 1, 0)], axis=0)

    qkv_new, qkv_moment, qkv_second = adam_step(qkv_w, g_qkv, qkv_m, qkv_v, clip, 2.0 * D**-0.5, count)
    out_new, out_moment, out_second = adam_step(out_w, g_out, out_m, out_v, clip, 1.0, count)
    in_new, in_moment, in_second = adam_step(ffn_in, g_ffn_in, ffn_in_m, ffn_in_v, clip, 2.0 * D**-0.5, count)
    fo_new, fo_moment, fo_second = adam_step(ffn_out, g_outw, ffn_out_m, ffn_out_v, clip, 2.0 * FF**-0.5, count)
    small_new, small_moment, small_second = adam_step(small_params, g_small, small_m, small_v, clip, 0.5, count)
    pos_new, pos_moment, pos_second = adam_step(pos_table, g_pos, pos_m, pos_v, clip, 1.0, count)
    gate_new, gate_moment, gate_second = adam_step(gate_proj, g_gate, gate_m, gate_v, clip, 2.0 * HD**-0.5, count)
    return (
        layer_out[None], feature_grad[None], grad_norm.reshape(1),
        qkv_new, qkv_moment, qkv_second, qkv_new.astype(b16),
        out_new, out_moment, out_second, out_new.astype(b16),
        in_new, in_moment, in_second, in_new.astype(b16),
        fo_new, fo_moment, fo_second, fo_new.astype(b16),
        g_small, small_new, small_moment, small_second,
        pos_new, pos_moment, pos_second, gate_new, gate_moment, gate_second,
    )


def solution(mesh):
    both = ("dp", "tensor")
    three = (P(None, "dp", None),)
    row = (P("dp", None),)
    col = (P(None, both),)
    rows2 = (P(both, None),)
    utt = P(both, None, None)
    in_specs = (
        (utt, P(both), P(both, None), P(), utt) + three * 3 + row * 3 + col * 3 + rows2 * 3 + (P(),) * 10
    )
    out_specs = (utt, utt, P()) + three * 4 + row * 4 + col * 4 + rows2 * 4 + (P(),) * 10
    fn = functools.partial(local, mesh.shape["dp"], mesh.shape["tensor"])
    return jax.shard_map(fn, mesh=mesh, in_specs=in_specs, out_specs=out_specs, check_vma=False)
```

time: 2330 us -> 506 us (0.22)
  local copies, waits for them, and re-layouts: 1340 us -> 40.6 us
  matrix products: 331 us -> 102 us
  waiting for transfers between devices: 353 us -> 133 us
  other arithmetic: 186 us -> 53.5 us
  starting transfers between devices: 0.71 us -> 81.6 us
  Pallas kernels: 0 us -> 78.8 us
  loops' own time: 49.1 us -> 0 us
  blocking collectives: 40.4 us -> 0 us
    reshape x11 -> x6, local copies, waits for them, and re-layouts: 515 us -> 1.01 us  [the longest x2 0.82 us: local(): pieces.append(flat[at:at + count].reshape(p.shape))]
    another operation x20 -> x15, local copies, waits for them, and re-layouts: 314 us -> 1.14 us  [the longest x2 0.81 us: local(): p.reshape(-1)]
    dot_general x31 -> x27, matrix products: 331 us -> 102 us  [the longest x26 95.9 us: dot(): return lax.dot_general(a, b, dims, preferred_element_type=jnp.float32)]
    while x49 -> x0, local copies, waits for them, and re-layouts: 160 us -> none
    slice x9 -> x11, local copies, waits for them, and re-layouts: 158 us -> 5.65 us  [the longest x1 1.94 us: local(): qkv_all[0]]
    all_gather x6 -> x0, waiting for transfers between devices: 133 us -> none  [the longest x1 45 us: local(): d_gathered = lax.all_gather(d_branch, 'tensor', axis=0, tiled=True)]
    ppermute x0 -> x54, waiting for transfers between devices: none -> 133 us  [shift(): return lax.ppermute(v, ('dp', 'tensor'), pairs)]
    reduce_sum x28 -> x18, other arithmetic: 138 us -> 13.9 us  [the longest x1 3.58 us: local(): d_bias_out = jnp.sum(d_branch.astype(f32), axis=0)]
  transfers between devices with their start and end apart: 13 -> 54, of which waited for: 9 -> 18; matrix products, arithmetic and copies ran while one was open for 76% -> 21% of each run, Pallas kernels for 0% -> 8%
where the time goes in v1:
time: 506 us; the launch traced here: 499 us
  waiting for transfers between devices  133 us (26%)
  matrix products  102 us (20%)
  starting transfers between devices  81.6 us (16%)
  Pallas kernels  78.8 us (16%)
  other arithmetic  53.5 us (11%)
  local copies, waits for them, and re-layouts  40.6 us (8%)
  between operations  10.4 us (2%)
    ppermute x54, waiting for transfers between devices, shift(): return lax.ppermute(v, ('dp', 'tensor'), pairs)  133 us
    dot_general x26, matrix products, dot(): return lax.dot_general(a, b, dims, preferred_element_type=jnp.float32)  95.9 us
    ppermute x54, starting transfers between devices, shift(): return lax.ppermute(v, ('dp', 'tensor'), pairs)  81.6 us
    pallas_call x1, Pallas kernels, attn_bwd(): pl.pallas_call(functools.partial(bwd_kernel, seq=seq, ib=ib), grid=(H,),...  36.9 us
    pallas_call x1, Pallas kernels, attn_fwd(): pl.pallas_call(functools.partial(fwd_kernel, seq=seq, ib=ib), grid_spec=p...  32.3 us
    unnamed x184, local copies, waits for them, and re-layouts  12.7 us
    dynamic_update_slice x8, local copies, waits for them, and re-layouts, gather_own(): out = lax.dynamic_update_index_in_dim(out, part, (at + k) % n, dim)  10.3 us
  transfers between devices with their start and end apart: 54, of which 18 were waited for; matrix products, arithmetic and copies ran while one was open for 21% of the time, Pallas kernels for 8%

profile of v1, /device:TPU:0, one launch (start us, length us, event | category | flops | bytes accessed | tf_op | source)
XLA Modules:
  0.0 499.4 jit_solution(16262429271813026787)
XLA Ops:
  4.2 5.0 %collective-permute-start = (bf16[4,48,768]{2,1,0:T(8,128)(2,1)}, bf16[4,48,768]{2,1,0:T(8,128)(2,1)}, u32[]{:S(2)}, u32[]{:S(2)}) collective-permute-start(bf16[4,48,768]{2,1,0:T(8,128)(2,1)} %pad_maximum_fusion.7), channel_id=1, source_target_pairs={{0,24},{1,25},{2,26},{3,27},{4,28},{5,29},{6,30},{7,31},{8,0},{9,1... | collective-permute-start | bytes 884744 | tf_op jit(solution)/shard_map/ppermute | solution.py:236
  24.7 4.3 collective-permute-start.7
  30.0 12.2 %collective-permute-done.1 = bf16[4,48,768]{2,1,0:T(8,128)(2,1)} collective-permute-done((bf16[4,48,768]{2,1,0:T(8,128)(2,1)}, bf16[4,48,768]{2,1,0:T(8,128)(2,1)}, u32[]{:S(2)}, u32[]{:S(2)}) %collective-permute-start.1) | collective-permute-done | bytes 294944 | tf_op jit(solution)/shard_map/ppermute | solution.py:236
  55.9 17.3 %collective-permute-done.3 = bf16[4,4,48,768]{3,2,1,0:T(8,128)(2,1)} collective-permute-done((bf16[4,4,48,768]{3,2,1,0:T(8,128)(2,1)S(1)}, bf16[4,4,48,768]{3,2,1,0:T(8,128)(2,1)}, u32[]{:S(2)}, u32[]{:S(2)}) %collective-permute-start.3) | collective-permute-done | bytes 1179680 | tf_op jit(solution)/shard_map/ppermute | solution.py:236
  91.0 4.4 collective-permute-done.18
  100.9 19.5 %collective-permute-done.14 = f32[1,2,4,96]{3,2,1,0:T(4,128)S(1)} collective-permute-done((f32[1,2,4,96]{3,2,1,0:T(4,128)S(1)}, f32[1,2,4,96]{3,2,1,0:T(4,128)S(1)}, u32[]{:S(2)}, u32[]{:S(2)}) %collective-permute-start.14) | collective-permute-done | bytes 3104 | tf_op jit(solution)/shard_map/ppermute | solution.py:236
  122.3 9.6 %shard_map.491.t_ref = f32[12,128,2048]{2,1,0:T(8,128)} custom-call(f32[12,1,2048]{2,1,0:T(1,128)} %add.580.off_ref), custom_call_target="tpu_custom_call" | custom-call | tf_op jit(solution)/shard_map/pallas_call | solution.py:46
  145.9 6.0 %fusion.10.q_ref.k_ref.v_ref = bf16[3,1024,768]{2,1,0:T(8,128)(2,1)} fusion(f32[3]{0:T(128)S(1)} %copy-done.77, f32[3,768]{1,0:T(4,128)S(1)} %copy-done.56, bf16[3,768,768]{2,1,0:T(8,128)(2,1)S(1)} %bitcast.286, bf16[1,1024,768]{1,2,0:T(8,128)(2,1)S(1)} %copy-done.11, f32[768]{0:T(1024)S(1)} %copy-done.70, pred[1024]{0:T(1024)(128)(4,1)S(1)} %copy-done.64), kind=kOutput, calls=%fused_computation.21 | convolution fusion | flops 3632529408 | bytes 9843724 | tf_op jit(solution)/shard_map/fi,kio->kfo/dot_general | solution.py:327
  153.9 32.3 %shard_map.492 = (bf16[12,1024,1024]{2,1,0:T(8,128)(2,1)}, bf16[1024,768]{1,0:T(8,128)(2,1)S(1)}, f32[1024,768]{1,0:T(8,128)}) custom-call(s32[1]{0:T(128)} %copy.343.len_ref, bf16[3,1024,768]{2,1,0:T(8,128)(2,1)} %fusion.10.q_ref.k_ref.v_ref, bf16[3,1024,768]{2,1,0:T(8,128)(2,1)} %fusion.10.q_ref.k_ref.v_ref, ...), custom_call_target="tpu_custom_call" | custom-call | tf_op jit(solution)/shard_map/pallas_call | solution.py:93
  189.4 5.1 %multiply_convert_fusion.4 = (bf16[1024,1536]{1,0:T(8,128)(2,1)S(1)}, f32[1024,1536]{1,0:T(8,128)}) fusion(f32[1536]{0:T(1024)S(1)} %copy-done.60, bf16[1024,768]{0,1:T(8,128)(2,1)S(1)} %fusion.26, bf16[1536,768]{1,0:T(8,128)(2,1)S(1)} %bitcast.289), kind=kOutput, calls=%fused_computation.19 | convolution fusion | flops 2425356288 | bytes 13375488 | tf_op jit(solution)/shard_map/dot_general | solution.py:38
  194.6 7.4 %multiply_convert_fusion.3 = (bf16[1024,1536]{1,0:T(8,128)(2,1)S(1)}, f32[1024,1536]{1,0:T(8,128)}) fusion(f32[1536]{0:T(1024)S(1)} %copy-done.59, bf16[1024,768]{0,1:T(8,128)(2,1)S(1)} %fusion.26, bf16[1536,768]{1,0:T(8,128)(2,1)} %bitcast.28), kind=kOutput, calls=%fused_computation.17 | convolution fusion | flops 2425356288 | bytes 13375488 | tf_op jit(solution)/shard_map/dot_general | solution.py:38
  202.0 5.6 %fusion.167 = f32[1024,768]{0,1:T(8,128)S(1)} fusion(bf16[1024,1536]{1,0:T(8,128)(2,1)S(1)} %get-tuple-element.315, bf16[1536,768]{1,0:T(8,128)(2,1)} %bitcast.29), kind=kOutput, calls=%fused_computation.349 | convolution fusion | flops 2415919104 | bytes 8650752 | tf_op jit(solution)/shard_map/dot_general | solution.py:38
  207.6 3.6 fusion.162
  217.5 7.9 %convert_reduce_fusion.1 = (f32[1536]{0:T(1024)S(1)}, bf16[1024,1536]{1,0:T(8,128)(2,1)S(1)}) fusion(f32[1024,1536]{1,0:T(8,128)} %get-tuple-element.318, f32[1536]{0:T(1024)S(1)} %copy-done.60, bf16[1024,768]{0,1:T(8,128)(2,1)S(1)} %get-tuple-element.268, bf16[1536,768]{1,0:T(8,128)(2,1)S(1)} %bitcast.292), kind=kOutput, calls=%fused_computation.14 | convolution fusion | flops 2439510528 | bytes 13381632 | tf_op jit(solution)/shard_map/dot_general | solution.py:38
  225.5 7.0 %convert_reduce_fusion = (f32[1536]{0:T(1024)S(1)}, bf16[1024,1536]{1,0:T(8,128)(2,1)S(1)}) fusion(f32[1024,1536]{1,0:T(8,128)S(1)} %bitcast.313, f32[1536]{0:T(1024)S(1)} %copy-done.59, bf16[1024,768]{0,1:T(8,128)(2,1)S(1)} %get-tuple-element.268, bf16[1536,768]{1,0:T(8,128)(2,1)} %bitcast.29), kind=kOutput, calls=%fused_computation.13 | convolution fusion | flops 2439510528 | bytes 13381632 | tf_op jit(solution)/shard_map/dot_general | solution.py:38
  232.5 7.2 %fusion.168 = f32[1024,768]{0,1:T(8,128)} fusion(bf16[1024,1536]{1,0:T(8,128)(2,1)S(1)} %get-tuple-element.325, bf16[1536,768]{1,0:T(8,128)(2,1)} %bitcast.28), kind=kOutput, calls=%fused_computation.350 | convolution fusion | flops 2415919104 | bytes 8650752 | tf_op jit(solution)/shard_map/dot_general | solution.py:38
  239.7 7.2 %multiply_reduce_fusion = (f32[768]{0:T(1024)}, f32[1024]{0:T(1024)S(1)}, f32[1024]{0:T(1024)S(1)}, f32[768]{0:T(1024)}, f32[1024,768]{0,1:T(8,128)S(1)}) fusion(f32[1024,768]{0,1:T(8,128)S(1)} %get-tuple-element.314, f32[1024]{0:T(1024)S(1)} %add_rsqrt_fusion.1, f32[1024]{0:T(1024)S(1)} %broadcast_multiply_fusion.7, f32[768]{0:T(1024)S(1)} %get-tuple-element.230, ...), kind=kOutput, calls=%fused_computation.50 | convolution fusion | flops 2431644160 | bytes 19706880 | tf_op jit(solution)/shard_map/dot_general | solution.py:38
  251.4 36.9 %shard_map.493 = (bf16[1024,768]{1,0:T(8,128)(2,1)S(1)}, bf16[1024,768]{1,0:T(8,128)(2,1)S(1)}, bf16[1024,768]{1,0:T(8,128)(2,1)}, f32[12,1,1024]{2,1,0:T(1,128)S(1)}, f32[12,1,2048]{2,1,0:T(1,128)S(1)}) custom-call(bf16[3,1024,768]{2,1,0:T(8,128)(2,1)} %fusion.10.q_ref.k_ref.v_ref, bf16[3,1024,768]{2,1,0:T(8,128)(2,1)} %fusion.10.q_ref.k_ref.v_ref, ...), custom_call_target="tpu_custom_call" | custom-call | tf_op jit(solution)/shard_map/pallas_call | solution.py:162
  292.3 4.0 convolution_convert_fusion
  296.3 4.3 convolution_convert_fusion.2
  340.4 3.7 copy.290
  346.5 5.9 %add_convert_fusion = bf16[1536,768]{1,0:T(8,128)(2,1)S(1)} fusion(bf16[1536,768]{1,0:T(8,128)(2,1)} %collective-permute-done.35, bf16[1024,1536]{1,0:T(8,128)(2,1)} %copy-done.80, bf16[1024,768]{0,1:T(8,128)(2,1)} %copy-done.17), kind=kOutput, calls=%fused_computation.25 | convolution fusion | flops 2421817344 | bytes 9437184 | tf_op jit(solution)/shard_map/dot_general | solution.py:38
  354.1 4.3 add_convert_fusion.1
  364.5 16.4 %collective-permute-done.36 = bf16[2,4,96,768]{3,2,1,0:T(8,128)(2,1)S(1)} collective-permute-done((bf16[2,4,96,768]{3,2,1,0:T(8,128)(2,1)S(1)}, bf16[2,4,96,768]{3,2,1,0:T(8,128)(2,1)S(1)}, u32[]{:S(2)}, u32[]{:S(2)}) %collective-permute-start.36) | collective-permute-done | bytes 1179680 | tf_op jit(solution)/shard_map/ppermute | solution.py:236
  382.8 4.7 collective-permute-done.30
  389.4 23.4 %collective-permute-done.24 = bf16[2,4,2,48,768]{4,3,2,1,0:T(8,128)(2,1)S(1)} collective-permute-done((bf16[2,4,2,48,768]{4,3,2,1,0:T(8,128)(2,1)S(1)}, bf16[2,4,2,48,768]{4,3,2,1,0:T(8,128)(2,1)S(1)}, u32[]{:S(2)}, u32[]{:S(2)}) %collective-permute-start.24) | collective-permute-done | bytes 1179680 | tf_op jit(solution)/shard_map/ppermute | solution.py:236
  414.7 10.2 %collective-permute-done.37 = bf16[4,96,768]{2,1,0:T(8,128)(2,1)S(1)} collective-permute-done((bf16[4,96,768]{2,1,0:T(8,128)(2,1)S(1)}, bf16[4,96,768]{2,1,0:T(8,128)(2,1)S(1)}, u32[]{:S(2)}, u32[]{:S(2)}) %collective-permute-start.37) | collective-permute-done | bytes 589856 | tf_op jit(solution)/shard_map/ppermute | solution.py:236
  430.0 3.7 collective-permute-start.34
  433.8 6.3 %collective-permute-done.32 = bf16[96,768]{1,0:T(8,128)(2,1)S(1)} collective-permute-done((bf16[96,768]{1,0:T(8,128)(2,1)S(1)}, bf16[96,768]{1,0:T(8,128)(2,1)S(1)}, u32[]{:S(2)}, u32[]{:S(2)}) %collective-permute-start.32) | collective-permute-done | bytes 147488 | tf_op jit(solution)/shard_map/ppermute | solution.py:236
  440.2 6.3 %collective-permute-start.26 = (bf16[2,48,768]{2,1,0:T(8,128)(2,1)S(1)}, bf16[2,48,768]{2,1,0:T(8,128)(2,1)S(1)}, u32[]{:S(2)}, u32[]{:S(2)}) collective-permute-start(bf16[2,48,768]{2,1,0:T(8,128)(2,1)S(1)} %get-tuple-element.291), channel_id=1, source_target_pairs={{0,8},{1,9},{2,10},{3,11},{4,12},{5,13},{6,14},{7,15},{8,16},{9,17... | collective-permute-start | bytes 442376 | tf_op jit(solution)/shard_map/ppermute | solution.py:236
  446.5 5.3 %collective-permute-done.33 = bf16[96,768]{1,0:T(8,128)(2,1)S(1)} collective-permute-done((bf16[96,768]{1,0:T(8,128)(2,1)S(1)}, bf16[96,768]{1,0:T(8,128)(2,1)S(1)}, u32[]{:S(2)}, u32[]{:S(2)}) %collective-permute-start.33) | collective-permute-done | bytes 147488 | tf_op jit(solution)/shard_map/ppermute | solution.py:236
  452.6 6.6 %collective-permute-start.40 = (bf16[96,768]{1,0:T(8,128)(2,1)S(1)}, bf16[96,768]{1,0:T(8,128)(2,1)}, u32[]{:S(2)}, u32[]{:S(2)}) collective-permute-start(bf16[96,768]{1,0:T(8,128)(2,1)S(1)} %get-tuple-element.286), channel_id=1, source_target_pairs={{0,24},{1,25},{2,26},{3,27},{4,28},{5,29},{6,30},{7,31},{8,0},{9,1... | collective-permute-start | bytes 442376 | tf_op jit(solution)/shard_map/ppermute | solution.py:236
  (465 shorter events, 185.4 us)
Async XLA Ops:
  4.2 20.5 %collective-permute-start = (bf16[4,48,768]{2,1,0:T(8,128)(2,1)}, bf16[4,48,768]{2,1,0:T(8,128)(2,1)}, u32[]{:S(2)}, u32[]{:S(2)}) collective-permute-start(bf16[4,48,768]{2,1,0:T(8,128)(2,1)} %pad_maximum_fusion.7), channel_id=1, source_target_pairs={{0,24},{1,25},{2,26},{3,27},{4,28},{5,29},{6,30},{7,31},{8,0},{9,1... | collective-permute-start | bytes 884744 | tf_op jit(solution)/shard_map/ppermute | solution.py:236
  9.2 32.9 %collective-permute-start.1 = (bf16[4,48,768]{2,1,0:T(8,128)(2,1)}, bf16[4,48,768]{2,1,0:T(8,128)(2,1)}, u32[]{:S(2)}, u32[]{:S(2)}) collective-permute-start(bf16[4,48,768]{2,1,0:T(8,128)(2,1)} %pad_maximum_fusion.7), channel_id=1, source_target_pairs={{0,16},{1,17},{2,18},{3,19},{4,20},{5,21},{6,22},{7,23},{8,24},{9,... | collective-permute-start | bytes 884744 | tf_op jit(solution)/shard_map/ppermute | solution.py:236
  9.3 33.9 %collective-permute-start.2 = (bf16[4,48,768]{2,1,0:T(8,128)(2,1)}, bf16[4,48,768]{2,1,0:T(8,128)(2,1)}, u32[]{:S(2)}, u32[]{:S(2)}) collective-permute-start(bf16[4,48,768]{2,1,0:T(8,128)(2,1)} %pad_maximum_fusion.7), channel_id=1, source_target_pairs={{0,8},{1,9},{2,10},{3,11},{4,12},{5,13},{6,14},{7,15},{8,16},{9,17... | collective-permute-start | bytes 884744 | tf_op jit(solution)/shard_map/ppermute | solution.py:236
  11.3 36.0 %collective-permute-start.5 = (bf16[1,1,1,96,768]{4,3,2,1,0:T(8,128)(2,1)S(1)}, bf16[1,1,1,96,768]{4,3,2,1,0:T(8,128)(2,1)}, u32[]{:S(2)}, u32[]{:S(2)}) collective-permute-start(bf16[1,1,1,96,768]{4,3,2,1,0:T(8,128)(2,1)S(1)} %slice_bitcast_fusion.14), channel_id=1, source_target_pairs={{0,24},{1,25},{2,26},{3,27},{4,28},{5,29},{6,30},{7,31},{8,0},{9,1... | collective-permute-start | bytes 442376 | tf_op jit(solution)/shard_map/ppermute | solution.py:236
  14.2 36.4 %collective-permute-start.6 = (bf16[1,1,1,96,768]{4,3,2,1,0:T(8,128)(2,1)S(1)}, bf16[1,1,1,96,768]{4,3,2,1,0:T(8,128)(2,1)}, u32[]{:S(2)}, u32[]{:S(2)}) collective-permute-start(bf16[1,1,1,96,768]{4,3,2,1,0:T(8,128)(2,1)S(1)} %slice_bitcast_fusion.14), channel_id=1, source_target_pairs={{0,16},{1,17},{2,18},{3,19},{4,20},{5,21},{6,22},{7,23},{8,24},{9,... | collective-permute-start | bytes 442376 | tf_op jit(solution)/shard_map/ppermute | solution.py:236
  24.7 25.9 %collective-permute-start.7 = (bf16[1,1,1,96,768]{4,3,2,1,0:T(8,128)(2,1)S(1)}, bf16[1,1,1,96,768]{4,3,2,1,0:T(8,128)(2,1)S(1)}, u32[]{:S(2)}, u32[]{:S(2)}) collective-permute-start(bf16[1,1,1,96,768]{4,3,2,1,0:T(8,128)(2,1)S(1)} %slice_bitcast_fusion.14), channel_id=1, source_target_pairs={{0,8},{1,9},{2,10},{3,11},{4,12},{5,13},{6,14},{7,15},{8,16},{9,17... | collective-permute-start | bytes 442376 | tf_op jit(solution)/shard_map/ppermute | solution.py:236
  42.1 34.4 %collective-permute-start.15 = (bf16[1,1,1,96,768]{4,3,2,1,0:T(8,128)(2,1)S(1)}, bf16[1,1,1,96,768]{4,3,2,1,0:T(8,128)(2,1)S(1)}, u32[]{:S(2)}, u32[]{:S(2)}) collective-permute-start(bf16[1,1,1,96,768]{4,3,2,1,0:T(8,128)(2,1)S(1)} %convert_bitcast_fusion.2), channel_id=1, source_target_pairs={{0,24},{1,25},{2,26},{3,27},{4,28},{5,29},{6,30},{7,31},{8,0},{9,1... | collective-permute-start | bytes 442376 | tf_op jit(solution)/shard_map/ppermute | solution.py:236
  44.1 29.1 %collective-permute-start.3 = (bf16[4,4,48,768]{3,2,1,0:T(8,128)(2,1)S(1)}, bf16[4,4,48,768]{3,2,1,0:T(8,128)(2,1)}, u32[]{:S(2)}, u32[]{:S(2)}) collective-permute-start(bf16[4,4,48,768]{3,2,1,0:T(8,128)(2,1)S(1)} %bitcast_dynamic-update-slice_fusion.2), channel_id=1, source_target_pairs={{0,4},{1,5},{2,6},{3,7},{4,0},{5,1},{6,2},{7,3},{8,12},{9,13},{10,... | collective-permute-start | bytes 3538952 | tf_op jit(solution)/shard_map/ppermute | solution.py:236
  47.3 31.7 %collective-permute-start.16 = (bf16[1,1,1,96,768]{4,3,2,1,0:T(8,128)(2,1)S(1)}, bf16[1,1,1,96,768]{4,3,2,1,0:T(8,128)(2,1)S(1)}, u32[]{:S(2)}, u32[]{:S(2)}) collective-permute-start(bf16[1,1,1,96,768]{4,3,2,1,0:T(8,128)(2,1)S(1)} %convert_bitcast_fusion.2), channel_id=1, source_target_pairs={{0,16},{1,17},{2,18},{3,19},{4,20},{5,21},{6,22},{7,23},{8,24},{9,... | collective-permute-start | bytes 442376 | tf_op jit(solution)/shard_map/ppermute | solution.py:236
  50.6 28.5 %collective-permute-start.17 = (bf16[1,1,1,96,768]{4,3,2,1,0:T(8,128)(2,1)S(1)}, bf16[1,1,1,96,768]{4,3,2,1,0:T(8,128)(2,1)S(1)}, u32[]{:S(2)}, u32[]{:S(2)}) collective-permute-start(bf16[1,1,1,96,768]{4,3,2,1,0:T(8,128)(2,1)S(1)} %convert_bitcast_fusion.2), channel_id=1, source_target_pairs={{0,8},{1,9},{2,10},{3,11},{4,12},{5,13},{6,14},{7,15},{8,16},{9,17... | collective-permute-start | bytes 442376 | tf_op jit(solution)/shard_map/ppermute | solution.py:236
  51.6 30.9 %collective-permute-start.8 = (bf16[1,1,4,96,768]{4,3,2,1,0:T(8,128)(2,1)S(1)}, bf16[1,1,4,96,768]{4,3,2,1,0:T(8,128)(2,1)S(1)}, u32[]{:S(2)}, u32[]{:S(2)}) collective-permute-start(bf16[1,1,4,96,768]{4,3,2,1,0:T(8,128)(2,1)S(1)} %pad_maximum_fusion.5), channel_id=1, source_target_pairs={{0,4},{1,5},{2,6},{3,7},{4,0},{5,1},{6,2},{7,3},{8,12},{9,13},{10,... | collective-permute-start | bytes 1769480 | tf_op jit(solution)/shard_map/ppermute | solution.py:236
  79.1 63.5 %collective-permute-start.4 = (bf16[4,2,4,48,768]{4,3,2,1,0:T(8,128)(2,1)}, bf16[4,2,4,48,768]{4,3,2,1,0:T(8,128)(2,1)}, u32[]{:S(2)}, u32[]{:S(2)}) collective-permute-start(bf16[4,2,4,48,768]{4,3,2,1,0:T(8,128)(2,1)} %bitcast_dynamic-update-slice_fusion), channel_id=1, source_target_pairs={{0,2},{1,3},{2,0},{3,1},{4,6},{5,7},{6,4},{7,5},{8,10},{9,11},{10,... | collective-permute-start | bytes 7077896 | tf_op jit(solution)/shard_map/ppermute | solution.py:236
  79.2 16.2 %collective-permute-start.18 = (bf16[1,1,4,96,768]{4,3,2,1,0:T(8,128)(2,1)S(1)}, bf16[1,1,4,96,768]{4,3,2,1,0:T(8,128)(2,1)S(1)}, u32[]{:S(2)}, u32[]{:S(2)}) collective-permute-start(bf16[1,1,4,96,768]{4,3,2,1,0:T(8,128)(2,1)S(1)} %pad_maximum_fusion.6), channel_id=1, source_target_pairs={{0,1},{1,0},{2,3},{3,2},{4,5},{5,4},{6,7},{7,6},{8,9},{9,8},{10,11... | collective-permute-start | bytes 1769480 | tf_op jit(solution)/shard_map/ppermute | solution.py:236
  86.4 52.5 %collective-permute-start.9 = (bf16[1,2,4,96,768]{4,3,2,1,0:T(8,128)(2,1)}, bf16[1,2,4,96,768]{4,3,2,1,0:T(8,128)(2,1)}, u32[]{:S(2)}, u32[]{:S(2)}) collective-permute-start(bf16[1,2,4,96,768]{4,3,2,1,0:T(8,128)(2,1)} %pad_maximum_fusion.3), channel_id=1, source_target_pairs={{0,1},{1,0},{2,3},{3,2},{4,5},{5,4},{6,7},{7,6},{8,9},{9,8},{10,11... | collective-permute-start | bytes 3538952 | tf_op jit(solution)/shard_map/ppermute | solution.py:236
  96.5 44.5 %collective-permute-start.19 = (bf16[2,1,4,96,768]{4,3,2,1,0:T(8,128)(2,1)}, bf16[2,1,4,96,768]{4,3,2,1,0:T(8,128)(2,1)}, u32[]{:S(2)}, u32[]{:S(2)}) collective-permute-start(bf16[2,1,4,96,768]{4,3,2,1,0:T(8,128)(2,1)} %pad_maximum_fusion.4), channel_id=1, source_target_pairs={{0,4},{1,5},{2,6},{3,7},{4,0},{5,1},{6,2},{7,3},{8,12},{9,13},{10,... | collective-permute-start | bytes 3538952 | tf_op jit(solution)/shard_map/ppermute | solution.py:236
  98.1 22.3 %collective-permute-start.14 = (f32[1,2,4,96]{3,2,1,0:T(4,128)S(1)}, f32[1,2,4,96]{3,2,1,0:T(4,128)S(1)}, u32[]{:S(2)}, u32[]{:S(2)}) collective-permute-start(f32[1,2,4,96]{3,2,1,0:T(4,128)S(1)} %pad_maximum_fusion.15), channel_id=1, source_target_pairs={{0,1},{1,0},{2,3},{3,2},{4,5},{5,4},{6,7},{7,6},{8,9},{9,8},{10,11... | collective-permute-start | bytes 9224 | tf_op jit(solution)/shard_map/ppermute | solution.py:236
  140.5 54.1 %collective-permute-start.20 = (bf16[2,2,4,96,768]{4,3,2,1,0:T(8,128)(2,1)S(1)}, bf16[2,2,4,96,768]{4,3,2,1,0:T(8,128)(2,1)}, u32[]{:S(2)}, u32[]{:S(2)}) collective-permute-start(bf16[2,2,4,96,768]{4,3,2,1,0:T(8,128)(2,1)S(1)} %pad_maximum_fusion.1), channel_id=1, source_target_pairs={{0,2},{1,3},{2,0},{3,1},{4,6},{5,7},{6,4},{7,5},{8,10},{9,11},{10,... | collective-permute-start | bytes 7077896 | tf_op jit(solution)/shard_map/ppermute | solution.py:236
  142.4 59.6 %collective-permute-start.22 = (bf16[2,2,4,96,768]{4,3,2,1,0:T(8,128)(2,1)S(1)}, bf16[2,2,4,96,768]{4,3,2,1,0:T(8,128)(2,1)}, u32[]{:S(2)}, u32[]{:S(2)}) collective-permute-start(bf16[2,2,4,96,768]{4,3,2,1,0:T(8,128)(2,1)S(1)} %pad_maximum_fusion.2), channel_id=1, source_target_pairs={{0,2},{1,3},{2,0},{3,1},{4,6},{5,7},{6,4},{7,5},{8,10},{9,11},{10,... | collective-permute-start | bytes 7077896 | tf_op jit(solution)/shard_map/ppermute | solution.py:236
  320.2 26.3 %collective-permute-start.35 = (bf16[1536,768]{1,0:T(8,128)(2,1)}, bf16[1536,768]{1,0:T(8,128)(2,1)}, u32[]{:S(2)}, u32[]{:S(2)}) collective-permute-start(bf16[1536,768]{1,0:T(8,128)(2,1)} %convolution_convert_fusion), channel_id=1, source_target_pairs={{0,2},{1,3},{2,0},{3,1},{4,6},{5,7},{6,4},{7,5},{8,10},{9,11},{10,... | collective-permute-start | bytes 7077896 | tf_op jit(solution)/shard_map/ppermute | solution.py:236
  324.6 29.5 %collective-permute-start.29 = (bf16[1536,768]{1,0:T(8,128)(2,1)}, bf16[1536,768]{1,0:T(8,128)(2,1)}, u32[]{:S(2)}, u32[]{:S(2)}) collective-permute-start(bf16[1536,768]{1,0:T(8,128)(2,1)} %convolution_convert_fusion.2), channel_id=1, source_target_pairs={{0,2},{1,3},{2,0},{3,1},{4,6},{5,7},{6,4},{7,5},{8,10},{9,11},{10,... | collective-permute-start | bytes 7077896 | tf_op jit(solution)/shard_map/ppermute | solution.py:236
  339.6 20.6 %collective-permute-start.23 = (bf16[2,2,4,2,48,768]{5,4,3,2,1,0:T(8,128)(2,1)}, bf16[2,2,4,2,48,768]{5,4,3,2,1,0:T(8,128)(2,1)}, u32[]{:S(2)}, u32[]{:S(2)}) collective-permute-start(bf16[2,2,4,2,48,768]{5,4,3,2,1,0:T(8,128)(2,1)} %dynamic-slice_bitcast_fusion), channel_id=1, source_target_pairs={{0,2},{1,3},{2,0},{3,1},{4,6},{5,7},{6,4},{7,5},{8,10},{9,11},{10,... | collective-permute-start | bytes 7077896 | tf_op jit(solution)/shard_map/ppermute | solution.py:236
  352.5 28.4 %collective-permute-start.36 = (bf16[2,4,96,768]{3,2,1,0:T(8,128)(2,1)S(1)}, bf16[2,4,96,768]{3,2,1,0:T(8,128)(2,1)S(1)}, u32[]{:S(2)}, u32[]{:S(2)}) collective-permute-start(bf16[2,4,96,768]{3,2,1,0:T(8,128)(2,1)S(1)} %slice_bitcast_fusion), channel_id=1, source_target_pairs={{0,4},{1,5},{2,6},{3,7},{4,0},{5,1},{6,2},{7,3},{8,12},{9,13},{10,... | collective-permute-start | bytes 3538952 | tf_op jit(solution)/shard_map/ppermute | solution.py:236
  358.6 28.8 %collective-permute-start.30 = (bf16[2,4,96,768]{3,2,1,0:T(8,128)(2,1)S(1)}, bf16[2,4,96,768]{3,2,1,0:T(8,128)(2,1)S(1)}, u32[]{:S(2)}, u32[]{:S(2)}) collective-permute-start(bf16[2,4,96,768]{3,2,1,0:T(8,128)(2,1)S(1)} %bitcast.296), channel_id=1, source_target_pairs={{0,1},{1,0},{2,3},{3,2},{4,5},{5,4},{6,7},{7,6},{8,9},{9,8},{10,11... | collective-permute-start | bytes 3538952 | tf_op jit(solution)/shard_map/ppermute | solution.py:236
  362.7 50.1 %collective-permute-start.24 = (bf16[2,4,2,48,768]{4,3,2,1,0:T(8,128)(2,1)S(1)}, bf16[2,4,2,48,768]{4,3,2,1,0:T(8,128)(2,1)S(1)}, u32[]{:S(2)}, u32[]{:S(2)}) collective-permute-start(bf16[2,4,2,48,768]{4,3,2,1,0:T(8,128)(2,1)S(1)} %dynamic-slice_bitcast_fusion.1), channel_id=1, source_target_pairs={{0,1},{1,0},{2,3},{3,2},{4,5},{5,4},{6,7},{7,6},{8,9},{9,8},{10,11... | collective-permute-start | bytes 3538952 | tf_op jit(solution)/shard_map/ppermute | solution.py:236
  381.3 43.7 %collective-permute-start.37 = (bf16[4,96,768]{2,1,0:T(8,128)(2,1)S(1)}, bf16[4,96,768]{2,1,0:T(8,128)(2,1)S(1)}, u32[]{:S(2)}, u32[]{:S(2)}) collective-permute-start(bf16[4,96,768]{2,1,0:T(8,128)(2,1)S(1)} %slice_bitcast_fusion.2), channel_id=1, source_target_pairs={{0,1},{1,0},{2,3},{3,2},{4,5},{5,4},{6,7},{7,6},{8,9},{9,8},{10,11... | collective-permute-start | bytes 1769480 | tf_op jit(solution)/shard_map/ppermute | solution.py:236
  387.8 41.8 %collective-permute-start.31 = (bf16[4,96,768]{2,1,0:T(8,128)(2,1)S(1)}, bf16[4,96,768]{2,1,0:T(8,128)(2,1)S(1)}, u32[]{:S(2)}, u32[]{:S(2)}) collective-permute-start(bf16[4,96,768]{2,1,0:T(8,128)(2,1)S(1)} %slice_bitcast_fusion.4), channel_id=1, source_target_pairs={{0,4},{1,5},{2,6},{3,7},{4,0},{5,1},{6,2},{7,3},{8,12},{9,13},{10,... | collective-permute-start | bytes 1769480 | tf_op jit(solution)/shard_map/ppermute | solution.py:236
  413.1 16.8 %collective-permute-start.25 = (bf16[2,4,48,768]{3,2,1,0:T(8,128)(2,1)S(1)}, bf16[2,4,48,768]{3,2,1,0:T(8,128)(2,1)S(1)}, u32[]{:S(2)}, u32[]{:S(2)}) collective-permute-start(bf16[2,4,48,768]{3,2,1,0:T(8,128)(2,1)S(1)} %dynamic-slice_bitcast_fusion.2), channel_id=1, source_target_pairs={{0,4},{1,5},{2,6},{3,7},{4,0},{5,1},{6,2},{7,3},{8,12},{9,13},{10,... | collective-permute-start | bytes 1769480 | tf_op jit(solution)/shard_map/ppermute | solution.py:236
  425.1 42.1 %collective-permute-start.38 = (bf16[96,768]{1,0:T(8,128)(2,1)S(1)}, bf16[96,768]{1,0:T(8,128)(2,1)S(1)}, u32[]{:S(2)}, u32[]{:S(2)}) collective-permute-start(bf16[96,768]{1,0:T(8,128)(2,1)S(1)} %get-tuple-element.285), channel_id=1, source_target_pairs={{0,8},{1,9},{2,10},{3,11},{4,12},{5,13},{6,14},{7,15},{8,16},{9,17... | collective-permute-start | bytes 442376 | tf_op jit(solution)/shard_map/ppermute | solution.py:236
  426.7 40.5 %collective-permute-start.39 = (bf16[96,768]{1,0:T(8,128)(2,1)S(1)}, bf16[96,768]{1,0:T(8,128)(2,1)S(1)}, u32[]{:S(2)}, u32[]{:S(2)}) collective-permute-start(bf16[96,768]{1,0:T(8,128)(2,1)S(1)} %get-tuple-element.287), channel_id=1, source_target_pairs={{0,16},{1,17},{2,18},{3,19},{4,20},{5,21},{6,22},{7,23},{8,24},{9,... | collective-permute-start | bytes 442376 | tf_op jit(solution)/shard_map/ppermute | solution.py:236
  429.9 21.9 %collective-permute-start.33 = (bf16[96,768]{1,0:T(8,128)(2,1)S(1)}, bf16[96,768]{1,0:T(8,128)(2,1)S(1)}, u32[]{:S(2)}, u32[]{:S(2)}) collective-permute-start(bf16[96,768]{1,0:T(8,128)(2,1)S(1)} %get-tuple-element.290), channel_id=1, source_target_pairs={{0,16},{1,17},{2,18},{3,19},{4,20},{5,21},{6,22},{7,23},{8,24},{9,... | collective-permute-start | bytes 442376 | tf_op jit(solution)/shard_map/ppermute | solution.py:236
  430.0 21.8 %collective-permute-start.34 = (bf16[96,768]{1,0:T(8,128)(2,1)S(1)}, bf16[96,768]{1,0:T(8,128)(2,1)S(1)}, u32[]{:S(2)}, u32[]{:S(2)}) collective-permute-start(bf16[96,768]{1,0:T(8,128)(2,1)S(1)} %get-tuple-element.289), channel_id=1, source_target_pairs={{0,24},{1,25},{2,26},{3,27},{4,28},{5,29},{6,30},{7,31},{8,0},{9,1... | collective-permute-start | bytes 442376 | tf_op jit(solution)/shard_map/ppermute | solution.py:236
  452.6 15.0 %collective-permute-start.40 = (bf16[96,768]{1,0:T(8,128)(2,1)S(1)}, bf16[96,768]{1,0:T(8,128)(2,1)}, u32[]{:S(2)}, u32[]{:S(2)}) collective-permute-start(bf16[96,768]{1,0:T(8,128)(2,1)S(1)} %get-tuple-element.286), channel_id=1, source_target_pairs={{0,24},{1,25},{2,26},{3,27},{4,28},{5,29},{6,30},{7,31},{8,0},{9,1... | collective-permute-start | bytes 442376 | tf_op jit(solution)/shard_map/ppermute | solution.py:236
  (111 other events, 1173.6 us)

commit v2 on v1

v2 whole, which is shorter than its diff:
```python
import functools

import jax
import jax.numpy as jnp
from jax import lax
from jax.experimental import pallas as pl
from jax.experimental.pallas import tpu as pltpu
from jax.sharding import PartitionSpec as P

D = 768
H = 12
HD = 64
FF = 3072
NB = 320
SPAN = 10
CLIP_NORM = 1.0
BETA_ONE = 0.9
BETA_TWO = 0.98
ADAM_EPS = 1e-08
DECAY_RATE = 0.01
NORM_EPS = 1e-05
NEG_BIG = -1e30
GROUPS = 3


def adam_step(weight, grad_in, moment, second, clip_factor, rate_in, count_in):
    scaled = grad_in * clip_factor
    new_moment = BETA_ONE * moment + (1.0 - BETA_ONE) * scaled
    new_second = BETA_TWO * second + (1.0 - BETA_TWO) * scaled * scaled
    first_fix = 1.0 - BETA_ONE**count_in
    second_fix = 1.0 - BETA_TWO**count_in
    update = new_moment / first_fix / (jnp.sqrt(new_second / second_fix) + ADAM_EPS)
    return (weight - rate_in * (update + DECAY_RATE * weight), new_moment, new_second)


VMEM = 60 << 20
NT = (((1,), (1,)), ((), ()))
TN = (((0,), (0,)), ((), ()))


def dot(a, b, dims=(((1,), (0,)), ((), ()))):
    return lax.dot_general(a, b, dims, preferred_element_type=jnp.float32)


def cost(us):
    return pl.CostEstimate(flops=0, bytes_accessed=int(us * 3.0e6), transcendentals=0)


def table_kernel(off_ref, out_ref):
    row = jnp.broadcast_to(off_ref[0], out_ref.shape[1:])
    out_ref[0] = pltpu.roll(row, 0, 1, stride=1, stride_axis=0)


def bias_tables(offr):
    n, w = offr.shape
    return pl.pallas_call(
        table_kernel,
        grid=(n,),
        in_specs=[pl.BlockSpec((1, 1, w), lambda h: (h, 0, 0))],
        out_specs=pl.BlockSpec((1, 128, w), lambda h: (h, 0, 0)),
        out_shape=jax.ShapeDtypeStruct((n, 128, w), jnp.float32),
        compiler_params=pltpu.CompilerParams(vmem_limit_bytes=VMEM),
        cost_estimate=cost(10),
    )(offr.reshape(n, 1, w))


def assemble_kernel(at_ref, mine_ref, peer_ref, out_ref, sem, *, zs, rows, cols):
    z0, y0, c0 = at_ref[0], at_ref[1], at_ref[2]
    copies = []
    for c, src in enumerate((mine_ref, peer_ref)):
        for y in range(2):
            for z in range(zs):
                block = (lax.rem(z0 + z, zs) * 2 + lax.rem(y0 + y, 2)) * 2 + lax.rem(c0 + c, 2)
                first = pl.multiple_of(block * rows, rows)
                for k in range(3):
                    there = out_ref.at[pl.ds(first, rows), pl.ds(k * cols, cols)]
                    copies.append(pltpu.make_async_copy(src.at[y, z, 3 + k], there, sem.at[len(copies)]))
    for copy in copies:
        copy.start()
    for copy in copies:
        copy.wait()


def assemble(at, mine, peer):
    _, zs, _, rows, cols = mine.shape
    hbm = pl.BlockSpec(memory_space=pl.ANY)
    return pl.pallas_call(
        functools.partial(assemble_kernel, zs=zs, rows=rows, cols=cols),
        in_specs=[pl.BlockSpec(memory_space=pltpu.SMEM), hbm, hbm],
        out_specs=pl.BlockSpec(memory_space=pltpu.VMEM),
        scratch_shapes=[pltpu.SemaphoreType.DMA((12 * zs,))],
        out_shape=jax.ShapeDtypeStruct((D, D), jnp.bfloat16),
        compiler_params=pltpu.CompilerParams(vmem_limit_bytes=VMEM),
        cost_estimate=cost(2),
    )(at, mine, peer)


def fwd_kernel(len_ref, at_ref, x_ref, mine_ref, peer_ref, bias_ref, t_ref, g_ref, *rest, seq, ib, zs, rows, kept):
    p_ref, o_ref, of_ref, rl_ref, qkv_ref, w_ref, s_ref, sem = rest[kept:]
    h = pl.program_id(0)

    @pl.when(h == 0)
    def _():
        z0, y0, c0 = at_ref[0], at_ref[1], at_ref[2]
        copies = []
        for c, src in enumerate((mine_ref, peer_ref)):
            for y in range(2):
                for z in range(zs):
                    block = (lax.rem(z0 + z, zs) * 2 + lax.rem(y0 + y, 2)) * 2 + lax.rem(c0 + c, 2)
                    first = pl.multiple_of(block * rows, rows)
                    there = w_ref.at[:, pl.ds(first, rows), :]
                    copies.append(pltpu.make_async_copy(src.at[y, z, pl.ds(0, 3)], there, sem.at[len(copies)]))
        for copy in copies:
            copy.start()
        for copy in copies:
            copy.wait()
        for k in range(3):
            r = dot(x_ref[...], w_ref[k]) + bias_ref[k]
            qkv_ref[k] = (r * HD**-0.5 if k == 0 else r).astype(jnp.bfloat16)

    par = lax.rem(h, 2)
    lane = lax.broadcasted_iota(jnp.int32, (seq, 128), 1)
    rowi = lax.broadcasted_iota(jnp.int32, (seq, 128), 0)
    inh = (lane // 64) == par
    flag = lane == (64 * (1 - par))
    one = jnp.bfloat16(1.0)
    zero = jnp.bfloat16(0.0)
    pair = pl.ds(pl.multiple_of(h // 2 * 128, 128), 128)
    bias = jnp.where(rowi < len_ref[0], 0.0, NEG_BIG).astype(jnp.bfloat16)
    qm = jnp.where(flag, one, jnp.where(inh, qkv_ref[0, :, pair], zero))
    km = jnp.where(flag, bias, qkv_ref[1, :, pair])
    vm = jnp.where(flag, one, qkv_ref[2, :, pair])
    vt = vm.T
    base = seq - 128
    for i0 in range(0, seq, ib):
        gate = g_ref[0, :, i0 : i0 + ib]
        qb = qm[i0 : i0 + ib]
        m = None
        for j0 in range(0, seq, 128):
            c0 = i0 - j0 + base
            s = dot(km[j0 : j0 + 128], qb, NT) + t_ref[0, :, c0 : c0 + ib] * gate
            s_ref[j0 : j0 + 128, :] = s
            mm = jnp.max(s.reshape(16, 8, ib), axis=0)
            m = mm if m is None else jnp.maximum(m, mm)
        m = jnp.max(m, axis=0, keepdims=True)
        for j0 in range(0, seq, 128):
            e = jnp.exp(s_ref[j0 : j0 + 128, :] - m).astype(jnp.bfloat16)
            p_ref[0, j0 : j0 + 128, i0 : i0 + ib] = e
        ct = dot(vt, p_ref[0, :, i0 : i0 + ib])
        total = jnp.where(par == 0, ct[64:65], ct[0:1])
        rl = 1.0 / total
        oc = (ct * rl).T
        rc = jnp.broadcast_to(rl, (128, ib)).T
        ih = inh[i0 : i0 + ib]
        o_ref[i0 : i0 + ib, :] = jnp.where(ih, oc.astype(jnp.bfloat16), o_ref[i0 : i0 + ib, :])
        of_ref[i0 : i0 + ib, :] = jnp.where(ih, oc, of_ref[i0 : i0 + ib, :])
        rl_ref[i0 : i0 + ib, :] = jnp.where(ih, rc, rl_ref[i0 : i0 + ib, :])


def attn_fwd(length, at, x, mine, peer, bias, table, gates, head0, heads, kept, ib=256):
    seq = x.shape[0]
    _, zs, _, rows, cols = mine.shape
    w = table.shape[-1]
    f32, b16 = jnp.float32, jnp.bfloat16
    out_pair = pl.BlockSpec((seq, 128), lambda h, n, a: (0, head0 // 2 + h // 2))
    hbm = pl.BlockSpec(memory_space=pl.ANY)
    return pl.pallas_call(
        functools.partial(fwd_kernel, seq=seq, ib=ib, zs=zs, rows=rows, kept=len(kept)),
        grid_spec=pltpu.PrefetchScalarGridSpec(
            num_scalar_prefetch=2,
            grid=(heads,),
            in_specs=[
                pl.BlockSpec((seq, D), lambda h, n, a: (0, 0)),
                hbm,
                hbm,
                pl.BlockSpec((3, 1, cols), lambda h, n, a: (0, 0, 0)),
                pl.BlockSpec((1, 128, w), lambda h, n, a: (head0 + h, 0, 0)),
                pl.BlockSpec((1, 1, seq), lambda h, n, a: (head0 + h, 0, 0)),
            ] + [hbm] * len(kept),
            out_specs=[pl.BlockSpec((1, seq, seq), lambda h, n, a: (h, 0, 0)), out_pair, out_pair, out_pair,
                       pl.BlockSpec((3, seq, cols), lambda h, n, a: (0, 0, 0)),
                       pl.BlockSpec((3, D, cols), lambda h, n, a: (0, 0, 0))],
            scratch_shapes=[pltpu.VMEM((seq, ib), f32), pltpu.SemaphoreType.DMA((4 * zs,))],
        ),
        out_shape=[jax.ShapeDtypeStruct((heads, seq, seq), b16), jax.ShapeDtypeStruct((seq, D), b16),
                   jax.ShapeDtypeStruct((seq, D), f32), jax.ShapeDtypeStruct((seq, D), f32),
                   jax.ShapeDtypeStruct((3, seq, cols), b16), jax.ShapeDtypeStruct((3, D, cols), b16)],
        input_output_aliases={8: 1, 9: 2, 10: 3} if kept else {},
        compiler_params=pltpu.CompilerParams(vmem_limit_bytes=VMEM),
        cost_estimate=cost(2.7 * heads + 4),
    )(length, at, x, mine, peer, bias, table, gates, *kept)


def bwd_kernel(q_ref, k_ref, v_ref, dc_ref, c_ref, p_ref, t_ref, g_ref, d_ref, dg_ref, do_ref, a_ref, ds_ref, *, seq, ib):
    par = lax.rem(pl.program_id(0), 2)
    lane = lax.broadcasted_iota(jnp.int32, (seq, 128), 1)
    inh = (lane // 64) == par
    f0 = lane == (64 * (1 - par))
    f1 = lane == (64 * (1 - par) + 1)
    one = jnp.bfloat16(1.0)
    dc = dc_ref[...]
    dcf = jnp.where(inh, dc.astype(jnp.float32), 0.0)
    delta = -jnp.sum(dcf * c_ref[...], axis=1, keepdims=True)
    hi = delta.astype(jnp.bfloat16).astype(jnp.float32)
    lo = delta - hi
    dca = jnp.where(f0, hi, jnp.where(f1, lo, dcf)).astype(jnp.bfloat16)
    va = jnp.where(f0 | f1, one, v_ref[0])
    kt = k_ref[0].T
    q = q_ref[0]
    base = seq - 128
    a_ref[...] = jnp.zeros_like(a_ref)
    for i0 in range(0, seq, ib):
        gate = g_ref[0, :, i0 : i0 + ib]
        dcb = dca[i0 : i0 + ib]
        dg = jnp.zeros((8, ib), jnp.float32)
        for j0 in range(0, seq, 128):
            c0 = i0 - j0 + base
            ds = dot(va[j0 : j0 + 128], dcb, NT) * p_ref[0, j0 : j0 + 128, i0 : i0 + ib].astype(jnp.float32)
            ds_ref[j0 : j0 + 128, i0 : i0 + ib] = ds.astype(jnp.bfloat16)
            dg = dg + jnp.sum((ds * t_ref[0, :, c0 : c0 + ib]).reshape(16, 8, ib), axis=0)
            a_ref[:, c0 : c0 + ib] += ds * gate
        dg_ref[0, :, i0 : i0 + ib] = jnp.sum(dg, axis=0, keepdims=True)
        dqt = dot(kt, ds_ref[:, i0 : i0 + ib]).T * HD**-0.5
        d_ref[0, i0 : i0 + ib, :] = jnp.where(inh[i0 : i0 + ib], dqt.astype(jnp.bfloat16), d_ref[0, i0 : i0 + ib, :])
    dk = dot(ds_ref[...], q)
    d_ref[1] = jnp.where(inh, dk.astype(jnp.bfloat16), d_ref[1])
    dv = dot(p_ref[0], dc)
    d_ref[2] = jnp.where(inh, dv.astype(jnp.bfloat16), d_ref[2])
    a = a_ref[...]
    w = a.shape[1]
    r = 64
    while r >= 8:
        a = a[:r] + pltpu.roll(a[r:], w - r, 1)
        r //= 2
    acc = a[0:1]
    for r in range(1, 8):
        acc = acc + pltpu.roll(a[r : r + 1], w - r, 1)
    do_ref[0] = acc


def attn_bwd(qkv, dctx, ctx, probs, table, gates, head0, heads, ib=256):
    seq = qkv.shape[1]
    w = table.shape[-1]

    def part(k):
        return pl.BlockSpec((1, seq, 128), lambda h: (k, 0, h // 2))

    pair = pl.BlockSpec((seq, 128), lambda h: (0, head0 // 2 + h // 2))
    return pl.pallas_call(
        functools.partial(bwd_kernel, seq=seq, ib=ib),
        grid=(heads,),
        in_specs=[
            part(0),
            part(1),
            part(2),
            pair,
            pair,
            pl.BlockSpec((1, seq, seq), lambda h: (h, 0, 0)),
            pl.BlockSpec((1, 128, w), lambda h: (head0 + h, 0, 0)),
            pl.BlockSpec((1, 1, seq), lambda h: (head0 + h, 0, 0)),
        ],
        out_specs=[
            pl.BlockSpec((3, seq, 128), lambda h: (0, 0, h // 2)),
            pl.BlockSpec((1, 1, seq), lambda h: (h, 0, 0)),
            pl.BlockSpec((1, 1, w), lambda h: (h, 0, 0)),
        ],
        scratch_shapes=[pltpu.VMEM((128, w), jnp.float32), pltpu.VMEM((seq, seq), jnp.bfloat16)],
        out_shape=[
            jax.ShapeDtypeStruct((3, seq, heads * HD), jnp.bfloat16),
            jax.ShapeDtypeStruct((heads, 1, seq), jnp.float32),
            jax.ShapeDtypeStruct((heads, 1, w), jnp.float32),
        ],
        compiler_params=pltpu.CompilerParams(vmem_limit_bytes=VMEM),
        cost_estimate=cost(3.0 * heads),
    )(qkv, qkv, qkv, dctx, ctx, probs, table, gates)


def wgrad_kernel(xt_ref, d_ref, a_ref, b_ref, g_ref, *, pair):
    xt = xt_ref[...]
    for k in range(3):
        g_ref[:, k * 256 : k * 256 + 256] = dot(xt, d_ref[k]).astype(jnp.bfloat16)
    if pair:
        g_ref[:, 768:1536] = dot(a_ref[...], b_ref[...], TN).astype(jnp.bfloat16)
    else:
        for k in range(3):
            g_ref[:, 768 + k * 256 : 1024 + k * 256] = dot(xt, a_ref[k]).astype(jnp.bfloat16)


def weight_grads(xt, d3, a, b, block=256):
    seq = xt.shape[1]
    pair = a.ndim == 2
    kinds = pl.BlockSpec((3, seq, 256), lambda i: (0, 0, 0))
    a_spec = pl.BlockSpec((seq, block), lambda i: (0, i)) if pair else kinds
    b_spec = pl.BlockSpec((seq, D), lambda i: (0, 0)) if pair else pl.BlockSpec((8, 128), lambda i: (0, 0))
    return pl.pallas_call(
        functools.partial(wgrad_kernel, pair=pair),
        grid=(D // block,),
        in_specs=[pl.BlockSpec((block, seq), lambda i: (i, 0)), kinds, a_spec, b_spec],
        out_specs=pl.BlockSpec((block, 2 * D), lambda i: (i, 0)),
        out_shape=jax.ShapeDtypeStruct((D, 2 * D), jnp.bfloat16),
        compiler_params=pltpu.CompilerParams(vmem_limit_bytes=VMEM),
        cost_estimate=cost(5),
    )(xt, d3, a, b)


def core_split_kernel(at_ref, d_ref, x_ref, keep_ref, send_ref, *, wide, places):
    g = dot(d_ref[...], x_ref[...], TN).astype(jnp.bfloat16)
    first = at_ref[2] == 0
    for k in range(places):
        low = g[2 * k * wide : (2 * k + 1) * wide]
        high = g[(2 * k + 1) * wide : (2 * k + 2) * wide]
        keep_ref[k] = jnp.where(first, low, high)
        send_ref[k] = jnp.where(first, high, low)


def core_split_grads(at, d, x, wide):
    seq, units = d.shape
    places = max(1, 384 // (2 * wide))
    cols = places * 2 * wide
    out = pl.BlockSpec((places, wide, D), lambda i: (i, 0, 0))
    shape = jax.ShapeDtypeStruct((units // (2 * wide), wide, D), jnp.bfloat16)
    return pl.pallas_call(
        functools.partial(core_split_kernel, wide=wide, places=places),
        grid=(units // cols,),
        in_specs=[pl.BlockSpec(memory_space=pltpu.SMEM), pl.BlockSpec((seq, cols), lambda i: (0, i)),
                  pl.BlockSpec((seq, D), lambda i: (0, 0))],
        out_specs=[out, out],
        out_shape=[shape, shape],
        compiler_params=pltpu.CompilerParams(vmem_limit_bytes=VMEM),
        cost_estimate=cost(8),
    )(at, d, x)


def row_norm(r):
    mean = jnp.mean(r, axis=-1, keepdims=True)
    cen = r - mean
    inv = lax.rsqrt(jnp.mean(cen * cen, axis=-1, keepdims=True) + NORM_EPS)
    return cen * inv, inv


def row_norm_back(cot, n, inv, gain):
    e = cot * gain
    return inv * (e - jnp.mean(e, axis=-1, keepdims=True) - n * jnp.mean(e * n, axis=-1, keepdims=True))


def mix_kernel(c_ref, w_ref, x_ref, mask_ref, small_ref, r_ref, low_ref):
    att = dot(c_ref[...], w_ref[...])
    mixed = jnp.where(mask_ref[...] > 0.5, small_ref[8:9], x_ref[...].astype(jnp.float32))
    r = mixed + att + small_ref[2:3]
    n, _ = row_norm(r)
    r_ref[...] = r
    low_ref[...] = (n * small_ref[3:4] + small_ref[4:5]).astype(jnp.bfloat16)


def mix_out(ctx, w_attn, rounded, mask, small, block=256):
    seq = rounded.shape[0]
    wide = pl.BlockSpec((block, D), lambda i: (i, 0))
    return pl.pallas_call(
        mix_kernel,
        grid=(seq // block,),
        in_specs=[wide, pl.BlockSpec((D, D), lambda i: (0, 0)), wide,
                  pl.BlockSpec((block, 1), lambda i: (i, 0)), pl.BlockSpec((9, D), lambda i: (0, 0))],
        out_specs=[wide, wide],
        out_shape=[jax.ShapeDtypeStruct((seq, D), jnp.float32), jax.ShapeDtypeStruct((seq, D), jnp.bfloat16)],
        compiler_params=pltpu.CompilerParams(vmem_limit_bytes=VMEM),
        cost_estimate=cost(4),
    )(ctx, w_attn, rounded, mask, small)


def gelu_both(x):
    cdf = 0.5 * (1.0 + lax.erf(x * 0.7071067811865476))
    dens = jnp.exp(-0.5 * x * x) * 0.3989422804014327
    return x * cdf, cdf + x * dens


def weight_copies(w_ref, wi_ref, wo_ref, sem):
    owners, own, _ = wi_ref.shape
    per = 768 // own
    copies = []
    for c in range(owners // per):
        here = pl.ds(c * per, per)
        copies.append((
            pltpu.make_async_copy(w_ref.at[here, pl.ds(0, own), :], wi_ref.at[here], sem.at[0, c]),
            pltpu.make_async_copy(w_ref.at[here, pl.ds(own, own), :], wo_ref.at[here], sem.at[1, c]),
        ))
    return per, copies


def by_step(w_ref, wi_ref, wo_ref, sem, body):
    per, copies = weight_copies(w_ref, wi_ref, wo_ref, sem)
    i = pl.program_id(0)

    @pl.when(i == 0)
    def _():
        for pair in copies:
            for copy in pair:
                copy.start()

        def wait(c):
            for copy in copies[c]:
                copy.wait()

        body(per, len(copies), wait)

    @pl.when(i > 0)
    def _():
        body(per, len(copies), lambda c: None)


def ffn_kernel(len_ref, low_ref, w_ref, b_ref, r_ref, cot_ref, small_ref,
               act_ref, slope_ref, out_ref, dres_ref, dlow_ref, red_ref, wi_ref, wo_ref, sem, *, block):
    i = pl.program_id(0)

    @pl.when(i == 0)
    def _():
        red_ref[...] = jnp.zeros_like(red_ref)

    def body(per, chunks, wait):
        low = low_ref[...]
        acc = None
        for c in range(chunks):
            wait(c)
            cols = slice(c * 768, c * 768 + 768)
            hid = dot(low, wi_ref[c * per : c * per + per].reshape(-1, D), NT) + b_ref[:, cols]
            act, slo = gelu_both(hid)
            act = act.astype(jnp.bfloat16)
            act_ref[:, cols] = act
            slope_ref[:, cols] = slo.astype(jnp.bfloat16)
            part = dot(act, wo_ref[c * per : c * per + per].reshape(-1, D))
            acc = part if acc is None else acc + part
        n1, _ = row_norm(r_ref[...])
        first = n1 * small_ref[3:4] + small_ref[4:5]
        n, inv = row_norm(first + (acc + small_ref[7:8]))
        out_ref[...] = n * small_ref[5:6] + small_ref[6:7]
        at = lax.broadcasted_iota(jnp.int32, (block, D), 0) + i * block
        cot = jnp.where(at < len_ref[0], cot_ref[...].astype(jnp.float32), 0.0)
        dres = row_norm_back(cot, n, inv, small_ref[5:6])
        dlow = dres.astype(jnp.bfloat16)
        dres_ref[...] = dres
        dlow_ref[...] = dlow
        for k, v in enumerate((cot * n, cot, dlow.astype(jnp.float32))):
            red_ref[k : k + 1] += jnp.sum(v, axis=0, keepdims=True)

    by_step(w_ref, wi_ref, wo_ref, sem, body)


def ffn_scratch(w_all):
    owners, rows, _ = w_all.shape
    own = (rows - 8) // 2
    return [
        pltpu.VMEM((owners, own, D), jnp.bfloat16),
        pltpu.VMEM((owners, own, D), jnp.bfloat16),
        pltpu.SemaphoreType.DMA((2, owners * own // 768)),
    ]


def ffn_forward(length, low, w_all, bias, r1, cot, small, block=256):
    seq = low.shape[0]
    wide = pl.BlockSpec((block, D), lambda i, n: (i, 0))
    hidden = pl.BlockSpec((block, FF), lambda i, n: (i, 0))
    f32, b16 = jnp.float32, jnp.bfloat16
    return pl.pallas_call(
        functools.partial(ffn_kernel, block=block),
        grid_spec=pltpu.PrefetchScalarGridSpec(
            num_scalar_prefetch=1,
            grid=(seq // block,),
            in_specs=[wide, pl.BlockSpec(memory_space=pl.ANY), pl.BlockSpec((1, FF), lambda i, n: (0, 0)), wide, wide,
                      pl.BlockSpec((9, D), lambda i, n: (0, 0))],
            out_specs=[hidden, hidden, wide, wide, wide, pl.BlockSpec((8, D), lambda i, n: (0, 0))],
            scratch_shapes=ffn_scratch(w_all),
        ),
        out_shape=[jax.ShapeDtypeStruct((seq, FF), b16), jax.ShapeDtypeStruct((seq, FF), b16),
                   jax.ShapeDtypeStruct((seq, D), f32), jax.ShapeDtypeStruct((seq, D), f32),
                   jax.ShapeDtypeStruct((seq, D), b16), jax.ShapeDtypeStruct((8, D), f32)],
        compiler_params=pltpu.CompilerParams(vmem_limit_bytes=VMEM),
        cost_estimate=cost(18),
    )(length, low, w_all, bias, r1, cot, small)


def ffn_back_kernel(dlow_ref, w_ref, slope_ref, dres_ref, r_ref, wa_ref, rl_ref, small_ref,
                    dh_ref, gb_ref, dr1_ref, da_ref, dc_ref, red_ref, wi_ref, wo_ref, sem):
    @pl.when(pl.program_id(0) == 0)
    def _():
        red_ref[...] = jnp.zeros_like(red_ref)
        gb_ref[...] = jnp.zeros_like(gb_ref)

    def body(per, chunks, wait):
        dlow = dlow_ref[...]
        acc = None
        for c in range(chunks):
            wait(c)
            cols = slice(c * 768, c * 768 + 768)
            dh = dot(dlow, wo_ref[c * per : c * per + per].reshape(-1, D), NT) * slope_ref[:, cols].astype(jnp.float32)
            dh = dh.astype(jnp.bfloat16)
            dh_ref[:, cols] = dh
            gb_ref[:, cols] += jnp.sum(dh.astype(jnp.float32), axis=0, keepdims=True)
            part = dot(dh, wi_ref[c * per : c * per + per].reshape(-1, D))
            acc = part if acc is None else acc + part
        n, inv = row_norm(r_ref[...])
        dfirst = dres_ref[...] + acc
        dr1 = row_norm_back(dfirst, n, inv, small_ref[3:4])
        low = dr1.astype(jnp.bfloat16)
        dr1_ref[...] = dr1
        da_ref[...] = low
        dc_ref[...] = (dot(low, wa_ref[...], NT) * rl_ref[...]).astype(jnp.bfloat16)
        for k, v in enumerate((low.astype(jnp.float32), dfirst * n, dfirst)):
            red_ref[k : k + 1] += jnp.sum(v, axis=0, keepdims=True)

    by_step(w_ref, wi_ref, wo_ref, sem, body)


def ffn_backward(dlow, w_all, slope, dres, r1, w_attn, rl, small, block=256):
    seq = dlow.shape[0]
    wide = pl.BlockSpec((block, D), lambda i: (i, 0))
    hidden = pl.BlockSpec((block, FF), lambda i: (i, 0))
    f32, b16 = jnp.float32, jnp.bfloat16
    return pl.pallas_call(
        ffn_back_kernel,
        grid=(seq // block,),
        in_specs=[wide, pl.BlockSpec(memory_space=pl.ANY), hidden, wide, wide,
                  pl.BlockSpec((D, D), lambda i: (0, 0)), wide, pl.BlockSpec((9, D), lambda i: (0, 0))],
        out_specs=[hidden, pl.BlockSpec((1, FF), lambda i: (0, 0)),
                   wide, wide, wide, pl.BlockSpec((8, D), lambda i: (0, 0))],
        out_shape=[jax.ShapeDtypeStruct((seq, FF), b16), jax.ShapeDtypeStruct((1, FF), f32),
                   jax.ShapeDtypeStruct((seq, D), f32), jax.ShapeDtypeStruct((seq, D), b16),
                   jax.ShapeDtypeStruct((seq, D), b16), jax.ShapeDtypeStruct((8, D), f32)],
        scratch_shapes=ffn_scratch(w_all),
        compiler_params=pltpu.CompilerParams(vmem_limit_bytes=VMEM),
        cost_estimate=cost(18),
    )(dlow, w_all, slope, dres, r1, w_attn, rl, small)


def input_kernel(dr_ref, d0_ref, d1_ref, d2_ref, w0_ref, w1_ref, w2_ref, z_ref, wg_ref, mask_ref,
                 fg_ref, red_ref):
    i = pl.program_id(0)
    acc = dr_ref[...] + dot(z_ref[...], wg_ref[...], TN)
    qs, vs = [], []
    for d_ref, w_ref in ((d0_ref, w0_ref), (d1_ref, w1_ref), (d2_ref, w2_ref)):
        for k in range(3):
            acc += dot(d_ref[k], w_ref[k], NT)
        qs.append(jnp.sum(d_ref[0].astype(jnp.float32), axis=0, keepdims=True))
        vs.append(jnp.sum(d_ref[2].astype(jnp.float32), axis=0, keepdims=True))
    masked = mask_ref[...] > 0.5
    fg_ref[...] = jnp.where(masked, 0.0, acc)
    dm = jnp.sum(jnp.where(masked, acc, 0.0), axis=0, keepdims=True)
    red = jnp.concatenate(
        [jnp.concatenate(qs, axis=1), jnp.concatenate(vs, axis=1), dm, jnp.zeros((5, D), jnp.float32)], axis=0
    )

    @pl.when(i == 0)
    def _():
        red_ref[...] = red

    @pl.when(i > 0)
    def _():
        red_ref[...] += red


def input_grad(dr1, ds, ws, dz, wg, mask, block=256):
    seq = dr1.shape[0]
    wide = pl.BlockSpec((block, D), lambda i: (i, 0))
    part = pl.BlockSpec((3, block, 256), lambda i: (0, i, 0))
    wpart = pl.BlockSpec((3, D, 256), lambda i: (0, 0, 0))
    return pl.pallas_call(
        input_kernel,
        grid=(seq // block,),
        in_specs=[wide, part, part, part, wpart, wpart, wpart,
                  pl.BlockSpec((dz.shape[0], block), lambda i: (0, i)),
                  pl.BlockSpec(wg.shape, lambda i: (0, 0)),
                  pl.BlockSpec((block, 1), lambda i: (i, 0))],
        out_specs=[wide, pl.BlockSpec((8, D), lambda i: (0, 0))],
        out_shape=[jax.ShapeDtypeStruct((seq, D), jnp.float32), jax.ShapeDtypeStruct((8, D), jnp.float32)],
        compiler_params=pltpu.CompilerParams(vmem_limit_bytes=VMEM),
        cost_estimate=cost(8),
    )(dr1, *ds, *ws, dz, wg, mask)


def split3(x):
    hi = x.astype(jnp.bfloat16)
    rest = x - hi.astype(jnp.float32)
    mid = rest.astype(jnp.bfloat16)
    low = (rest - mid.astype(jnp.float32)).astype(jnp.bfloat16)
    return hi, mid, low


def tree_sum(parts):
    while len(parts) > 1:
        half = len(parts) // 2
        parts = [parts[i] + parts[i + half] for i in range(half)]
    return parts[0]


def added(parts):
    return sum(p.astype(jnp.float32) for p in parts)


class Net:
    def __init__(self, dp_size, t_size):
        self.t = t_size
        self.sizes = {"z": dp_size // 4, "y": 2, "c": 2, "x": t_size}
        d = lax.axis_index("dp")
        self.at = {"z": d // 4, "y": d // 2 % 2, "c": d % 2, "x": lax.axis_index("tensor")}

    def shift(self, v, axis, k):
        pairs = []
        sz = self.sizes
        for z in range(sz["z"]):
            for y in range(2):
                for c in range(2):
                    for x in range(sz["x"]):
                        src = {"z": z, "y": y, "c": c, "x": x}
                        dst = dict(src)
                        dst[axis] = (src[axis] - k) % sz[axis]
                        flat = [((q["z"] * 2 + q["y"]) * 2 + q["c"]) * sz["x"] + q["x"] for q in (src, dst)]
                        pairs.append(tuple(flat))
        return lax.ppermute(v, ("dp", "tensor"), pairs)

    def gather(self, v, axis, dim):
        return jnp.concatenate([v] + [self.shift(v, axis, k) for k in range(1, self.sizes[axis])], axis=dim)

    def scatter(self, parts, axis, dim):
        n = self.sizes[axis]
        at = self.at[axis]

        def slot(i):
            return [lax.dynamic_index_in_dim(p, i, dim, False) for p in parts]

        arrived = []
        for k in range(1, n):
            send = added(slot((at + k) % n)).astype(jnp.bfloat16)
            arrived.append(self.shift(send, axis, n - k))
        return slot(at), arrived

    def gather_own(self, v, axis, dim):
        n = self.sizes[axis]
        at = self.at[axis]
        out = jnp.zeros(v.shape[:dim] + (n,) + v.shape[dim:], v.dtype)
        for k in range(n):
            part = v if k == 0 else self.shift(v, axis, k)
            out = lax.dynamic_update_index_in_dim(out, part, (at + k) % n, dim)
        return out

    def total(self, v, axes=("c", "x", "y", "z")):
        for axis in axes:
            v = tree_sum([v] + [self.shift(v, axis, k) for k in range(1, self.sizes[axis])])
        return v


def rolled(net, v, dims, sign):
    for dim, axis in dims:
        v = jnp.roll(v, sign * net.at[axis], dim)
    return v


def natural(net, places, mine, peer):
    if mine.shape[3] % 16 == 0:
        return assemble(places, mine, peer)
    v = rolled(net, jnp.stack([mine, peer])[:, :, :, 3:], ((0, "c"), (1, "y"), (2, "z")), 1)
    return v.transpose(2, 1, 0, 4, 3, 5).reshape(D, D)


def wide_rows(net, places, mine, peer):
    if mine.shape[3] % 16 == 0:
        return places, mine, peer
    zs, kinds, cols = net.sizes["z"], mine.shape[2], mine.shape[4]
    v = rolled(net, jnp.stack([mine, peer]), ((0, "c"), (1, "y"), (2, "z")), 1)
    v = v.transpose(2, 1, 0, 4, 3, 5)
    v = v.reshape(1, 2, 2, -1, kinds, cols).transpose(2, 1, 0, 4, 3, 5)
    return places * 0, v[0], v[1]


def local(dp_size, t_size, features, lengths, span_starts, buckets, cotangent,
          qkv_w, qkv_m, qkv_v, out_w, out_m, out_v, ffn_in, ffn_in_m, ffn_in_v,
          ffn_out, ffn_out_m, ffn_out_v, small_params, small_m, small_v,
          pos_table, pos_m, pos_v, gate_proj, gate_m, gate_v, step_count):
    f32, b16 = jnp.float32, jnp.bfloat16
    net = Net(dp_size, t_size)
    zs = net.sizes["z"]
    seq = features.shape[1]
    own = ffn_out.shape[0]
    rows = qkv_w.shape[1]
    scale = HD**-0.5

    bar = lax.optimization_barrier
    places = jnp.stack([net.at["z"], net.at["y"], net.at["c"], net.at["x"]]).astype(jnp.int32)
    cols = D // GROUPS
    group_heads = H // GROUPS
    both = ("dp", "tensor")

    bias_row = jnp.pad(ffn_in[D:].astype(b16), ((0, 7), (0, D - own)))
    ffn_own = jnp.concatenate([ffn_in[:D].T.astype(b16), ffn_out.astype(b16), bias_row])

    qkv_low = qkv_w.astype(b16)[None, None]
    u0, u1, u2 = [qkv_low[..., g * cols : (g + 1) * cols] for g in range(3)]
    out_parts = out_w.astype(b16).reshape(rows, 3, cols).transpose(1, 0, 2)[None, None]
    u2 = jnp.concatenate([u2, out_parts], axis=2)
    positions = jnp.arange(seq, dtype=jnp.int32)
    starts = span_starts[0]
    masked = jnp.any((positions[:, None] >= starts[None, :]) & (positions[:, None] < starts[None, :] + SPAN), axis=1)[:, None]
    mask = masked.astype(f32)
    rounded = jnp.where(masked, small_params[8][None, :].astype(b16), features[0])
    z0 = net.gather(u0, "z", 1)
    z0, u1, u2, rounded, mask, buckets = bar((z0, u1, u2, rounded, mask, buckets))

    y0 = net.gather(z0, "y", 0)
    z1 = net.gather(u1, "z", 1)
    rev = jnp.flip(buckets)
    order = jnp.concatenate([rev[127:], jnp.full((1,), -1, jnp.int32), rev[:127]])
    onehot = (jnp.arange(NB, dtype=jnp.int32)[:, None] == order[None, :]).astype(b16)
    off3 = dot(jnp.concatenate(split3(pos_table[:NB].T), axis=0), onehot).reshape(3, H, 2 * seq)
    table = bias_tables(off3[0] + off3[1] + off3[2])
    y0, z1, u2, table, rounded, ffn_own = bar((y0, z1, u2, table, rounded, ffn_own))

    w_all = lax.all_gather(ffn_own, both, axis=0)
    w_all_k = w_all
    if own % 16:
        w_all_k = jnp.concatenate(
            [w_all[:, k * own : (k + 1) * own].reshape(4, -1, D) for k in range(2)] + [jnp.zeros((4, 8, D), b16)], axis=1)

    p0 = net.shift(y0, "c", 1)
    ga = jnp.sum(gate_proj[:HD, :4], axis=1)
    gb = jnp.sum(gate_proj[:HD, 4:], axis=1)
    za = jnp.sum(gate_proj[HD, :4])
    zb = jnp.sum(gate_proj[HD, 4:])
    eye = jnp.eye(H, dtype=f32)[:, :, None]
    wg = jnp.concatenate([(eye * ga).reshape(H, D), (eye * gb).reshape(H, D)], axis=0)
    wg3 = split3(wg)
    z3 = dot(jnp.concatenate(wg3, axis=0), rounded, NT).reshape(3, 2 * H, seq)
    z_all = z3[0] + z3[1] + z3[2]
    gate_a = jax.nn.sigmoid(z_all[:H] + za)
    gate_b = jax.nn.sigmoid(z_all[H:] + zb)
    const = pos_table[NB][:, None]
    gates = (gate_a * (gate_b * const - 1.0) + 2.0).reshape(H, 1, seq)
    rounded_t = rounded.T
    bias3 = jnp.stack([small_params[0], jnp.zeros((D,), f32), small_params[1]])[:, None, :]

    def attend(g, mine, peer, kept):
        at, mine, peer = wide_rows(net, places, mine, peer)
        bias = bias3[:, :, g * cols : (g + 1) * cols]
        return attn_fwd(lengths, at, rounded, mine, peer, bias, table, gates, g * group_heads, group_heads, kept)

    p0, z1, u2, gates, rounded_t = bar((p0, z1, u2, gates, rounded_t))
    y1 = net.gather(z1, "y", 0)
    z2 = net.gather(u2, "z", 1)
    probs0, *kept, q0, w0 = attend(0, y0, p0, ())
    y1, z2, probs0, q0, w0, *kept = bar((y1, z2, probs0, q0, w0, *kept))
    p1 = net.shift(y1, "c", 1)
    y2 = net.gather(z2, "y", 0)
    probs1, *kept, q1, w1 = attend(1, y1, p1, kept)
    y2, probs1, q1, w1, *kept = bar((y2, probs1, q1, w1, *kept))
    p2 = net.shift(y2, "c", 1)
    w_attn = natural(net, places, y2, p2)
    probs2, context, context_f, inv_sum, q2, w2 = attend(2, y2, p2, kept)
    qkv, w_qkv, probs = (q0, q1, q2), (w0, w1, w2), (probs0, probs1, probs2)
    r1, low = mix_out(context, w_attn, rounded, mask, small_params)

    bias_in = w_all[:, 2 * own, :own].reshape(1, -1).astype(f32)
    act, slope, layer_out, d_res2, d_branch, red2 = ffn_forward(
        lengths, low, w_all_k, bias_in, r1, cotangent[0], small_params)
    g_outw = dot(act, d_branch, TN).astype(b16)
    g_outw, d_branch = bar((g_outw, d_branch))
    g_outw = lax.psum_scatter(g_outw, both, scatter_dimension=0, tiled=True)
    d_hidden, g_bias_in, d_res1, d_attention, d_context, red1 = ffn_backward(
        d_branch, w_all_k, slope, d_res2, r1, w_attn, inv_sum, small_params)

    def attend_back(g):
        return attn_bwd(qkv[g], d_context, context_f, probs[g], table, gates, g * group_heads, group_heads)

    def by_owner(v):
        return v.reshape(zs, 2, 2, rows, v.shape[-1])

    g_keep, g_send = core_split_grads(places, d_hidden, low, t_size * own)
    g_got = net.shift(g_send, "c", 1)
    d0, dg0, do0 = attend_back(0)
    g_keep, g_got, d0, dg0, do0, d_context = bar((g_keep, g_got, d0, dg0, do0, d_context))
    gi = [v.reshape(zs, 2, t_size, own, D) for v in (g_keep, g_got)]
    part_a = [v[..., : own // 2, :] for v in gi]
    part_b = [v[..., own // 2 :, :] for v in gi]
    stay_a, got_a = net.scatter(part_a, "y", 1)
    stay_b, got_b = net.scatter(part_b, "x", 2)
    m1 = by_owner(weight_grads(rounded_t, d0, context, d_attention))
    stay_1, got_1 = net.scatter([m1], "c", 2)
    d1, dg1, do1 = attend_back(1)
    got_a, got_b, got_1, d1, dg1, do1, d_context = bar((got_a, got_b, got_1, d1, dg1, do1, d_context))
    stay_a, got_a = net.scatter(stay_a + got_a, "x", 1)
    stay_b, got_b = net.scatter(stay_b + got_b, "y", 1)
    stay_1, got_1 = net.scatter(stay_1 + got_1, "y", 1)
    d2, dg2, do2 = attend_back(2)
    got_a, got_b, got_1, d2, dg2, do2, g_outw = bar((got_a, got_b, got_1, d2, dg2, do2, g_outw))
    gi = jnp.concatenate([added(stay_a + got_a), added(stay_b + got_b)], axis=1).astype(b16)
    stay_i, got_i = net.scatter([gi], "z", 0)
    stay_1, got_1 = net.scatter(stay_1 + got_1, "z", 0)
    m2 = by_owner(weight_grads(rounded_t, d1, d2, jnp.zeros((8, 128), f32)))
    stay_2, got_2 = net.scatter([m2], "c", 2)

    dgate = jnp.concatenate([dg0, dg1, dg2], axis=0).reshape(H, seq)
    doff = jnp.concatenate([do0, do1, do2], axis=0).reshape(H, 2 * seq)
    d_a = dgate * (gate_b * const - 1.0) * gate_a * (1.0 - gate_a)
    d_b = dgate * gate_a * const * gate_b * (1.0 - gate_b)
    d_const = jnp.sum(dgate * gate_a * gate_b, axis=1)
    dz = jnp.concatenate([d_a, d_b], axis=0)
    dz_hi = dz.astype(b16)
    dz_lo = (dz - dz_hi.astype(f32)).astype(b16)
    feature_grad, red0 = input_grad(
        d_res1, (d0, d1, d2), w_qkv, jnp.concatenate([dz_hi, dz_lo, dz_hi], axis=0),
        jnp.concatenate([wg3[0], wg3[0], wg3[1]], axis=0), mask)
    g_z2 = dot(jnp.concatenate([dz_hi, dz_lo], axis=0), rounded).reshape(2, 2, H, H, HD)
    g_z = jnp.sum((g_z2[0] + g_z2[1]) * eye, axis=(1, 2))
    g_zb = jnp.sum(dz.reshape(2, H * seq), axis=1)
    g_gate_local = jnp.repeat(jnp.concatenate([g_z, g_zb[:, None]], axis=1).T, 4, axis=1)
    pos3 = dot(onehot, jnp.concatenate(split3(doff), axis=0), NT).reshape(NB, 3, H)
    pos_local = jnp.concatenate([jnp.sum(pos3, axis=1), d_const[None, :]], axis=0)
    small_local = jnp.concatenate([red0[:2], red1[:3], red2[:3], red0[2:3]], axis=0)

    got_i, got_1, got_2, feature_grad, small_local, pos_local, g_gate_local = bar(
        (got_i, got_1, got_2, feature_grad, small_local, pos_local, g_gate_local))
    g_in = added(stay_i + got_i)
    g_outw = g_outw.astype(f32)
    stay_2, got_2 = net.scatter(stay_2 + got_2, "y", 1)
    own_ffn = jnp.sum(jnp.square(g_in)) + jnp.sum(jnp.square(g_outw))
    m1 = added(stay_1 + got_1)
    got_2, own_ffn, m1 = bar((got_2, own_ffn, m1))
    stay_2, got_2 = net.scatter(stay_2 + got_2, "z", 0)
    m = jnp.stack([m1, added(stay_2 + got_2)]).astype(b16)
    m = tree_sum([m.astype(f32)] + [net.shift(m, "x", k).astype(f32) for k in range(1, t_size)])
    own_sum = jnp.sum(jnp.square(m)) * (1.0 / t_size) + own_ffn
    parts = [small_local, pos_local, g_gate_local, g_bias_in]
    counts = [p.size for p in parts]
    pad = -(sum(counts) + 1) % 1024
    flat = jnp.concatenate(
        [p.reshape(-1) for p in parts] + [own_sum.reshape(1), jnp.zeros((pad,), f32)]).reshape(-1, 128)
    flat = net.total(flat).reshape(-1)
    own_sum = flat[sum(counts)]
    m = m.reshape(2, rows, 2, 3, cols)
    g_qkv = jnp.stack([m[0, :, 0], m[1, :, 0], m[1, :, 1]], axis=2).transpose(1, 0, 2, 3).reshape(3, rows, D)
    g_out = m[0, :, 1].reshape(rows, D)
    pieces, at = [], 0
    for p, count in zip(parts, counts):
        pieces.append(flat[at : at + count].reshape(p.shape))
        at += count
    g_small, g_pos, g_gate, g_bias = pieces
    shared = sum(jnp.sum(jnp.square(p)) for p in pieces)
    grad_norm = jnp.sqrt(own_sum + shared)
    clip = jnp.minimum(1.0, CLIP_NORM / (grad_norm + 1e-06))
    count = step_count[0].astype(f32)
    me = lax.axis_index("dp") * t_size + lax.axis_index("tensor")
    g_bias = lax.dynamic_slice_in_dim(g_bias.reshape(-1, own), me, 1, 0)
    g_ffn_in = jnp.concatenate([g_in.T, g_bias], axis=0)

    qkv_new, qkv_moment, qkv_second = adam_step(qkv_w, g_qkv, qkv_m, qkv_v, clip, 2.0 * D**-0.5, count)
    out_new, out_moment, out_second = adam_step(out_w, g_out, out_m, out_v, clip, 1.0, count)
    in_new, in_moment, in_second = adam_step(ffn_in, g_ffn_in, ffn_in_m, ffn_in_v, clip, 2.0 * D**-0.5, count)
    fo_new, fo_moment, fo_second = adam_step(ffn_out, g_outw, ffn_out_m, ffn_out_v, clip, 2.0 * FF**-0.5, count)
    small_new, small_moment, small_second = adam_step(small_params, g_small, small_m, small_v, clip, 0.5, count)
    pos_new, pos_moment, pos_second = adam_step(pos_table, g_pos, pos_m, pos_v, clip, 1.0, count)
    gate_new, gate_moment, gate_second = adam_step(gate_proj, g_gate, gate_m, gate_v, clip, 2.0 * HD**-0.5, count)
    return (
        layer_out[None], feature_grad[None], grad_norm.reshape(1),
        qkv_new, qkv_moment, qkv_second, qkv_new.astype(b16),
        out_new, out_moment, out_second, out_new.astype(b16),
        in_new, in_moment, in_second, in_new.astype(b16),
        fo_new, fo_moment, fo_second, fo_new.astype(b16),
        g_small, small_new, small_moment, small_second,
        pos_new, pos_moment, pos_second, gate_new, gate_moment, gate_second,
    )


def solution(mesh):
    both = ("dp", "tensor")
    three = (P(None, "dp", None),)
    row = (P("dp", None),)
    col = (P(None, both),)
    rows2 = (P(both, None),)
    utt = P(both, None, None)
    in_specs = (
        (utt, P(both), P(both, None), P(), utt) + three * 3 + row * 3 + col * 3 + rows2 * 3 + (P(),) * 10
    )
    out_specs = (utt, utt, P()) + three * 4 + row * 4 + col * 4 + rows2 * 4 + (P(),) * 10
    fn = functools.partial(local, mesh.shape["dp"], mesh.shape["tensor"])
    return jax.shard_map(fn, mesh=mesh, in_specs=in_specs, out_specs=out_specs, check_vma=False)
```

time: 506 us -> 441 us (0.87)
  Pallas kernels: 78.8 us -> 193 us
  matrix products: 102 us -> 11.9 us
  waiting for transfers between devices: 133 us -> 63.4 us
  starting transfers between devices: 81.6 us -> 53.7 us
  between operations: 10.4 us -> 23.3 us
    pallas_call x3 -> x15, Pallas kernels: 78.8 us -> 193 us  [the longest x3 51.3 us: attn_fwd(): pl.pallas_call(functools.partial(fwd_kernel, seq=seq, ib=ib, zs=zs, rows=...]
    dot_general x26 -> x5, matrix products: 95.9 us -> 11.9 us  [dot(): return lax.dot_general(a, b, dims, preferred_element_type=jnp.float32)]
    ppermute x54 -> x40, waiting for transfers between devices: 133 us -> 55.8 us  [shift(): return lax.ppermute(v, ('dp', 'tensor'), pairs)]
    ppermute x54 -> x40, starting transfers between devices: 81.6 us -> 53.6 us  [shift(): return lax.ppermute(v, ('dp', 'tensor'), pairs)]
    convert_element_type x9 -> x12, other arithmetic: 4.27 us -> 14.6 us  [the longest x8 13.7 us: scatter(): send = added(slot((at + k) % n)).astype(jnp.bfloat16)]
    dynamic_update_slice x8 -> x0, local copies, waits for them, and re-layouts: 10.3 us -> none  [gather_own(): out = lax.dynamic_update_index_in_dim(out, part, (at + k) % n, dim)]
    reduce_sum x10 -> x2, other arithmetic: 11.1 us -> 1.36 us  [local(): own_ffn = jnp.sum(jnp.square(g_in)) + jnp.sum(jnp.square(g_outw))]
    all_gather x0 -> x1, waiting for transfers between devices: none -> 7.47 us  [local(): w_all = lax.all_gather(ffn_own, both, axis=0)]
  transfers between devices with their start and end apart: 54 -> 42, of which waited for: 18 -> 18; matrix products, arithmetic and copies ran while one was open for 21% -> 11% of each run, Pallas kernels for 8% -> 36%
where the time goes in v2:
time: 441 us; the launch traced here: 434 us
  Pallas kernels  193 us (44%)
  waiting for transfers between devices  63.4 us (14%)
  starting transfers between devices  53.7 us (12%)
  other arithmetic  49.4 us (11%)
  local copies, waits for them, and re-layouts  39.7 us (9%)
  between operations  23.3 us (5%)
  matrix products  11.9 us (3%)
    ppermute x40, waiting for transfers between devices, shift(): return lax.ppermute(v, ('dp', 'tensor'), pairs)  55.8 us
    ppermute x40, starting transfers between devices, shift(): return lax.ppermute(v, ('dp', 'tensor'), pairs)  53.6 us
    pallas_call x3, Pallas kernels, attn_fwd(): pl.pallas_call(functools.partial(fwd_kernel, seq=seq, ib=ib, zs=zs, rows=...  51.3 us
    pallas_call x3, Pallas kernels, attn_bwd(): pl.pallas_call(functools.partial(bwd_kernel, seq=seq, ib=ib), grid=(heads...  42.8 us
    pallas_call x1, Pallas kernels, ffn_backward(): pl.pallas_call(ffn_back_kernel, grid=(seq // block,), in_specs=[wide, pl....  22.4 us
    pallas_call x1, Pallas kernels, ffn_forward(): pl.pallas_call(functools.partial(ffn_kernel, block=block), grid_spec=pltp...  22.2 us
    pallas_call x2, Pallas kernels, weight_grads(): pl.pallas_call(functools.partial(wgrad_kernel, pair=pair), grid=(D // blo...  14 us
    convert_element_type x8, other arithmetic, scatter(): send = added(slot((at + k) % n)).astype(jnp.bfloat16)  13.7 us
  transfers between devices with their start and end apart: 42, of which 18 were waited for; matrix products, arithmetic and copies ran while one was open for 11% of the time, Pallas kernels for 36%

profile of v2, /device:TPU:0, one launch (start us, length us, event | category | flops | bytes accessed | tf_op | source)
XLA Modules:
  0.0 434.5 jit_solution(17224343644257563187)
XLA Ops:
  9.1 5.0 %collective-permute-start = (bf16[1,1,3,48,256]{4,3,2,1,0:T(8,128)(2,1)}, bf16[1,1,3,48,256]{4,3,2,1,0:T(8,128)(2,1)}, u32[]{:S(2)}, u32[]{:S(2)}) collective-permute-start(bf16[1,1,3,48,256]{4,3,2,1,0:T(8,128)(2,1)} %get-tuple-element.397), channel_id=1, source_target_pairs={{0,24},{1,25},{2,26},{3,27},{4,28},{5,29},{6,30},{7,31},{8,0},{9,1... | collective-permute-start | bytes 221192 | tf_op jit(solution)/shard_map/ppermute | solution.py:616
  26.3 2.9 collective-permute-start.4
  33.4 9.6 %shard_map.482.t_ref = f32[12,128,2048]{2,1,0:T(8,128)} custom-call(f32[12,1,2048]{2,1,0:T(1,128)} %add.631.off_ref), custom_call_target="tpu_custom_call" | custom-call | bytes 30000000 | tf_op jit(solution)/shard_map/pallas_call | solution.py:56
  59.3 17.0 %shard_map.483 = (bf16[4,1024,1024]{2,1,0:T(8,128)(2,1)}, bf16[1024,768]{1,0:T(8,128)(2,1)}, f32[1024,768]{1,0:T(8,128)}, f32[1024,768]{1,0:T(8,128)}, bf16[3,10...) custom-call(s32[1]{0:T(128)S(6)} %copy.335.len_ref, s32[4]{0:T(128)} %pad_add_fusion.at_ref, ...), custom_call_target="tpu_custom_call" | custom-call | bytes 44400000 | tf_op jit(solution)/shard_map/pallas_call | solution.py:167
  79.4 17.1 %shard_map.484 = (bf16[4,1024,1024]{2,1,0:T(8,128)(2,1)}, bf16[1024,768]{1,0:T(8,128)(2,1)}, f32[1024,768]{1,0:T(8,128)}, f32[1024,768]{1,0:T(8,128)}, bf16[3,10...) custom-call(s32[1]{0:T(128)S(6)} %copy.335.len_ref, ...), custom_call_target="tpu_custom_call", output_to_operand_aliasing={{1}: (8, {}), {2}: (9, {}), {3}: (10, {})} | custom-call | bytes 44400000 | tf_op jit(solution)/shard_map/pallas_call | solution.py:167
  100.8 3.8 shard_map.486.w_ref.wa_ref
  104.7 17.1 %shard_map.485 = (bf16[4,1024,1024]{2,1,0:T(8,128)(2,1)}, bf16[1024,768]{1,0:T(8,128)(2,1)}, f32[1024,768]{1,0:T(8,128)}, f32[1024,768]{1,0:T(8,128)}, bf16[3,10...) custom-call(s32[1]{0:T(128)S(6)} %copy.335.len_ref, ...), custom_call_target="tpu_custom_call", output_to_operand_aliasing={{1}: (8, {}), {2}: (9, {}), {3}: (10, {})} | custom-call | bytes 44400000 | tf_op jit(solution)/shard_map/pallas_call | solution.py:167
  121.8 6.6 %shard_map.487 = (f32[1024,768]{1,0:T(8,128)}, bf16[1024,768]{1,0:T(8,128)(2,1)}) custom-call(bf16[1024,768]{1,0:T(8,128)(2,1)} %get-tuple-element.177.c_ref.a_ref, bf16[768,768]{1,0:T(8,128)(2,1)} %shard_map.486.w_ref.wa_ref, bf16[1024,768]{1,0:T(8,128)(2,1)} %copy.255.x_ref, f32[1024,1]{1,0:T(8,128)} %copy.258.mask_ref, f32[9,768]{1,0:T(8,128)} %small_ref.5), custom_call_target="tpu_custom_call" | custom-call | bytes 12000000 | tf_op jit(solution)/shard_map/pallas_call | solution.py:358
  128.4 7.5 %all-gather.3.cloned.1.call-done = bf16[6400,768]{1,0:T(8,128)(2,1)} async-done(((bf16[200,768]{1,0:T(8,128)(2,1)}), bf16[6400,768]{1,0:T(8,128)(2,1)}) %all-gather.3.cloned.1.call-update) | async-done | bytes 9830416 | tf_op jit(solution)/shard_map/all_gather | solution.py:714
  137.4 22.2 %shard_map.488 = (bf16[1024,3072]{1,0:T(8,128)(2,1)}, bf16[1024,3072]{1,0:T(8,128)(2,1)}, f32[1024,768]{1,0:T(8,128)}, f32[1024,768]{1,0:T(8,128)}, bf16[1024,768]{1,0:T(8,128)(2,1)}, /*index=5*/f32[8,768]{1,0:T(8,128)}) custom-call(s32[1]{0:T(128)S(6)} %copy.335.len_ref, bf16[1024,768]{1,0:T(8,128)(2,1)} %get-tuple-element.179.low_ref.x_ref, ...), custom_call_target="tpu_custom_call" | custom-call | bytes 54000000 | tf_op jit(solution)/shard_map/pallas_call | solution.py:462
  159.7 9.1 %convolution_convert_fusion = bf16[3072,768]{1,0:T(8,128)(2,1)} fusion(bf16[1024,3072]{1,0:T(8,128)(2,1)} %get-tuple-element.183, bf16[1024,768]{1,0:T(8,128)(2,1)} %get-tuple-element.185.dlow_ref), kind=kOutput, calls=%fused_computation | convolution fusion | flops 4834197504 | bytes 12582912 | tf_op jit(solution)/shard_map/dot_general | solution.py:42
  168.8 22.4 %shard_map.489 = (bf16[1024,3072]{1,0:T(8,128)(2,1)}, f32[1,3072]{1,0:T(1,128)}, f32[1024,768]{1,0:T(8,128)}, bf16[1024,768]{1,0:T(8,128)(2,1)}, bf16[1024,768]{1,0:T(8,128)(2,1)}, /*index=5*/f32[8,768]{1,0:T(8,128)}) custom-call(bf16[1024,768]{1,0:T(8,128)(2,1)} %get-tuple-element.185.dlow_ref, bf16[32,200,768]{2,1,0:T(8,128)(2,1)} %bitcast.256, ...), custom_call_target="tpu_custom_call" | custom-call | bytes 54000000 | tf_op jit(solution)/shard_map/pallas_call | solution.py:517
  191.3 11.1 %shard_map.490 = (bf16[8,192,768]{2,1,0:T(8,128)(2,1)}, bf16[8,192,768]{2,1,0:T(8,128)(2,1)}) custom-call(s32[4]{0:T(128)} %pad_add_fusion.at_ref, bf16[1024,3072]{1,0:T(8,128)(2,1)} %get-tuple-element.189.d_ref, bf16[1024,768]{1,0:T(8,128)(2,1)} %get-tuple-element.179.low_ref.x_ref), custom_call_target="tpu_custom_call" | custom-call | bytes 24000000 | tf_op jit(solution)/shard_map/pallas_call | solution.py:322
  202.7 14.1 %shard_map.491 = (bf16[3,1024,256]{2,1,0:T(8,128)(2,1)}, f32[4,1,1024]{2,1,0:T(1,128)}, f32[4,1,2048]{2,1,0:T(1,128)}) custom-call(bf16[3,1024,256]{2,1,0:T(8,128)(2,1)} %get-tuple-element.192.q_ref.k_ref.v_ref, bf16[3,1024,256]{2,1,0:T(8,128)(2,1)} %get-tuple-element.192.q_ref.k_ref.v_ref, bf16[3,1024,256]{2,1,0:T(8,128)(2,1)} %get-tuple-element.192.q_ref.k_ref.v_ref, ...), custom_call_target="tpu_custom_call" | custom-call | bytes 36000000 | tf_op jit(solution)/shard_map/pallas_call | solution.py:249
  216.8 7.8 %shard_map.492 = bf16[768,1536]{1,0:T(8,128)(2,1)} custom-call(bf16[768,1024]{1,0:T(8,128)(2,1)} %bitcast.252, bf16[3,1024,256]{2,1,0:T(8,128)(2,1)} %get-tuple-element.202.d_ref.d0_ref, bf16[1024,768]{1,0:T(8,128)(2,1)} %get-tuple-element.177.c_ref.a_ref, bf16[1024,768]{1,0:T(8,128)(2,1)} %get-tuple-element.203.b_ref), custom_call_target="tpu_custom_call" | custom-call | bytes 15000000 | tf_op jit(solution)/shard_map/pallas_call | solution.py:295
  233.5 14.6 %shard_map.493 = (bf16[3,1024,256]{2,1,0:T(8,128)(2,1)}, f32[4,1,1024]{2,1,0:T(1,128)}, f32[4,1,2048]{2,1,0:T(1,128)}) custom-call(bf16[3,1024,256]{2,1,0:T(8,128)(2,1)} %get-tuple-element.204.q_ref.k_ref.v_ref, bf16[3,1024,256]{2,1,0:T(8,128)(2,1)} %get-tuple-element.204.q_ref.k_ref.v_ref, bf16[3,1024,256]{2,1,0:T(8,128)(2,1)} %get-tuple-element.204.q_ref.k_ref.v_ref, ...), custom_call_target="tpu_custom_call" | custom-call | bytes 36000000 | tf_op jit(solution)/shard_map/pallas_call | solution.py:249
  248.1 4.5 %collective-permute-done.16 = bf16[4,2,48,768]{3,2,0,1:T(8,128)(2,1)} collective-permute-done((bf16[4,2,48,768]{3,2,0,1:T(8,128)(2,1)}, bf16[4,2,48,768]{3,2,0,1:T(8,128)(2,1)}, u32[]{:S(2)}, u32[]{:S(2)}) %collective-permute-start.16) | collective-permute-done | bytes 589856 | tf_op jit(solution)/shard_map/ppermute | solution.py:616
  267.5 14.2 %shard_map.494 = (bf16[3,1024,256]{2,1,0:T(8,128)(2,1)}, f32[4,1,1024]{2,1,0:T(1,128)}, f32[4,1,2048]{2,1,0:T(1,128)}) custom-call(bf16[3,1024,256]{2,1,0:T(8,128)(2,1)} %get-tuple-element.213.q_ref.k_ref.v_ref, bf16[3,1024,256]{2,1,0:T(8,128)(2,1)} %get-tuple-element.213.q_ref.k_ref.v_ref, bf16[3,1024,256]{2,1,0:T(8,128)(2,1)} %get-tuple-element.213.q_ref.k_ref.v_ref, ...), custom_call_target="tpu_custom_call" | custom-call | bytes 36000000 | tf_op jit(solution)/shard_map/pallas_call | solution.py:249
  282.5 2.9 subtract_multiply_fusion.1
  287.7 9.3 %shard_map.496 = (f32[1024,768]{1,0:T(8,128)}, f32[8,768]{1,0:T(8,128)}) custom-call(f32[1024,768]{1,0:T(8,128)} %get-tuple-element.225.dr_ref, bf16[3,1024,256]{2,1,0:T(8,128)(2,1)} %get-tuple-element.202.d_ref.d0_ref, bf16[3,1024,256]{2,1,0:T(8,128)(2,1)} %get-tuple-element.223.d_ref.d1_ref, bf16[3,1024,256]{2,1,0:T(8,128)(2,1)} %get-tuple-element.224.a_ref.d2_ref, ...), custom_call_target="tpu_custom_call" | custom-call | bytes 24000000 | tf_op jit(solution)/shard_map/pallas_call | solution.py:564
  305.2 6.3 %shard_map.495 = bf16[768,1536]{1,0:T(8,128)(2,1)} custom-call(bf16[768,1024]{1,0:T(8,128)(2,1)} %bitcast.253, bf16[3,1024,256]{2,1,0:T(8,128)(2,1)} %get-tuple-element.223.d_ref.d1_ref, bf16[3,1024,256]{2,1,0:T(8,128)(2,1)} %get-tuple-element.224.a_ref.d2_ref, f32[8,128]{1,0:T(8,128)} %broadcast_in_dim.63.b_ref), custom_call_target="tpu_custom_call" | custom-call | bytes 15000000 | tf_op jit(solution)/shard_map/pallas_call | solution.py:295
  317.9 2.8 collective-permute-start.27
  326.4 5.0 %collective-permute-done.26 = bf16[48,1536]{1,0:T(8,128)(2,1)} collective-permute-done((bf16[48,1536]{1,0:T(8,128)(2,1)}, bf16[48,1536]{1,0:T(8,128)(2,1)}, u32[]{:S(2)}, u32[]{:S(2)}) %collective-permute-start.26) | collective-permute-done | bytes 147488 | tf_op jit(solution)/shard_map/ppermute | solution.py:616
  331.4 3.8 collective-permute-start.24
  335.9 7.6 %collective-permute-done.23 = bf16[96,768]{1,0:T(8,128)(2,1)S(1)} collective-permute-done((bf16[96,768]{1,0:T(8,128)(2,1)}, bf16[96,768]{1,0:T(8,128)(2,1)S(1)}, u32[]{:S(2)}, u32[]{:S(2)}) %collective-permute-start.23) | collective-permute-done | bytes 147488 | tf_op jit(solution)/shard_map/ppermute | solution.py:616
  351.0 10.4 %collective-permute-done.29 = bf16[4,48,1536]{2,1,0:T(8,128)(2,1)} collective-permute-done((bf16[4,48,1536]{2,1,0:T(8,128)(2,1)}, bf16[4,48,1536]{2,1,0:T(8,128)(2,1)}, u32[]{:S(2)}, u32[]{:S(2)}) %collective-permute-start.29) | collective-permute-done | bytes 589856 | tf_op jit(solution)/shard_map/ppermute | solution.py:616
  362.8 3.8 collective-permute-start.30
  370.9 5.4 %collective-permute-done.31 = bf16[48,1536]{1,0:T(8,128)(2,1)S(1)} collective-permute-done((bf16[48,1536]{1,0:T(8,128)(2,1)S(1)}, bf16[48,1536]{1,0:T(8,128)(2,1)S(1)}, u32[]{:S(2)}, u32[]{:S(2)}) %collective-permute-start.31) | collective-permute-done | bytes 147488 | tf_op jit(solution)/shard_map/ppermute | solution.py:616
  379.5 6.8 %collective-permute-done.33 = bf16[2,48,1536]{2,1,0:T(8,128)(2,1)S(1)} collective-permute-done((bf16[2,48,1536]{2,1,0:T(8,128)(2,1)S(1)}, bf16[2,48,1536]{2,1,0:T(8,128)(2,1)S(1)}, u32[]{:S(2)}, u32[]{:S(2)}) %collective-permute-start.33) | collective-permute-done | bytes 294944 | tf_op jit(solution)/shard_map/ppermute | solution.py:616
  397.8 2.8 collective-permute-start.37
  400.6 3.4 collective-permute-start.38
  405.8 4.2 collective-permute-done.39
  (358 shorter events, 130.0 us)
Async XLA Ops:
  7.2 128.6 %all-gather.3.cloned.1.call-start = ((), (), s32[]{:S(2)}) async-start(), calls=%async_computation.2 | async-start | bytes 10137600 | tf_op jit(solution)/shard_map/all_gather | solution.py:714
  9.1 16.1 %collective-permute-start = (bf16[1,1,3,48,256]{4,3,2,1,0:T(8,128)(2,1)}, bf16[1,1,3,48,256]{4,3,2,1,0:T(8,128)(2,1)}, u32[]{:S(2)}, u32[]{:S(2)}) collective-permute-start(bf16[1,1,3,48,256]{4,3,2,1,0:T(8,128)(2,1)} %get-tuple-element.397), channel_id=1, source_target_pairs={{0,24},{1,25},{2,26},{3,27},{4,28},{5,29},{6,30},{7,31},{8,0},{9,1... | collective-permute-start | bytes 221192 | tf_op jit(solution)/shard_map/ppermute | solution.py:616
  14.2 11.1 %collective-permute-start.1 = (bf16[1,1,3,48,256]{4,3,2,1,0:T(8,128)(2,1)}, bf16[1,1,3,48,256]{4,3,2,1,0:T(8,128)(2,1)}, u32[]{:S(2)}, u32[]{:S(2)}) collective-permute-start(bf16[1,1,3,48,256]{4,3,2,1,0:T(8,128)(2,1)} %get-tuple-element.397), channel_id=1, source_target_pairs={{0,16},{1,17},{2,18},{3,19},{4,20},{5,21},{6,22},{7,23},{8,24},{9,... | collective-permute-start | bytes 221192 | tf_op jit(solution)/shard_map/ppermute | solution.py:616
  14.2 11.1 %collective-permute-start.2 = (bf16[1,1,3,48,256]{4,3,2,1,0:T(8,128)(2,1)}, bf16[1,1,3,48,256]{4,3,2,1,0:T(8,128)(2,1)}, u32[]{:S(2)}, u32[]{:S(2)}) collective-permute-start(bf16[1,1,3,48,256]{4,3,2,1,0:T(8,128)(2,1)} %get-tuple-element.397), channel_id=1, source_target_pairs={{0,8},{1,9},{2,10},{3,11},{4,12},{5,13},{6,14},{7,15},{8,16},{9,17... | collective-permute-start | bytes 221192 | tf_op jit(solution)/shard_map/ppermute | solution.py:616
  26.3 16.7 %collective-permute-start.4 = (bf16[1,1,3,48,256]{4,3,2,1,0:T(8,128)(2,1)S(1)}, bf16[1,1,3,48,256]{4,3,2,1,0:T(8,128)(2,1)S(1)}, u32[]{:S(2)}, u32[]{:S(2)}) collective-permute-start(bf16[1,1,3,48,256]{4,3,2,1,0:T(8,128)(2,1)S(1)} %get-tuple-element.143), channel_id=1, source_target_pairs={{0,24},{1,25},{2,26},{3,27},{4,28},{5,29},{6,30},{7,31},{8,0},{9,1... | collective-permute-start | bytes 221192 | tf_op jit(solution)/shard_map/ppermute | solution.py:616
  29.2 13.8 %collective-permute-start.5 = (bf16[1,1,3,48,256]{4,3,2,1,0:T(8,128)(2,1)S(1)}, bf16[1,1,3,48,256]{4,3,2,1,0:T(8,128)(2,1)S(1)}, u32[]{:S(2)}, u32[]{:S(2)}) collective-permute-start(bf16[1,1,3,48,256]{4,3,2,1,0:T(8,128)(2,1)S(1)} %get-tuple-element.143), channel_id=1, source_target_pairs={{0,16},{1,17},{2,18},{3,19},{4,20},{5,21},{6,22},{7,23},{8,24},{9,... | collective-permute-start | bytes 221192 | tf_op jit(solution)/shard_map/ppermute | solution.py:616
  30.3 12.7 %collective-permute-start.6 = (bf16[1,1,3,48,256]{4,3,2,1,0:T(8,128)(2,1)S(1)}, bf16[1,1,3,48,256]{4,3,2,1,0:T(8,128)(2,1)S(1)}, u32[]{:S(2)}, u32[]{:S(2)}) collective-permute-start(bf16[1,1,3,48,256]{4,3,2,1,0:T(8,128)(2,1)S(1)} %get-tuple-element.143), channel_id=1, source_target_pairs={{0,8},{1,9},{2,10},{3,11},{4,12},{5,13},{6,14},{7,15},{8,16},{9,17... | collective-permute-start | bytes 221192 | tf_op jit(solution)/shard_map/ppermute | solution.py:616
  30.5 12.6 %collective-permute-start.3 = (bf16[1,4,3,48,256]{4,3,2,1,0:T(8,128)(2,1)S(1)}, bf16[1,4,3,48,256]{4,3,2,1,0:T(8,128)(2,1)}, u32[]{:S(2)}, u32[]{:S(2)}) collective-permute-start(bf16[1,4,3,48,256]{4,3,2,1,0:T(8,128)(2,1)S(1)} %pad_maximum_fusion.4), channel_id=1, source_target_pairs={{0,4},{1,5},{2,6},{3,7},{4,0},{5,1},{6,2},{7,3},{8,12},{9,13},{10,... | collective-permute-start | bytes 884744 | tf_op jit(solution)/shard_map/ppermute | solution.py:616
  44.1 237.6 %reduce-scatter.2.cloned.1.call-start = ((), (), s32[]{:S(2)}) async-start(), calls=%async_computation.1 | async-start | bytes 4866048 | tf_op jit(solution)/shard_map/reduce_scatter | solution.py:762
  48.6 27.8 %collective-permute-start.10 = (bf16[1,1,6,48,256]{4,3,2,1,0:T(8,128)(2,1)S(1)}, bf16[1,1,6,48,256]{4,3,2,1,0:T(8,128)(2,1)S(1)}, u32[]{:S(2)}, u32[]{:S(2)}) collective-permute-start(bf16[1,1,6,48,256]{4,3,2,1,0:T(8,128)(2,1)S(1)} %pad_maximum_fusion.7), channel_id=1, source_target_pairs={{0,16},{1,17},{2,18},{3,19},{4,20},{5,21},{6,22},{7,23},{8,24},{9,... | collective-permute-start | bytes 442376 | tf_op jit(solution)/shard_map/ppermute | solution.py:616
  50.4 26.0 %collective-permute-start.11 = (bf16[1,1,6,48,256]{4,3,2,1,0:T(8,128)(2,1)S(1)}, bf16[1,1,6,48,256]{4,3,2,1,0:T(8,128)(2,1)S(1)}, u32[]{:S(2)}, u32[]{:S(2)}) collective-permute-start(bf16[1,1,6,48,256]{4,3,2,1,0:T(8,128)(2,1)S(1)} %pad_maximum_fusion.7), channel_id=1, source_target_pairs={{0,8},{1,9},{2,10},{3,11},{4,12},{5,13},{6,14},{7,15},{8,16},{9,17... | collective-permute-start | bytes 442376 | tf_op jit(solution)/shard_map/ppermute | solution.py:616
  52.9 23.4 %collective-permute-start.9 = (bf16[1,1,6,48,256]{4,3,2,1,0:T(8,128)(2,1)S(1)}, bf16[1,1,6,48,256]{4,3,2,1,0:T(8,128)(2,1)S(1)}, u32[]{:S(2)}, u32[]{:S(2)}) collective-permute-start(bf16[1,1,6,48,256]{4,3,2,1,0:T(8,128)(2,1)S(1)} %pad_maximum_fusion.7), channel_id=1, source_target_pairs={{0,24},{1,25},{2,26},{3,27},{4,28},{5,29},{6,30},{7,31},{8,0},{9,1... | collective-permute-start | bytes 442376 | tf_op jit(solution)/shard_map/ppermute | solution.py:616
  54.2 22.2 %collective-permute-start.8 = (bf16[1,4,3,48,256]{4,3,2,1,0:T(8,128)(2,1)S(1)}, bf16[1,4,3,48,256]{4,3,2,1,0:T(8,128)(2,1)S(1)}, u32[]{:S(2)}, u32[]{:S(2)}) collective-permute-start(bf16[1,4,3,48,256]{4,3,2,1,0:T(8,128)(2,1)S(1)} %pad_maximum_fusion.5), channel_id=1, source_target_pairs={{0,4},{1,5},{2,6},{3,7},{4,0},{5,1},{6,2},{7,3},{8,12},{9,13},{10,... | collective-permute-start | bytes 884744 | tf_op jit(solution)/shard_map/ppermute | solution.py:616
  76.6 20.1 %collective-permute-start.12 = (bf16[1,4,6,48,256]{4,3,2,1,0:T(8,128)(2,1)S(1)}, bf16[1,4,6,48,256]{4,3,2,1,0:T(8,128)(2,1)S(1)}, u32[]{:S(2)}, u32[]{:S(2)}) collective-permute-start(bf16[1,4,6,48,256]{4,3,2,1,0:T(8,128)(2,1)S(1)} %pad_maximum_fusion.3), channel_id=1, source_target_pairs={{0,4},{1,5},{2,6},{3,7},{4,0},{5,1},{6,2},{7,3},{8,12},{9,13},{10,... | collective-permute-start | bytes 1769480 | tf_op jit(solution)/shard_map/ppermute | solution.py:616
  202.4 14.4 %collective-permute-start.15 = (bf16[8,192,768]{2,1,0:T(8,128)(2,1)}, bf16[8,192,768]{2,1,0:T(8,128)(2,1)S(1)}, u32[]{:S(2)}, u32[]{:S(2)}) collective-permute-start(bf16[8,192,768]{2,1,0:T(8,128)(2,1)} %get-tuple-element.191), channel_id=1, source_target_pairs={{0,2},{1,3},{2,0},{3,1},{4,6},{5,7},{6,4},{7,5},{8,10},{9,11},{10,... | collective-permute-start | bytes 7077896 | tf_op jit(solution)/shard_map/ppermute | solution.py:616
  227.2 25.4 %collective-permute-start.18 = (bf16[4,2,48,1536]{3,2,1,0:T(8,128)(2,1)}, bf16[4,2,48,1536]{3,2,1,0:T(8,128)(2,1)}, u32[]{:S(2)}, u32[]{:S(2)}) collective-permute-start(bf16[4,2,48,1536]{3,2,1,0:T(8,128)(2,1)} %dynamic-slice_bitcast_fusion.1), channel_id=1, source_target_pairs={{0,2},{1,3},{2,0},{3,1},{4,6},{5,7},{6,4},{7,5},{8,10},{9,11},{10,... | collective-permute-start | bytes 3538952 | tf_op jit(solution)/shard_map/ppermute | solution.py:616
  230.5 17.6 %collective-permute-start.17 = (bf16[4,2,48,768]{3,2,0,1:T(8,128)(2,1)}, bf16[4,2,48,768]{3,2,0,1:T(8,128)(2,1)}, u32[]{:S(2)}, u32[]{:S(2)}) collective-permute-start(bf16[4,2,48,768]{3,2,0,1:T(8,128)(2,1)} %fusion.8), channel_id=1, source_target_pairs={{0,1},{1,0},{2,3},{3,2},{4,5},{5,4},{6,7},{7,6},{8,9},{9,8},{10,11... | collective-permute-start | bytes 1769480 | tf_op jit(solution)/shard_map/ppermute | solution.py:616
  233.0 19.6 %collective-permute-start.16 = (bf16[4,2,48,768]{3,2,0,1:T(8,128)(2,1)}, bf16[4,2,48,768]{3,2,0,1:T(8,128)(2,1)}, u32[]{:S(2)}, u32[]{:S(2)}) collective-permute-start(bf16[4,2,48,768]{3,2,0,1:T(8,128)(2,1)} %fusion.7), channel_id=1, source_target_pairs={{0,4},{1,5},{2,6},{3,7},{4,0},{5,1},{6,2},{7,3},{8,12},{9,13},{10,... | collective-permute-start | bytes 1769480 | tf_op jit(solution)/shard_map/ppermute | solution.py:616
  254.8 26.9 %collective-permute-start.21 = (bf16[4,48,1536]{2,1,0:T(8,128)(2,1)}, bf16[4,48,1536]{2,1,0:T(8,128)(2,1)}, u32[]{:S(2)}, u32[]{:S(2)}) collective-permute-start(bf16[4,48,1536]{2,1,0:T(8,128)(2,1)} %fusion.5), channel_id=1, source_target_pairs={{0,4},{1,5},{2,6},{3,7},{4,0},{5,1},{6,2},{7,3},{8,12},{9,13},{10,... | collective-permute-start | bytes 1769480 | tf_op jit(solution)/shard_map/ppermute | solution.py:616
  257.1 24.6 %collective-permute-start.20 = (bf16[4,48,768]{2,1,0:T(8,128)(2,1)}, bf16[4,48,768]{2,1,0:T(8,128)(2,1)}, u32[]{:S(2)}, u32[]{:S(2)}) collective-permute-start(bf16[4,48,768]{2,1,0:T(8,128)(2,1)} %fusion.12), channel_id=1, source_target_pairs={{0,4},{1,5},{2,6},{3,7},{4,0},{5,1},{6,2},{7,3},{8,12},{9,13},{10,... | collective-permute-start | bytes 884744 | tf_op jit(solution)/shard_map/ppermute | solution.py:616
  260.5 21.1 %collective-permute-start.19 = (bf16[4,48,768]{2,1,0:T(8,128)(2,1)}, bf16[4,48,768]{2,1,0:T(8,128)(2,1)}, u32[]{:S(2)}, u32[]{:S(2)}) collective-permute-start(bf16[4,48,768]{2,1,0:T(8,128)(2,1)} %fusion.13), channel_id=1, source_target_pairs={{0,1},{1,0},{2,3},{3,2},{4,5},{5,4},{6,7},{7,6},{8,9},{9,8},{10,11... | collective-permute-start | bytes 884744 | tf_op jit(solution)/shard_map/ppermute | solution.py:616
  313.9 29.7 %collective-permute-start.28 = (bf16[4,2,48,1536]{3,2,1,0:T(8,128)(2,1)}, bf16[4,2,48,1536]{3,2,1,0:T(8,128)(2,1)}, u32[]{:S(2)}, u32[]{:S(2)}) collective-permute-start(bf16[4,2,48,1536]{3,2,1,0:T(8,128)(2,1)} %dynamic-slice_bitcast_fusion), channel_id=1, source_target_pairs={{0,2},{1,3},{2,0},{3,1},{4,6},{5,7},{6,4},{7,5},{8,10},{9,11},{10,... | collective-permute-start | bytes 3538952 | tf_op jit(solution)/shard_map/ppermute | solution.py:616
  316.1 9.0 %collective-permute-start.25 = (bf16[48,1536]{1,0:T(8,128)(2,1)}, bf16[48,1536]{1,0:T(8,128)(2,1)}, u32[]{:S(2)}, u32[]{:S(2)}) collective-permute-start(bf16[48,1536]{1,0:T(8,128)(2,1)} %get-tuple-element.381), channel_id=1, source_target_pairs={{0,8},{1,9},{2,10},{3,11},{4,12},{5,13},{6,14},{7,15},{8,16},{9,17... | collective-permute-start | bytes 442376 | tf_op jit(solution)/shard_map/ppermute | solution.py:616
  317.6 13.8 %collective-permute-start.26 = (bf16[48,1536]{1,0:T(8,128)(2,1)}, bf16[48,1536]{1,0:T(8,128)(2,1)}, u32[]{:S(2)}, u32[]{:S(2)}) collective-permute-start(bf16[48,1536]{1,0:T(8,128)(2,1)} %get-tuple-element.380), channel_id=1, source_target_pairs={{0,16},{1,17},{2,18},{3,19},{4,20},{5,21},{6,22},{7,23},{8,24},{9,... | collective-permute-start | bytes 442376 | tf_op jit(solution)/shard_map/ppermute | solution.py:616
  317.9 18.1 %collective-permute-start.27 = (bf16[48,1536]{1,0:T(8,128)(2,1)}, bf16[48,1536]{1,0:T(8,128)(2,1)}, u32[]{:S(2)}, u32[]{:S(2)}) collective-permute-start(bf16[48,1536]{1,0:T(8,128)(2,1)} %get-tuple-element.379), channel_id=1, source_target_pairs={{0,24},{1,25},{2,26},{3,27},{4,28},{5,29},{6,30},{7,31},{8,0},{9,1... | collective-permute-start | bytes 442376 | tf_op jit(solution)/shard_map/ppermute | solution.py:616
  324.4 11.6 %collective-permute-start.22 = (bf16[96,768]{1,0:T(8,128)(2,1)}, bf16[96,768]{1,0:T(8,128)(2,1)S(1)}, u32[]{:S(2)}, u32[]{:S(2)}) collective-permute-start(bf16[96,768]{1,0:T(8,128)(2,1)} %get-tuple-element.393), channel_id=1, source_target_pairs={{0,8},{1,9},{2,10},{3,11},{4,12},{5,13},{6,14},{7,15},{8,16},{9,17... | collective-permute-start | bytes 442376 | tf_op jit(solution)/shard_map/ppermute | solution.py:616
  325.1 18.4 %collective-permute-start.23 = (bf16[96,768]{1,0:T(8,128)(2,1)}, bf16[96,768]{1,0:T(8,128)(2,1)S(1)}, u32[]{:S(2)}, u32[]{:S(2)}) collective-permute-start(bf16[96,768]{1,0:T(8,128)(2,1)} %get-tuple-element.394), channel_id=1, source_target_pairs={{0,16},{1,17},{2,18},{3,19},{4,20},{5,21},{6,22},{7,23},{8,24},{9,... | collective-permute-start | bytes 442376 | tf_op jit(solution)/shard_map/ppermute | solution.py:616
  331.4 12.1 %collective-permute-start.24 = (bf16[96,768]{1,0:T(8,128)(2,1)}, bf16[96,768]{1,0:T(8,128)(2,1)S(1)}, u32[]{:S(2)}, u32[]{:S(2)}) collective-permute-start(bf16[96,768]{1,0:T(8,128)(2,1)} %get-tuple-element.392), channel_id=1, source_target_pairs={{0,24},{1,25},{2,26},{3,27},{4,28},{5,29},{6,30},{7,31},{8,0},{9,1... | collective-permute-start | bytes 442376 | tf_op jit(solution)/shard_map/ppermute | solution.py:616
  345.6 15.8 %collective-permute-start.29 = (bf16[4,48,1536]{2,1,0:T(8,128)(2,1)}, bf16[4,48,1536]{2,1,0:T(8,128)(2,1)}, u32[]{:S(2)}, u32[]{:S(2)}) collective-permute-start(bf16[4,48,1536]{2,1,0:T(8,128)(2,1)} %fusion.4), channel_id=1, source_target_pairs={{0,4},{1,5},{2,6},{3,7},{4,0},{5,1},{6,2},{7,3},{8,12},{9,13},{10,... | collective-permute-start | bytes 1769480 | tf_op jit(solution)/shard_map/ppermute | solution.py:616
  366.6 9.7 %collective-permute-start.31 = (bf16[48,1536]{1,0:T(8,128)(2,1)S(1)}, bf16[48,1536]{1,0:T(8,128)(2,1)S(1)}, u32[]{:S(2)}, u32[]{:S(2)}) collective-permute-start(bf16[48,1536]{1,0:T(8,128)(2,1)S(1)} %get-tuple-element.378), channel_id=1, source_target_pairs={{0,16},{1,17},{2,18},{3,19},{4,20},{5,21},{6,22},{7,23},{8,24},{9,... | collective-permute-start | bytes 442376 | tf_op jit(solution)/shard_map/ppermute | solution.py:616
  367.0 9.3 %collective-permute-start.32 = (bf16[48,1536]{1,0:T(8,128)(2,1)S(1)}, bf16[48,1536]{1,0:T(8,128)(2,1)S(1)}, u32[]{:S(2)}, u32[]{:S(2)}) collective-permute-start(bf16[48,1536]{1,0:T(8,128)(2,1)S(1)} %get-tuple-element.377), channel_id=1, source_target_pairs={{0,24},{1,25},{2,26},{3,27},{4,28},{5,29},{6,30},{7,31},{8,0},{9,1... | collective-permute-start | bytes 442376 | tf_op jit(solution)/shard_map/ppermute | solution.py:616
  377.4 8.9 %collective-permute-start.33 = (bf16[2,48,1536]{2,1,0:T(8,128)(2,1)S(1)}, bf16[2,48,1536]{2,1,0:T(8,128)(2,1)S(1)}, u32[]{:S(2)}, u32[]{:S(2)}) collective-permute-start(bf16[2,48,1536]{2,1,0:T(8,128)(2,1)S(1)} %pad_maximum_fusion.6), channel_id=1, source_target_pairs={{0,1},{1,0},{2,3},{3,2},{4,5},{5,4},{6,7},{7,6},{8,9},{9,8},{10,11... | collective-permute-start | bytes 884744 | tf_op jit(solution)/shard_map/ppermute | solution.py:616
  (80 other events, 443.1 us)
Sparse Core Ops, SparseCore 0:
  44.3 91.5 all-gather.2
  168.9 109.2 reduce-scatter.1

commit v3 on v2

--- a/solution.py
+++ b/solution.py
@@ -47,20 +47,24 @@
 
 
 def table_kernel(off_ref, out_ref):
-    row = jnp.broadcast_to(off_ref[0], out_ref.shape[1:])
-    out_ref[0] = pltpu.roll(row, 0, 1, stride=1, stride_axis=0)
-
-
-def bias_tables(offr):
+    heads, _, w = out_ref.shape
+    for h in range(heads):
+        row = jnp.broadcast_to(off_ref[h], (8, w))
+        eight = pltpu.roll(row, 0, 1, stride=1, stride_axis=0)
+        for r in range(0, 128, 8):
+            out_ref[h, r : r + 8] = pltpu.roll(eight, r, 1) if r else eight
+
+
+def bias_tables(offr, heads=4):
     n, w = offr.shape
     return pl.pallas_call(
         table_kernel,
-        grid=(n,),
-        in_specs=[pl.BlockSpec((1, 1, w), lambda h: (h, 0, 0))],
-        out_specs=pl.BlockSpec((1, 128, w), lambda h: (h, 0, 0)),
+        grid=(n // heads,),
+        in_specs=[pl.BlockSpec((heads, 1, w), lambda h: (h, 0, 0))],
+        out_specs=pl.BlockSpec((heads, 128, w), lambda h: (h, 0, 0)),
         out_shape=jax.ShapeDtypeStruct((n, 128, w), jnp.float32),
         compiler_params=pltpu.CompilerParams(vmem_limit_bytes=VMEM),
-        cost_estimate=cost(10),
+        cost_estimate=cost(8),
     )(offr.reshape(n, 1, w))
 
 
@@ -132,20 +136,25 @@
     vm = jnp.where(flag, one, qkv_ref[2, :, pair])
     vt = vm.T
     base = seq - 128
-    for i0 in range(0, seq, ib):
+    def scores(i0):
         gate = g_ref[0, :, i0 : i0 + ib]
         qb = qm[i0 : i0 + ib]
         m = None
         for j0 in range(0, seq, 128):
             c0 = i0 - j0 + base
             s = dot(km[j0 : j0 + 128], qb, NT) + t_ref[0, :, c0 : c0 + ib] * gate
-            s_ref[j0 : j0 + 128, :] = s
+            s_ref[i0 // ib % 2, j0 : j0 + 128, :] = s
             mm = jnp.max(s.reshape(16, 8, ib), axis=0)
             m = mm if m is None else jnp.maximum(m, mm)
-        m = jnp.max(m, axis=0, keepdims=True)
+        return jnp.max(m, axis=0, keepdims=True)
+
+    m = scores(0)
+    for i0 in range(0, seq, ib):
+        m_next = scores(i0 + ib) if i0 + ib < seq else None
         for j0 in range(0, seq, 128):
-            e = jnp.exp(s_ref[j0 : j0 + 128, :] - m).astype(jnp.bfloat16)
+            e = jnp.exp(s_ref[i0 // ib % 2, j0 : j0 + 128, :] - m).astype(jnp.bfloat16)
             p_ref[0, j0 : j0 + 128, i0 : i0 + ib] = e
+        m = m_next
         ct = dot(vt, p_ref[0, :, i0 : i0 + ib])
         total = jnp.where(par == 0, ct[64:65], ct[0:1])
         rl = 1.0 / total
@@ -180,7 +189,7 @@
             out_specs=[pl.BlockSpec((1, seq, seq), lambda h, n, a: (h, 0, 0)), out_pair, out_pair, out_pair,
                        pl.BlockSpec((3, seq, cols), lambda h, n, a: (0, 0, 0)),
                        pl.BlockSpec((3, D, cols), lambda h, n, a: (0, 0, 0))],
-            scratch_shapes=[pltpu.VMEM((seq, ib), f32), pltpu.SemaphoreType.DMA((4 * zs,))],
+            scratch_shapes=[pltpu.VMEM((2, seq, ib), f32), pltpu.SemaphoreType.DMA((4 * zs,))],
         ),
         out_shape=[jax.ShapeDtypeStruct((heads, seq, seq), b16), jax.ShapeDtypeStruct((seq, D), b16),
                    jax.ShapeDtypeStruct((seq, D), f32), jax.ShapeDtypeStruct((seq, D), f32),
@@ -303,32 +312,29 @@
     )(xt, d3, a, b)
 
 
-def core_split_kernel(at_ref, d_ref, x_ref, keep_ref, send_ref, *, wide, places):
-    g = dot(d_ref[...], x_ref[...], TN).astype(jnp.bfloat16)
-    first = at_ref[2] == 0
-    for k in range(places):
-        low = g[2 * k * wide : (2 * k + 1) * wide]
-        high = g[(2 * k + 1) * wide : (2 * k + 2) * wide]
-        keep_ref[k] = jnp.where(first, low, high)
-        send_ref[k] = jnp.where(first, high, low)
-
-
-def core_split_grads(at, d, x, wide):
-    seq, units = d.shape
-    places = max(1, 384 // (2 * wide))
-    cols = places * 2 * wide
-    out = pl.BlockSpec((places, wide, D), lambda i: (i, 0, 0))
-    shape = jax.ShapeDtypeStruct((units // (2 * wide), wide, D), jnp.bfloat16)
+def ffn_grad_kernel(dh_ref, act_ref, low_ref, dlow_ref, g_ref):
+    per, two, _ = g_ref.shape
+    own = two // 2
+    g_ref[:, :own] = dot(dh_ref[...], low_ref[...], TN).astype(jnp.bfloat16).reshape(per, own, D)
+    g_ref[:, own:] = dot(act_ref[...], dlow_ref[...], TN).astype(jnp.bfloat16).reshape(per, own, D)
+
+
+def ffn_grads(dh, act, low, dlow, own, cols=768):
+    seq = dh.shape[0]
+    if own % 16:
+        parts = [dot(a, b, TN).astype(jnp.bfloat16).reshape(-1, own, D) for a, b in ((dh, low), (act, dlow))]
+        return jnp.concatenate(parts, axis=1)
+    hidden = pl.BlockSpec((seq, cols), lambda i: (0, i))
+    wide = pl.BlockSpec((seq, D), lambda i: (0, 0))
     return pl.pallas_call(
-        functools.partial(core_split_kernel, wide=wide, places=places),
-        grid=(units // cols,),
-        in_specs=[pl.BlockSpec(memory_space=pltpu.SMEM), pl.BlockSpec((seq, cols), lambda i: (0, i)),
-                  pl.BlockSpec((seq, D), lambda i: (0, 0))],
-        out_specs=[out, out],
-        out_shape=[shape, shape],
+        ffn_grad_kernel,
+        grid=(FF // cols,),
+        in_specs=[hidden, hidden, wide, wide],
+        out_specs=pl.BlockSpec((cols // own, 2 * own, D), lambda i: (i, 0, 0)),
+        out_shape=jax.ShapeDtypeStruct((FF // own, 2 * own, D), jnp.bfloat16),
         compiler_params=pltpu.CompilerParams(vmem_limit_bytes=VMEM),
-        cost_estimate=cost(8),
-    )(at, d, x)
+        cost_estimate=cost(16),
+    )(dh, act, low, dlow)
 
 
 def row_norm(r):
@@ -341,30 +347,6 @@
 def row_norm_back(cot, n, inv, gain):
     e = cot * gain
     return inv * (e - jnp.mean(e, axis=-1, keepdims=True) - n * jnp.mean(e * n, axis=-1, keepdims=True))
-
-
-def mix_kernel(c_ref, w_ref, x_ref, mask_ref, small_ref, r_ref, low_ref):
-    att = dot(c_ref[...], w_ref[...])
-    mixed = jnp.where(mask_ref[...] > 0.5, small_ref[8:9], x_ref[...].astype(jnp.float32))
-    r = mixed + att + small_ref[2:3]
-    n, _ = row_norm(r)
-    r_ref[...] = r
-    low_ref[...] = (n * small_ref[3:4] + small_ref[4:5]).astype(jnp.bfloat16)
-
-
-def mix_out(ctx, w_attn, rounded, mask, small, block=256):
-    seq = rounded.shape[0]
-    wide = pl.BlockSpec((block, D), lambda i: (i, 0))
-    return pl.pallas_call(
-        mix_kernel,
-        grid=(seq // block,),
-        in_specs=[wide, pl.BlockSpec((D, D), lambda i: (0, 0)), wide,
-                  pl.BlockSpec((block, 1), lambda i: (i, 0)), pl.BlockSpec((9, D), lambda i: (0, 0))],
-        out_specs=[wide, wide],
-        out_shape=[jax.ShapeDtypeStruct((seq, D), jnp.float32), jax.ShapeDtypeStruct((seq, D), jnp.bfloat16)],
-        compiler_params=pltpu.CompilerParams(vmem_limit_bytes=VMEM),
-        cost_estimate=cost(4),
-    )(ctx, w_attn, rounded, mask, small)
 
 
 def gelu_both(x):
@@ -407,127 +389,99 @@
         body(per, len(copies), lambda c: None)
 
 
-def ffn_kernel(len_ref, low_ref, w_ref, b_ref, r_ref, cot_ref, small_ref,
-               act_ref, slope_ref, out_ref, dres_ref, dlow_ref, red_ref, wi_ref, wo_ref, sem, *, block):
-    i = pl.program_id(0)
-
-    @pl.when(i == 0)
-    def _():
-        red_ref[...] = jnp.zeros_like(red_ref)
-
-    def body(per, chunks, wait):
-        low = low_ref[...]
-        acc = None
-        for c in range(chunks):
-            wait(c)
-            cols = slice(c * 768, c * 768 + 768)
-            hid = dot(low, wi_ref[c * per : c * per + per].reshape(-1, D), NT) + b_ref[:, cols]
-            act, slo = gelu_both(hid)
-            act = act.astype(jnp.bfloat16)
-            act_ref[:, cols] = act
-            slope_ref[:, cols] = slo.astype(jnp.bfloat16)
-            part = dot(act, wo_ref[c * per : c * per + per].reshape(-1, D))
-            acc = part if acc is None else acc + part
-        n1, _ = row_norm(r_ref[...])
-        first = n1 * small_ref[3:4] + small_ref[4:5]
-        n, inv = row_norm(first + (acc + small_ref[7:8]))
-        out_ref[...] = n * small_ref[5:6] + small_ref[6:7]
-        at = lax.broadcasted_iota(jnp.int32, (block, D), 0) + i * block
-        cot = jnp.where(at < len_ref[0], cot_ref[...].astype(jnp.float32), 0.0)
-        dres = row_norm_back(cot, n, inv, small_ref[5:6])
-        dlow = dres.astype(jnp.bfloat16)
-        dres_ref[...] = dres
-        dlow_ref[...] = dlow
-        for k, v in enumerate((cot * n, cot, dlow.astype(jnp.float32))):
-            red_ref[k : k + 1] += jnp.sum(v, axis=0, keepdims=True)
-
-    by_step(w_ref, wi_ref, wo_ref, sem, body)
-
-
-def ffn_scratch(w_all):
+def ffn_scratch(w_all, block):
     owners, rows, _ = w_all.shape
     own = (rows - 8) // 2
     return [
         pltpu.VMEM((owners, own, D), jnp.bfloat16),
         pltpu.VMEM((owners, own, D), jnp.bfloat16),
+        pltpu.VMEM((block, FF), jnp.bfloat16),
         pltpu.SemaphoreType.DMA((2, owners * own // 768)),
     ]
 
 
-def ffn_forward(length, low, w_all, bias, r1, cot, small, block=256):
-    seq = low.shape[0]
-    wide = pl.BlockSpec((block, D), lambda i, n: (i, 0))
-    hidden = pl.BlockSpec((block, FF), lambda i, n: (i, 0))
+def middle_kernel(len_ref, c_ref, wa_ref, x_ref, mask_ref, w_ref, b_ref, cot_ref, rl_ref, small_ref,
+                  low_ref, act_ref, dh_ref, dlow_ref, out_ref, dr1_ref, da_ref, dc_ref, gb_ref, red_ref,
+                  wi_ref, wo_ref, slope_ref, sem, *, block):
+    i = pl.program_id(0)
     f32, b16 = jnp.float32, jnp.bfloat16
-    return pl.pallas_call(
-        functools.partial(ffn_kernel, block=block),
-        grid_spec=pltpu.PrefetchScalarGridSpec(
-            num_scalar_prefetch=1,
-            grid=(seq // block,),
-            in_specs=[wide, pl.BlockSpec(memory_space=pl.ANY), pl.BlockSpec((1, FF), lambda i, n: (0, 0)), wide, wide,
-                      pl.BlockSpec((9, D), lambda i, n: (0, 0))],
-            out_specs=[hidden, hidden, wide, wide, wide, pl.BlockSpec((8, D), lambda i, n: (0, 0))],
-            scratch_shapes=ffn_scratch(w_all),
-        ),
-        out_shape=[jax.ShapeDtypeStruct((seq, FF), b16), jax.ShapeDtypeStruct((seq, FF), b16),
-                   jax.ShapeDtypeStruct((seq, D), f32), jax.ShapeDtypeStruct((seq, D), f32),
-                   jax.ShapeDtypeStruct((seq, D), b16), jax.ShapeDtypeStruct((8, D), f32)],
-        compiler_params=pltpu.CompilerParams(vmem_limit_bytes=VMEM),
-        cost_estimate=cost(18),
-    )(length, low, w_all, bias, r1, cot, small)
-
-
-def ffn_back_kernel(dlow_ref, w_ref, slope_ref, dres_ref, r_ref, wa_ref, rl_ref, small_ref,
-                    dh_ref, gb_ref, dr1_ref, da_ref, dc_ref, red_ref, wi_ref, wo_ref, sem):
-    @pl.when(pl.program_id(0) == 0)
+
+    @pl.when(i == 0)
     def _():
         red_ref[...] = jnp.zeros_like(red_ref)
         gb_ref[...] = jnp.zeros_like(gb_ref)
 
     def body(per, chunks, wait):
-        dlow = dlow_ref[...]
+        def weights(ref, c):
+            return ref[c * per : c * per + per].reshape(-1, D)
+
+        mixed = jnp.where(mask_ref[...] > 0.5, small_ref[8:9], x_ref[...].astype(f32))
+        n1, inv1 = row_norm(mixed + dot(c_ref[...], wa_ref[...]) + small_ref[2:3])
+        first = n1 * small_ref[3:4] + small_ref[4:5]
+        low = first.astype(b16)
+        low_ref[...] = low
         acc = None
         for c in range(chunks):
             wait(c)
             cols = slice(c * 768, c * 768 + 768)
-            dh = dot(dlow, wo_ref[c * per : c * per + per].reshape(-1, D), NT) * slope_ref[:, cols].astype(jnp.float32)
-            dh = dh.astype(jnp.bfloat16)
+            act, slo = gelu_both(dot(low, weights(wi_ref, c), NT) + b_ref[:, cols])
+            act = act.astype(b16)
+            act_ref[:, cols] = act
+            slope_ref[:, cols] = slo.astype(b16)
+            part = dot(act, weights(wo_ref, c))
+            acc = part if acc is None else acc + part
+        n2, inv2 = row_norm(first + (acc + small_ref[7:8]))
+        out_ref[...] = n2 * small_ref[5:6] + small_ref[6:7]
+        at = lax.broadcasted_iota(jnp.int32, (block, D), 0) + i * block
+        cot = jnp.where(at < len_ref[0], cot_ref[...].astype(f32), 0.0)
+        dres = row_norm_back(cot, n2, inv2, small_ref[5:6])
+        dlow = dres.astype(b16)
+        dlow_ref[...] = dlow
+        for k, v in enumerate((cot * n2, cot, dlow.astype(f32))):
+            red_ref[3 + k : 4 + k] += jnp.sum(v, axis=0, keepdims=True)
+        acc = dres
+        for c in range(chunks):
+            cols = slice(c * 768, c * 768 + 768)
+            dh = (dot(dlow, weights(wo_ref, c), NT) * slope_ref[:, cols].astype(f32)).astype(b16)
             dh_ref[:, cols] = dh
-            gb_ref[:, cols] += jnp.sum(dh.astype(jnp.float32), axis=0, keepdims=True)
-            part = dot(dh, wi_ref[c * per : c * per + per].reshape(-1, D))
-            acc = part if acc is None else acc + part
-        n, inv = row_norm(r_ref[...])
-        dfirst = dres_ref[...] + acc
-        dr1 = row_norm_back(dfirst, n, inv, small_ref[3:4])
-        low = dr1.astype(jnp.bfloat16)
+            gb_ref[:, cols] += jnp.sum(dh.astype(f32), axis=0, keepdims=True)
+            acc = acc + dot(dh, weights(wi_ref, c))
+        dr1 = row_norm_back(acc, n1, inv1, small_ref[3:4])
+        da = dr1.astype(b16)
         dr1_ref[...] = dr1
-        da_ref[...] = low
-        dc_ref[...] = (dot(low, wa_ref[...], NT) * rl_ref[...]).astype(jnp.bfloat16)
-        for k, v in enumerate((low.astype(jnp.float32), dfirst * n, dfirst)):
+        da_ref[...] = da
+        dc_ref[...] = (dot(da, wa_ref[...], NT) * rl_ref[...]).astype(b16)
+        for k, v in enumerate((da.astype(f32), acc * n1, acc)):
             red_ref[k : k + 1] += jnp.sum(v, axis=0, keepdims=True)
 
     by_step(w_ref, wi_ref, wo_ref, sem, body)
 
 
-def ffn_backward(dlow, w_all, slope, dres, r1, w_attn, rl, small, block=256):
-    seq = dlow.shape[0]
-    wide = pl.BlockSpec((block, D), lambda i: (i, 0))
-    hidden = pl.BlockSpec((block, FF), lambda i: (i, 0))
+def middle(length, ctx, w_attn, rounded, mask, w_all, bias, cot, rl, small, block=256):
+    seq = ctx.shape[0]
+    wide = pl.BlockSpec((block, D), lambda i, n: (i, 0))
+    hidden = pl.BlockSpec((block, FF), lambda i, n: (i, 0))
+    one = pl.BlockSpec((1, FF), lambda i, n: (0, 0))
     f32, b16 = jnp.float32, jnp.bfloat16
+
+    def shape(cols, kind, rows=seq):
+        return jax.ShapeDtypeStruct((rows, cols), kind)
+
     return pl.pallas_call(
-        ffn_back_kernel,
-        grid=(seq // block,),
-        in_specs=[wide, pl.BlockSpec(memory_space=pl.ANY), hidden, wide, wide,
-                  pl.BlockSpec((D, D), lambda i: (0, 0)), wide, pl.BlockSpec((9, D), lambda i: (0, 0))],
-        out_specs=[hidden, pl.BlockSpec((1, FF), lambda i: (0, 0)),
-                   wide, wide, wide, pl.BlockSpec((8, D), lambda i: (0, 0))],
-        out_shape=[jax.ShapeDtypeStruct((seq, FF), b16), jax.ShapeDtypeStruct((1, FF), f32),
-                   jax.ShapeDtypeStruct((seq, D), f32), jax.ShapeDtypeStruct((seq, D), b16),
-                   jax.ShapeDtypeStruct((seq, D), b16), jax.ShapeDtypeStruct((8, D), f32)],
-        scratch_shapes=ffn_scratch(w_all),
+        functools.partial(middle_kernel, block=block),
+        grid_spec=pltpu.PrefetchScalarGridSpec(
+            num_scalar_prefetch=1,
+            grid=(seq // block,),
+            in_specs=[wide, pl.BlockSpec((D, D), lambda i, n: (0, 0)), wide, pl.BlockSpec((block, 1), lambda i, n: (i, 0)),
+                      pl.BlockSpec(memory_space=pl.ANY), one, wide, wide, pl.BlockSpec((9, D), lambda i, n: (0, 0))],
+            out_specs=[wide, hidden, hidden, wide, wide, wide, wide, wide, one, pl.BlockSpec((8, D), lambda i, n: (0, 0))],
+            scratch_shapes=ffn_scratch(w_all, block),
+        ),
+        out_shape=[shape(D, b16), shape(FF, b16), shape(FF, b16), shape(D, b16), shape(D, f32), shape(D, f32),
+                   shape(D, b16), shape(D, b16), shape(FF, f32, 1), shape(D, f32, 8)],
         compiler_params=pltpu.CompilerParams(vmem_limit_bytes=VMEM),
-        cost_estimate=cost(18),
-    )(dlow, w_all, slope, dres, r1, w_attn, rl, small)
+        cost_estimate=cost(40),
+    )(length, ctx, w_attn, rounded, mask, w_all, bias, cot, rl, small)
 
 
 def input_kernel(dr_ref, d0_ref, d1_ref, d2_ref, w0_ref, w1_ref, w2_ref, z_ref, wg_ref, mask_ref,
@@ -601,7 +555,7 @@
         d = lax.axis_index("dp")
         self.at = {"z": d // 4, "y": d // 2 % 2, "c": d % 2, "x": lax.axis_index("tensor")}
 
-    def shift(self, v, axis, k):
+    def shift(self, v, axis, k, swap=False):
         pairs = []
         sz = self.sizes
         for z in range(sz["z"]):
@@ -610,7 +564,7 @@
                     for x in range(sz["x"]):
                         src = {"z": z, "y": y, "c": c, "x": x}
                         dst = dict(src)
-                        dst[axis] = (src[axis] - k) % sz[axis]
+                        dst[axis] = src[axis] ^ k if swap else (src[axis] - k) % sz[axis]
                         flat = [((q["z"] * 2 + q["y"]) * 2 + q["c"]) * sz["x"] + q["x"] for q in (src, dst)]
                         pairs.append(tuple(flat))
         return lax.ppermute(v, ("dp", "tensor"), pairs)
@@ -642,7 +596,10 @@
 
     def total(self, v, axes=("c", "x", "y", "z")):
         for axis in axes:
-            v = tree_sum([v] + [self.shift(v, axis, k) for k in range(1, self.sizes[axis])])
+            bit = 1
+            while bit < self.sizes[axis]:
+                v = v + self.shift(v, axis, bit, True)
+                bit *= 2
         return v
 
 
@@ -687,37 +644,31 @@
     group_heads = H // GROUPS
     both = ("dp", "tensor")
 
+    qkv_low = qkv_w[None, None]
+    u0, u1, u2 = [qkv_low[..., g * cols : (g + 1) * cols].astype(b16) for g in range(3)]
+    z0 = net.gather(u0, "z", 1)
+    rev = jnp.flip(buckets)
+    order = jnp.concatenate([rev[127:], jnp.full((1,), -1, jnp.int32), rev[:127]])
+    onehot = (jnp.arange(NB, dtype=jnp.int32)[:, None] == order[None, :]).astype(b16)
+    off3 = dot(jnp.concatenate(split3(pos_table[:NB].T), axis=0), onehot).reshape(3, H, 2 * seq)
+    table = bias_tables(off3[0] + off3[1] + off3[2])
     bias_row = jnp.pad(ffn_in[D:].astype(b16), ((0, 7), (0, D - own)))
     ffn_own = jnp.concatenate([ffn_in[:D].T.astype(b16), ffn_out.astype(b16), bias_row])
-
-    qkv_low = qkv_w.astype(b16)[None, None]
-    u0, u1, u2 = [qkv_low[..., g * cols : (g + 1) * cols] for g in range(3)]
-    out_parts = out_w.astype(b16).reshape(rows, 3, cols).transpose(1, 0, 2)[None, None]
-    u2 = jnp.concatenate([u2, out_parts], axis=2)
+    z0, u1, table, features, ffn_own, out_w, gate_proj = bar((z0, u1, table, features, ffn_own, out_w, gate_proj))
+
+    w_all = lax.all_gather(ffn_own, both, axis=0)
+    w_all_k = w_all
+    if own % 16:
+        w_all_k = jnp.concatenate(
+            [w_all[:, k * own : (k + 1) * own].reshape(4, -1, D) for k in range(2)] + [jnp.zeros((4, 8, D), b16)], axis=1)
+
+    y0 = net.gather(z0, "y", 0)
+    z1 = net.gather(u1, "z", 1)
     positions = jnp.arange(seq, dtype=jnp.int32)
     starts = span_starts[0]
     masked = jnp.any((positions[:, None] >= starts[None, :]) & (positions[:, None] < starts[None, :] + SPAN), axis=1)[:, None]
     mask = masked.astype(f32)
     rounded = jnp.where(masked, small_params[8][None, :].astype(b16), features[0])
-    z0 = net.gather(u0, "z", 1)
-    z0, u1, u2, rounded, mask, buckets = bar((z0, u1, u2, rounded, mask, buckets))
-
-    y0 = net.gather(z0, "y", 0)
-    z1 = net.gather(u1, "z", 1)
-    rev = jnp.flip(buckets)
-    order = jnp.concatenate([rev[127:], jnp.full((1,), -1, jnp.int32), rev[:127]])
-    onehot = (jnp.arange(NB, dtype=jnp.int32)[:, None] == order[None, :]).astype(b16)
-    off3 = dot(jnp.concatenate(split3(pos_table[:NB].T), axis=0), onehot).reshape(3, H, 2 * seq)
-    table = bias_tables(off3[0] + off3[1] + off3[2])
-    y0, z1, u2, table, rounded, ffn_own = bar((y0, z1, u2, table, rounded, ffn_own))
-
-    w_all = lax.all_gather(ffn_own, both, axis=0)
-    w_all_k = w_all
-    if own % 16:
-        w_all_k = jnp.concatenate(
-            [w_all[:, k * own : (k + 1) * own].reshape(4, -1, D) for k in range(2)] + [jnp.zeros((4, 8, D), b16)], axis=1)
-
-    p0 = net.shift(y0, "c", 1)
     ga = jnp.sum(gate_proj[:HD, :4], axis=1)
     gb = jnp.sum(gate_proj[:HD, 4:], axis=1)
     za = jnp.sum(gate_proj[HD, :4])
@@ -733,13 +684,18 @@
     gates = (gate_a * (gate_b * const - 1.0) + 2.0).reshape(H, 1, seq)
     rounded_t = rounded.T
     bias3 = jnp.stack([small_params[0], jnp.zeros((D,), f32), small_params[1]])[:, None, :]
+    out_parts = out_w.astype(b16).reshape(rows, 3, cols).transpose(1, 0, 2)[None, None]
+    u2 = jnp.concatenate([u2, out_parts], axis=2)
+    y0, z1, u2, rounded, gates, rounded_t = bar((y0, z1, u2, rounded, gates, rounded_t))
+
+    p0 = net.shift(y0, "c", 1)
 
     def attend(g, mine, peer, kept):
         at, mine, peer = wide_rows(net, places, mine, peer)
         bias = bias3[:, :, g * cols : (g + 1) * cols]
         return attn_fwd(lengths, at, rounded, mine, peer, bias, table, gates, g * group_heads, group_heads, kept)
 
-    p0, z1, u2, gates, rounded_t = bar((p0, z1, u2, gates, rounded_t))
+    p0, z1, u2 = bar((p0, z1, u2))
     y1 = net.gather(z1, "y", 0)
     z2 = net.gather(u2, "z", 1)
     probs0, *kept, q0, w0 = attend(0, y0, p0, ())
@@ -752,16 +708,10 @@
     w_attn = natural(net, places, y2, p2)
     probs2, context, context_f, inv_sum, q2, w2 = attend(2, y2, p2, kept)
     qkv, w_qkv, probs = (q0, q1, q2), (w0, w1, w2), (probs0, probs1, probs2)
-    r1, low = mix_out(context, w_attn, rounded, mask, small_params)
 
     bias_in = w_all[:, 2 * own, :own].reshape(1, -1).astype(f32)
-    act, slope, layer_out, d_res2, d_branch, red2 = ffn_forward(
-        lengths, low, w_all_k, bias_in, r1, cotangent[0], small_params)
-    g_outw = dot(act, d_branch, TN).astype(b16)
-    g_outw, d_branch = bar((g_outw, d_branch))
-    g_outw = lax.psum_scatter(g_outw, both, scatter_dimension=0, tiled=True)
-    d_hidden, g_bias_in, d_res1, d_attention, d_context, red1 = ffn_backward(
-        d_branch, w_all_k, slope, d_res2, r1, w_attn, inv_sum, small_params)
+    low, act, d_hidden, d_branch, layer_out, d_res1, d_attention, d_context, g_bias_in, red = middle(
+        lengths, context, w_attn, rounded, mask, w_all_k, bias_in, cotangent[0], inv_sum, small_params)
 
     def attend_back(g):
         return attn_bwd(qkv[g], d_context, context_f, probs[g], table, gates, g * group_heads, group_heads)
@@ -769,27 +719,18 @@
     def by_owner(v):
         return v.reshape(zs, 2, 2, rows, v.shape[-1])
 
-    g_keep, g_send = core_split_grads(places, d_hidden, low, t_size * own)
-    g_got = net.shift(g_send, "c", 1)
+    g_ffn = ffn_grads(d_hidden, act, low, d_branch, own)
+    g_ffn, d_context = bar((g_ffn, d_context))
+    g_ffn = lax.psum_scatter(g_ffn.reshape(dp_size, t_size, 2 * own, D), "dp", scatter_dimension=0, tiled=False)
     d0, dg0, do0 = attend_back(0)
-    g_keep, g_got, d0, dg0, do0, d_context = bar((g_keep, g_got, d0, dg0, do0, d_context))
-    gi = [v.reshape(zs, 2, t_size, own, D) for v in (g_keep, g_got)]
-    part_a = [v[..., : own // 2, :] for v in gi]
-    part_b = [v[..., own // 2 :, :] for v in gi]
-    stay_a, got_a = net.scatter(part_a, "y", 1)
-    stay_b, got_b = net.scatter(part_b, "x", 2)
     m1 = by_owner(weight_grads(rounded_t, d0, context, d_attention))
+    m1, d0, dg0, do0, d_context = bar((m1, d0, dg0, do0, d_context))
     stay_1, got_1 = net.scatter([m1], "c", 2)
     d1, dg1, do1 = attend_back(1)
-    got_a, got_b, got_1, d1, dg1, do1, d_context = bar((got_a, got_b, got_1, d1, dg1, do1, d_context))
-    stay_a, got_a = net.scatter(stay_a + got_a, "x", 1)
-    stay_b, got_b = net.scatter(stay_b + got_b, "y", 1)
+    got_1, d1, dg1, do1, d_context = bar((got_1, d1, dg1, do1, d_context))
     stay_1, got_1 = net.scatter(stay_1 + got_1, "y", 1)
     d2, dg2, do2 = attend_back(2)
-    got_a, got_b, got_1, d2, dg2, do2, g_outw = bar((got_a, got_b, got_1, d2, dg2, do2, g_outw))
-    gi = jnp.concatenate([added(stay_a + got_a), added(stay_b + got_b)], axis=1).astype(b16)
-    stay_i, got_i = net.scatter([gi], "z", 0)
-    stay_1, got_1 = net.scatter(stay_1 + got_1, "z", 0)
+    got_1, d2, dg2, do2 = bar((got_1, d2, dg2, do2))
     m2 = by_owner(weight_grads(rounded_t, d1, d2, jnp.zeros((8, 128), f32)))
     stay_2, got_2 = net.scatter([m2], "c", 2)
 
@@ -801,51 +742,57 @@
     dz = jnp.concatenate([d_a, d_b], axis=0)
     dz_hi = dz.astype(b16)
     dz_lo = (dz - dz_hi.astype(f32)).astype(b16)
-    feature_grad, red0 = input_grad(
-        d_res1, (d0, d1, d2), w_qkv, jnp.concatenate([dz_hi, dz_lo, dz_hi], axis=0),
-        jnp.concatenate([wg3[0], wg3[0], wg3[1]], axis=0), mask)
     g_z2 = dot(jnp.concatenate([dz_hi, dz_lo], axis=0), rounded).reshape(2, 2, H, H, HD)
     g_z = jnp.sum((g_z2[0] + g_z2[1]) * eye, axis=(1, 2))
     g_zb = jnp.sum(dz.reshape(2, H * seq), axis=1)
     g_gate_local = jnp.repeat(jnp.concatenate([g_z, g_zb[:, None]], axis=1).T, 4, axis=1)
     pos3 = dot(onehot, jnp.concatenate(split3(doff), axis=0), NT).reshape(NB, 3, H)
     pos_local = jnp.concatenate([jnp.sum(pos3, axis=1), d_const[None, :]], axis=0)
-    small_local = jnp.concatenate([red0[:2], red1[:3], red2[:3], red0[2:3]], axis=0)
-
-    got_i, got_1, got_2, feature_grad, small_local, pos_local, g_gate_local = bar(
-        (got_i, got_1, got_2, feature_grad, small_local, pos_local, g_gate_local))
-    g_in = added(stay_i + got_i)
-    g_outw = g_outw.astype(f32)
+    got_2, got_1, dz_hi, dz_lo, pos_local, g_gate_local, d_res1 = bar(
+        (got_2, got_1, dz_hi, dz_lo, pos_local, g_gate_local, d_res1))
     stay_2, got_2 = net.scatter(stay_2 + got_2, "y", 1)
-    own_ffn = jnp.sum(jnp.square(g_in)) + jnp.sum(jnp.square(g_outw))
-    m1 = added(stay_1 + got_1)
-    got_2, own_ffn, m1 = bar((got_2, own_ffn, m1))
-    stay_2, got_2 = net.scatter(stay_2 + got_2, "z", 0)
-    m = jnp.stack([m1, added(stay_2 + got_2)]).astype(b16)
-    m = tree_sum([m.astype(f32)] + [net.shift(m, "x", k).astype(f32) for k in range(1, t_size)])
-    own_sum = jnp.sum(jnp.square(m)) * (1.0 / t_size) + own_ffn
+    stay_1, got_1 = net.scatter(stay_1 + got_1, "z", 0)
+    feature_grad, red0 = input_grad(
+        d_res1, (d0, d1, d2), w_qkv, jnp.concatenate([dz_hi, dz_lo, dz_hi], axis=0),
+        jnp.concatenate([wg3[0], wg3[0], wg3[1]], axis=0), mask)
+    small_local = jnp.concatenate([red0[:2], red[:6], red0[2:3]], axis=0)
+
     parts = [small_local, pos_local, g_gate_local, g_bias_in]
     counts = [p.size for p in parts]
     pad = -(sum(counts) + 1) % 1024
-    flat = jnp.concatenate(
-        [p.reshape(-1) for p in parts] + [own_sum.reshape(1), jnp.zeros((pad,), f32)]).reshape(-1, 128)
+    packed = jnp.concatenate([p.reshape(-1) for p in parts])
+    got_2, got_1, feature_grad, packed = bar((got_2, got_1, feature_grad, packed))
+    stay_2, got_2 = net.scatter(stay_2 + got_2, "z", 0)
+    m1 = added(stay_1 + got_1).astype(b16)
+    m1 = tree_sum([m1.astype(f32)] + [net.shift(m1, "x", k).astype(f32) for k in range(1, t_size)])
+    got_2, m1, g_ffn = bar((got_2, m1, g_ffn))
+    m2 = added(stay_2 + got_2).astype(b16)
+    m2 = tree_sum([m2.astype(f32)] + [net.shift(m2, "x", k).astype(f32) for k in range(1, t_size)])
+    stay_f, got_f = net.scatter([g_ffn], "x", 0)
+    g_ffn = added(stay_f + got_f)
+    own_ffn = jnp.sum(jnp.square(g_ffn)) + jnp.sum(jnp.square(m1)) * (1.0 / t_size)
+    g_in_t = g_ffn[:own].T
+    g_outw = g_ffn[own:]
+    own_sum = jnp.sum(jnp.square(m2)) * (1.0 / t_size) + own_ffn
+    flat = jnp.concatenate([packed, own_sum.reshape(1), jnp.zeros((pad,), f32)]).reshape(-1, 128)
     flat = net.total(flat).reshape(-1)
     own_sum = flat[sum(counts)]
-    m = m.reshape(2, rows, 2, 3, cols)
-    g_qkv = jnp.stack([m[0, :, 0], m[1, :, 0], m[1, :, 1]], axis=2).transpose(1, 0, 2, 3).reshape(3, rows, D)
-    g_out = m[0, :, 1].reshape(rows, D)
+    shared = jnp.sum(jnp.where(jnp.arange(flat.size) < sum(counts), flat * flat, 0.0))
+    m1 = m1.reshape(rows, 2, 3, cols)
+    m2 = m2.reshape(rows, 2, 3, cols)
+    g_qkv = jnp.stack([m1[:, 0], m2[:, 0], m2[:, 1]], axis=2).transpose(1, 0, 2, 3).reshape(3, rows, D)
+    g_out = m1[:, 1].reshape(rows, D)
     pieces, at = [], 0
     for p, count in zip(parts, counts):
         pieces.append(flat[at : at + count].reshape(p.shape))
         at += count
     g_small, g_pos, g_gate, g_bias = pieces
-    shared = sum(jnp.sum(jnp.square(p)) for p in pieces)
     grad_norm = jnp.sqrt(own_sum + shared)
     clip = jnp.minimum(1.0, CLIP_NORM / (grad_norm + 1e-06))
     count = step_count[0].astype(f32)
     me = lax.axis_index("dp") * t_size + lax.axis_index("tensor")
     g_bias = lax.dynamic_slice_in_dim(g_bias.reshape(-1, own), me, 1, 0)
-    g_ffn_in = jnp.concatenate([g_in.T, g_bias], axis=0)
+    g_ffn_in = jnp.concatenate([g_in_t, g_bias], axis=0)
 
     qkv_new, qkv_moment, qkv_second = adam_step(qkv_w, g_qkv, qkv_m, qkv_v, clip, 2.0 * D**-0.5, count)
     out_new, out_moment, out_second = adam_step(out_w, g_out, out_m, out_v, clip, 1.0, count)

time: 441 us -> 377 us (0.85)
  waiting for transfers between devices: 63.4 us -> 38.5 us
  Pallas kernels: 193 us -> 179 us
  matrix products: 11.9 us -> 2.76 us
  starting transfers between devices: 53.7 us -> 46.9 us
  other arithmetic: 49.4 us -> 43.9 us
    ppermute x40 -> x33, waiting for transfers between devices: 55.8 us -> 38.4 us  [shift(): return lax.ppermute(v, ('dp', 'tensor'), pairs)]
    pallas_call x5 -> x3, Pallas kernels: 71.9 us -> 61.9 us  [the longest x1 39.3 us: middle(): pl.pallas_call(functools.partial(middle_kernel, block=block), grid_spec=p...]
    dot_general x5 -> x4, matrix products: 11.9 us -> 2.76 us  [dot(): return lax.dot_general(a, b, dims, preferred_element_type=jnp.float32)]
    all_gather x1, waiting for transfers between devices: 7.47 us -> 0.02 us  [local(): w_all = lax.all_gather(ffn_own, both, axis=0)]
    ppermute x40 -> x33, starting transfers between devices: 53.6 us -> 46.8 us  [shift(): return lax.ppermute(v, ('dp', 'tensor'), pairs)]
    convert_element_type x8 -> x4, other arithmetic: 13.7 us -> 8.03 us  [scatter(): send = added(slot((at + k) % n)).astype(jnp.bfloat16)]
  transfers between devices with their start and end apart: 42 -> 35, of which waited for: 18 -> 15; matrix products, arithmetic and copies ran while one was open for 11% -> 18% of each run, Pallas kernels for 36% -> 34%
where the time goes in v3:
time: 377 us; the launch traced here: 370 us
  Pallas kernels  179 us (47%)
  starting transfers between devices  46.9 us (12%)
  other arithmetic  43.9 us (12%)
  waiting for transfers between devices  38.5 us (10%)
  local copies, waits for them, and re-layouts  37.8 us (10%)
  between operations  21.3 us (6%)
    pallas_call x3, Pallas kernels, attn_fwd(): pl.pallas_call(functools.partial(fwd_kernel, seq=seq, ib=ib, zs=zs, rows=...  48.1 us
    ppermute x33, starting transfers between devices, shift(): return lax.ppermute(v, ('dp', 'tensor'), pairs)  46.8 us
    pallas_call x3, Pallas kernels, attn_bwd(): pl.pallas_call(functools.partial(bwd_kernel, seq=seq, ib=ib), grid=(heads...  42.8 us
    pallas_call x1, Pallas kernels, middle(): pl.pallas_call(functools.partial(middle_kernel, block=block), grid_spec=p...  39.3 us
    ppermute x33, waiting for transfers between devices, shift(): return lax.ppermute(v, ('dp', 'tensor'), pairs)  38.4 us
    pallas_call x1, Pallas kernels, ffn_grads(): pl.pallas_call(ffn_grad_kernel, grid=(FF // cols,), in_specs=[hidden, hid...  15 us
    pallas_call x2, Pallas kernels, weight_grads(): pl.pallas_call(functools.partial(wgrad_kernel, pair=pair), grid=(D // blo...  13.8 us
    pallas_call x1, Pallas kernels, input_grad(): pl.pallas_call(input_kernel, grid=(seq // block,), in_specs=[wide, part,...  9.32 us
  transfers between devices with their start and end apart: 35, of which 15 were waited for; matrix products, arithmetic and copies ran while one was open for 18% of the time, Pallas kernels for 34%

profile of v3, /device:TPU:0, one launch (start us, length us, event | category | flops | bytes accessed | tf_op | source)
XLA Modules:
  0.0 370.5 jit_solution(13805238136021071768)
XLA Ops:
  9.0 5.0 %collective-permute-start = (bf16[1,1,3,48,256]{4,3,2,1,0:T(8,128)(2,1)S(1)}, bf16[1,1,3,48,256]{4,3,2,1,0:T(8,128)(2,1)S(1)}, u32[]{:S(2)}, u32[]{:S(2)}) collective-permute-start(bf16[1,1,3,48,256]{4,3,2,1,0:T(8,128)(2,1)S(1)} %get-tuple-element.375), channel_id=1, source_target_pairs={{0,24},{1,25},{2,26},{3,27},{4,28},{5,29},{6,30},{7,31},{8,0},{9,1... | collective-permute-start | bytes 221192 | tf_op jit(solution)/shard_map/ppermute | solution.py:570
  17.8 7.7 %shard_map.482.t_ref = f32[12,128,2048]{2,1,0:T(8,128)} custom-call(f32[12,1,2048]{2,1,0:T(1,128)} %add.489.off_ref), custom_call_target="tpu_custom_call" | custom-call | bytes 24000000 | tf_op jit(solution)/shard_map/pallas_call | solution.py:60
  28.5 2.9 collective-permute-start.4
  46.4 2.1 collective-permute-start.10
  58.1 16.0 %shard_map.483 = (bf16[4,1024,1024]{2,1,0:T(8,128)(2,1)}, bf16[1024,768]{1,0:T(8,128)(2,1)}, f32[1024,768]{1,0:T(8,128)}, f32[1024,768]{1,0:T(8,128)}, bf16[3,10...) custom-call(s32[1]{0:T(128)S(6)} %copy.295.len_ref, s32[4]{0:T(128)} %pad_add_fusion.at_ref, ...), custom_call_target="tpu_custom_call" | custom-call | bytes 44400000 | tf_op jit(solution)/shard_map/pallas_call | solution.py:176
  79.2 16.0 %shard_map.484 = (bf16[4,1024,1024]{2,1,0:T(8,128)(2,1)}, bf16[1024,768]{1,0:T(8,128)(2,1)}, f32[1024,768]{1,0:T(8,128)}, f32[1024,768]{1,0:T(8,128)}, bf16[3,10...) custom-call(s32[1]{0:T(128)S(6)} %copy.295.len_ref, ...), custom_call_target="tpu_custom_call", output_to_operand_aliasing={{1}: (8, {}), {2}: (9, {}), {3}: (10, {})} | custom-call | bytes 44400000 | tf_op jit(solution)/shard_map/pallas_call | solution.py:176
  95.2 4.5 %collective-permute-done.12 = bf16[1,4,6,48,256]{4,3,2,1,0:T(8,128)(2,1)} collective-permute-done((bf16[1,4,6,48,256]{4,3,2,1,0:T(8,128)(2,1)S(1)}, bf16[1,4,6,48,256]{4,3,2,1,0:T(8,128)(2,1)}, u32[]{:S(2)}, u32[]{:S(2)}) %collective-permute-start.12) | collective-permute-done | bytes 589856 | tf_op jit(solution)/shard_map/ppermute | solution.py:570
  104.1 3.3 shard_map.486.wa_ref
  107.5 16.1 %shard_map.485 = (bf16[4,1024,1024]{2,1,0:T(8,128)(2,1)}, bf16[1024,768]{1,0:T(8,128)(2,1)}, f32[1024,768]{1,0:T(8,128)}, f32[1024,768]{1,0:T(8,128)}, bf16[3,10...) custom-call(s32[1]{0:T(128)S(6)} %copy.295.len_ref, ...), custom_call_target="tpu_custom_call", output_to_operand_aliasing={{1}: (8, {}), {2}: (9, {}), {3}: (10, {})} | custom-call | bytes 44400000 | tf_op jit(solution)/shard_map/pallas_call | solution.py:176
  125.1 39.3 %shard_map.487 = (bf16[1024,768]{1,0:T(8,128)(2,1)}, bf16[1024,3072]{1,0:T(8,128)(2,1)}, bf16[1024,3072]{1,0:T(8,128)(2,1)}, bf16[1024,768]{1,0:T(8,128)(2,1)}, ...) custom-call(s32[1]{0:T(128)S(6)} %copy.295.len_ref, ...), custom_call_target="tpu_custom_call" | custom-call | bytes 120000000 | tf_op jit(solution)/shard_map/pallas_call | solution.py:470
  164.4 15.0 %shard_map.488 = bf16[32,192,768]{2,1,0:T(8,128)(2,1)} custom-call(bf16[1024,3072]{1,0:T(8,128)(2,1)} %get-tuple-element.174.dh_ref, bf16[1024,3072]{1,0:T(8,128)(2,1)} %get-tuple-element.175.act_ref, bf16[1024,768]{1,0:T(8,128)(2,1)} %get-tuple-element.176.low_ref, bf16[1024,768]{1,0:T(8,128)(2,1)} %get-tuple-element.177.dlow_ref), custom_call_target="tpu_custom_call" | custom-call | bytes 48000000 | tf_op jit(solution)/shard_map/pallas_call | solution.py:329
  179.4 14.3 %shard_map.489 = (bf16[3,1024,256]{2,1,0:T(8,128)(2,1)}, f32[4,1,1024]{2,1,0:T(1,128)}, f32[4,1,2048]{2,1,0:T(1,128)}) custom-call(bf16[3,1024,256]{2,1,0:T(8,128)(2,1)} %get-tuple-element.173.q_ref.k_ref.v_ref, bf16[3,1024,256]{2,1,0:T(8,128)(2,1)} %get-tuple-element.173.q_ref.k_ref.v_ref, bf16[3,1024,256]{2,1,0:T(8,128)(2,1)} %get-tuple-element.173.q_ref.k_ref.v_ref, ...), custom_call_target="tpu_custom_call" | custom-call | bytes 36000000 | tf_op jit(solution)/shard_map/pallas_call | solution.py:258
  193.7 7.3 %shard_map.490 = bf16[768,1536]{1,0:T(8,128)(2,1)} custom-call(bf16[768,1024]{1,0:T(8,128)(2,1)} %fusion.92.xt_ref, bf16[3,1024,256]{2,1,0:T(8,128)(2,1)} %get-tuple-element.213.d_ref.d0_ref, bf16[1024,768]{1,0:T(8,128)(2,1)} %get-tuple-element.168.c_ref.a_ref, bf16[1024,768]{1,0:T(8,128)(2,1)} %get-tuple-element.183.b_ref), custom_call_target="tpu_custom_call" | custom-call | bytes 15000000 | tf_op jit(solution)/shard_map/pallas_call | solution.py:304
  201.0 2.4 dynamic-slice_bitcast_fusion.1
  203.4 14.4 %shard_map.491 = (bf16[3,1024,256]{2,1,0:T(8,128)(2,1)}, f32[4,1,1024]{2,1,0:T(1,128)}, f32[4,1,2048]{2,1,0:T(1,128)}) custom-call(bf16[3,1024,256]{2,1,0:T(8,128)(2,1)} %get-tuple-element.187.q_ref.k_ref.v_ref, bf16[3,1024,256]{2,1,0:T(8,128)(2,1)} %get-tuple-element.187.q_ref.k_ref.v_ref, bf16[3,1024,256]{2,1,0:T(8,128)(2,1)} %get-tuple-element.187.q_ref.k_ref.v_ref, ...), custom_call_target="tpu_custom_call" | custom-call | bytes 36000000 | tf_op jit(solution)/shard_map/pallas_call | solution.py:258
  217.9 2.4 fusion.5
  220.7 14.1 %shard_map.492 = (bf16[3,1024,256]{2,1,0:T(8,128)(2,1)}, f32[4,1,1024]{2,1,0:T(1,128)}, f32[4,1,2048]{2,1,0:T(1,128)}) custom-call(bf16[3,1024,256]{2,1,0:T(8,128)(2,1)} %get-tuple-element.195.q_ref.k_ref.v_ref, bf16[3,1024,256]{2,1,0:T(8,128)(2,1)} %get-tuple-element.195.q_ref.k_ref.v_ref, bf16[3,1024,256]{2,1,0:T(8,128)(2,1)} %get-tuple-element.195.q_ref.k_ref.v_ref, ...), custom_call_target="tpu_custom_call" | custom-call | bytes 36000000 | tf_op jit(solution)/shard_map/pallas_call | solution.py:258
  242.3 6.5 %shard_map.493 = bf16[768,1536]{1,0:T(8,128)(2,1)} custom-call(bf16[768,1024]{1,0:T(8,128)(2,1)} %fusion.92.xt_ref, bf16[3,1024,256]{2,1,0:T(8,128)(2,1)} %get-tuple-element.193.d_ref.d1_ref, bf16[3,1024,256]{2,1,0:T(8,128)(2,1)} %get-tuple-element.201.a_ref.d2_ref, f32[8,128]{1,0:T(8,128)} %broadcast_in_dim.67.b_ref), custom_call_target="tpu_custom_call" | custom-call | bytes 15000000 | tf_op jit(solution)/shard_map/pallas_call | solution.py:304
  248.8 2.5 dynamic-slice_bitcast_fusion
  260.3 2.0 fusion.4
  264.3 2.1 fusion.23
  267.9 2.4 collective-permute-start.20
  272.5 9.3 %shard_map.494 = (f32[1024,768]{1,0:T(8,128)}, f32[8,768]{1,0:T(8,128)}) custom-call(f32[1024,768]{1,0:T(8,128)} %get-tuple-element.212.dr_ref, bf16[3,1024,256]{2,1,0:T(8,128)(2,1)} %get-tuple-element.213.d_ref.d0_ref, bf16[3,1024,256]{2,1,0:T(8,128)(2,1)} %get-tuple-element.193.d_ref.d1_ref, bf16[3,1024,256]{2,1,0:T(8,128)(2,1)} %get-tuple-element.201.a_ref.d2_ref, ...), custom_call_target="tpu_custom_call" | custom-call | bytes 24000000 | tf_op jit(solution)/shard_map/pallas_call | solution.py:518
  296.6 7.5 %collective-permute-start.22 = (bf16[48,1536]{1,0:T(8,128)(2,1)S(1)}, bf16[48,1536]{1,0:T(8,128)(2,1)S(1)}, u32[]{:S(2)}, u32[]{:S(2)}) collective-permute-start(bf16[48,1536]{1,0:T(8,128)(2,1)S(1)} %get-tuple-element.362), channel_id=1, source_target_pairs={{0,8},{1,9},{2,10},{3,11},{4,12},{5,13},{6,14},{7,15},{8,16},{9,17... | collective-permute-start | bytes 442376 | tf_op jit(solution)/shard_map/ppermute | solution.py:570
  306.6 2.0 collective-permute-done.22
  308.6 5.3 %collective-permute-done.23 = bf16[48,1536]{1,0:T(8,128)(2,1)S(1)} collective-permute-done((bf16[48,1536]{1,0:T(8,128)(2,1)S(1)}, bf16[48,1536]{1,0:T(8,128)(2,1)S(1)}, u32[]{:S(2)}, u32[]{:S(2)}) %collective-permute-start.23) | collective-permute-done | bytes 147488 | tf_op jit(solution)/shard_map/ppermute | solution.py:570
  321.0 2.3 collective-permute-done.26
  324.7 3.9 %collective-permute-done.27 = bf16[192,768]{1,0:T(8,128)(2,1)S(1)} collective-permute-done((bf16[192,768]{1,0:T(8,128)(2,1)S(1)}, bf16[192,768]{1,0:T(8,128)(2,1)S(1)}, u32[]{:S(2)}, u32[]{:S(2)}) %collective-permute-start.27) | collective-permute-done | bytes 294944 | tf_op jit(solution)/shard_map/ppermute | solution.py:570
  331.9 3.8 %collective-permute-done.29 = f32[120,128]{1,0:T(8,128)S(1)} collective-permute-done((f32[120,128]{1,0:T(8,128)S(1)}, f32[120,128]{1,0:T(8,128)S(1)}, u32[]{:S(2)}, u32[]{:S(2)}) %collective-permute-start.29) | collective-permute-done | bytes 61472 | tf_op jit(solution)/shard_map/ppermute | solution.py:570
  337.2 2.8 collective-permute-done.30
  340.0 3.1 collective-permute-start.31
  347.4 3.2 collective-permute-done.32
  (315 shorter events, 107.4 us)
Async XLA Ops:
  7.2 116.3 %all-gather.3.cloned.1.call-start = ((), (), s32[]{:S(2)}) async-start(), calls=%async_computation.2 | async-start | bytes 10137600 | tf_op jit(solution)/shard_map/all_gather | solution.py:659
  9.0 17.5 %collective-permute-start = (bf16[1,1,3,48,256]{4,3,2,1,0:T(8,128)(2,1)S(1)}, bf16[1,1,3,48,256]{4,3,2,1,0:T(8,128)(2,1)S(1)}, u32[]{:S(2)}, u32[]{:S(2)}) collective-permute-start(bf16[1,1,3,48,256]{4,3,2,1,0:T(8,128)(2,1)S(1)} %get-tuple-element.375), channel_id=1, source_target_pairs={{0,24},{1,25},{2,26},{3,27},{4,28},{5,29},{6,30},{7,31},{8,0},{9,1... | collective-permute-start | bytes 221192 | tf_op jit(solution)/shard_map/ppermute | solution.py:570
  14.0 12.4 %collective-permute-start.1 = (bf16[1,1,3,48,256]{4,3,2,1,0:T(8,128)(2,1)S(1)}, bf16[1,1,3,48,256]{4,3,2,1,0:T(8,128)(2,1)S(1)}, u32[]{:S(2)}, u32[]{:S(2)}) collective-permute-start(bf16[1,1,3,48,256]{4,3,2,1,0:T(8,128)(2,1)S(1)} %get-tuple-element.375), channel_id=1, source_target_pairs={{0,16},{1,17},{2,18},{3,19},{4,20},{5,21},{6,22},{7,23},{8,24},{9,... | collective-permute-start | bytes 221192 | tf_op jit(solution)/shard_map/ppermute | solution.py:570
  14.0 12.4 %collective-permute-start.2 = (bf16[1,1,3,48,256]{4,3,2,1,0:T(8,128)(2,1)S(1)}, bf16[1,1,3,48,256]{4,3,2,1,0:T(8,128)(2,1)S(1)}, u32[]{:S(2)}, u32[]{:S(2)}) collective-permute-start(bf16[1,1,3,48,256]{4,3,2,1,0:T(8,128)(2,1)S(1)} %get-tuple-element.375), channel_id=1, source_target_pairs={{0,8},{1,9},{2,10},{3,11},{4,12},{5,13},{6,14},{7,15},{8,16},{9,17... | collective-permute-start | bytes 221192 | tf_op jit(solution)/shard_map/ppermute | solution.py:570
  27.2 288.0 %reduce-scatter.2.cloned.1.call-start = ((), (), s32[]{:S(2)}) async-start(), calls=%async_computation.1 | async-start | bytes 10027008 | tf_op jit(solution)/shard_map/reduce_scatter | solution.py:724
  28.5 11.7 %collective-permute-start.4 = (bf16[1,1,3,48,256]{4,3,2,1,0:T(8,128)(2,1)S(1)}, bf16[1,1,3,48,256]{4,3,2,1,0:T(8,128)(2,1)}, u32[]{:S(2)}, u32[]{:S(2)}) collective-permute-start(bf16[1,1,3,48,256]{4,3,2,1,0:T(8,128)(2,1)S(1)} %get-tuple-element.134), channel_id=1, source_target_pairs={{0,24},{1,25},{2,26},{3,27},{4,28},{5,29},{6,30},{7,31},{8,0},{9,1... | collective-permute-start | bytes 221192 | tf_op jit(solution)/shard_map/ppermute | solution.py:570
  31.4 8.9 %collective-permute-start.5 = (bf16[1,1,3,48,256]{4,3,2,1,0:T(8,128)(2,1)S(1)}, bf16[1,1,3,48,256]{4,3,2,1,0:T(8,128)(2,1)}, u32[]{:S(2)}, u32[]{:S(2)}) collective-permute-start(bf16[1,1,3,48,256]{4,3,2,1,0:T(8,128)(2,1)S(1)} %get-tuple-element.134), channel_id=1, source_target_pairs={{0,16},{1,17},{2,18},{3,19},{4,20},{5,21},{6,22},{7,23},{8,24},{9,... | collective-permute-start | bytes 221192 | tf_op jit(solution)/shard_map/ppermute | solution.py:570
  32.5 7.8 %collective-permute-start.6 = (bf16[1,1,3,48,256]{4,3,2,1,0:T(8,128)(2,1)S(1)}, bf16[1,1,3,48,256]{4,3,2,1,0:T(8,128)(2,1)}, u32[]{:S(2)}, u32[]{:S(2)}) collective-permute-start(bf16[1,1,3,48,256]{4,3,2,1,0:T(8,128)(2,1)S(1)} %get-tuple-element.134), channel_id=1, source_target_pairs={{0,8},{1,9},{2,10},{3,11},{4,12},{5,13},{6,14},{7,15},{8,16},{9,17... | collective-permute-start | bytes 221192 | tf_op jit(solution)/shard_map/ppermute | solution.py:570
  33.5 9.8 %collective-permute-start.3 = (bf16[1,4,3,48,256]{4,3,2,1,0:T(8,128)(2,1)}, bf16[1,4,3,48,256]{4,3,2,1,0:T(8,128)(2,1)S(1)}, u32[]{:S(2)}, u32[]{:S(2)}) collective-permute-start(bf16[1,4,3,48,256]{4,3,2,1,0:T(8,128)(2,1)} %pad_maximum_fusion.4), channel_id=1, source_target_pairs={{0,4},{1,5},{2,6},{3,7},{4,0},{5,1},{6,2},{7,3},{8,12},{9,13},{10,... | collective-permute-start | bytes 884744 | tf_op jit(solution)/shard_map/ppermute | solution.py:570
  46.4 27.8 %collective-permute-start.10 = (bf16[1,1,6,48,256]{4,3,2,1,0:T(8,128)(2,1)S(1)}, bf16[1,1,6,48,256]{4,3,2,1,0:T(8,128)(2,1)}, u32[]{:S(2)}, u32[]{:S(2)}) collective-permute-start(bf16[1,1,6,48,256]{4,3,2,1,0:T(8,128)(2,1)S(1)} %pad_maximum_fusion.6), channel_id=1, source_target_pairs={{0,16},{1,17},{2,18},{3,19},{4,20},{5,21},{6,22},{7,23},{8,24},{9,... | collective-permute-start | bytes 442376 | tf_op jit(solution)/shard_map/ppermute | solution.py:570
  48.5 25.7 %collective-permute-start.11 = (bf16[1,1,6,48,256]{4,3,2,1,0:T(8,128)(2,1)S(1)}, bf16[1,1,6,48,256]{4,3,2,1,0:T(8,128)(2,1)}, u32[]{:S(2)}, u32[]{:S(2)}) collective-permute-start(bf16[1,1,6,48,256]{4,3,2,1,0:T(8,128)(2,1)S(1)} %pad_maximum_fusion.6), channel_id=1, source_target_pairs={{0,8},{1,9},{2,10},{3,11},{4,12},{5,13},{6,14},{7,15},{8,16},{9,17... | collective-permute-start | bytes 442376 | tf_op jit(solution)/shard_map/ppermute | solution.py:570
  50.5 23.7 %collective-permute-start.9 = (bf16[1,1,6,48,256]{4,3,2,1,0:T(8,128)(2,1)S(1)}, bf16[1,1,6,48,256]{4,3,2,1,0:T(8,128)(2,1)}, u32[]{:S(2)}, u32[]{:S(2)}) collective-permute-start(bf16[1,1,6,48,256]{4,3,2,1,0:T(8,128)(2,1)S(1)} %pad_maximum_fusion.6), channel_id=1, source_target_pairs={{0,24},{1,25},{2,26},{3,27},{4,28},{5,29},{6,30},{7,31},{8,0},{9,1... | collective-permute-start | bytes 442376 | tf_op jit(solution)/shard_map/ppermute | solution.py:570
  52.4 22.9 %collective-permute-start.8 = (bf16[1,4,3,48,256]{4,3,2,1,0:T(8,128)(2,1)S(1)}, bf16[1,4,3,48,256]{4,3,2,1,0:T(8,128)(2,1)}, u32[]{:S(2)}, u32[]{:S(2)}) collective-permute-start(bf16[1,4,3,48,256]{4,3,2,1,0:T(8,128)(2,1)S(1)} %pad_maximum_fusion.5), channel_id=1, source_target_pairs={{0,4},{1,5},{2,6},{3,7},{4,0},{5,1},{6,2},{7,3},{8,12},{9,13},{10,... | collective-permute-start | bytes 884744 | tf_op jit(solution)/shard_map/ppermute | solution.py:570
  76.4 23.3 %collective-permute-start.12 = (bf16[1,4,6,48,256]{4,3,2,1,0:T(8,128)(2,1)S(1)}, bf16[1,4,6,48,256]{4,3,2,1,0:T(8,128)(2,1)}, u32[]{:S(2)}, u32[]{:S(2)}) collective-permute-start(bf16[1,4,6,48,256]{4,3,2,1,0:T(8,128)(2,1)S(1)} %pad_maximum_fusion.3), channel_id=1, source_target_pairs={{0,4},{1,5},{2,6},{3,7},{4,0},{5,1},{6,2},{7,3},{8,12},{9,13},{10,... | collective-permute-start | bytes 1769480 | tf_op jit(solution)/shard_map/ppermute | solution.py:570
  100.9 3.2 collective-permute-start.14
  203.4 14.5 %collective-permute-start.15 = (bf16[4,2,48,1536]{3,2,1,0:T(8,128)(2,1)}, bf16[4,2,48,1536]{3,2,1,0:T(8,128)(2,1)S(1)}, u32[]{:S(2)}, u32[]{:S(2)}) collective-permute-start(bf16[4,2,48,1536]{3,2,1,0:T(8,128)(2,1)} %dynamic-slice_bitcast_fusion.1), channel_id=1, source_target_pairs={{0,2},{1,3},{2,0},{3,1},{4,6},{5,7},{6,4},{7,5},{8,10},{9,11},{10,... | collective-permute-start | bytes 3538952 | tf_op jit(solution)/shard_map/ppermute | solution.py:570
  220.3 16.2 %collective-permute-start.16 = (bf16[4,48,1536]{2,1,0:T(8,128)(2,1)}, bf16[4,48,1536]{2,1,0:T(8,128)(2,1)S(1)}, u32[]{:S(2)}, u32[]{:S(2)}) collective-permute-start(bf16[4,48,1536]{2,1,0:T(8,128)(2,1)} %fusion.5), channel_id=1, source_target_pairs={{0,4},{1,5},{2,6},{3,7},{4,0},{5,1},{6,2},{7,3},{8,12},{9,13},{10,... | collective-permute-start | bytes 1769480 | tf_op jit(solution)/shard_map/ppermute | solution.py:570
  251.3 8.4 %collective-permute-start.17 = (bf16[4,2,48,1536]{3,2,1,0:T(8,128)(2,1)}, bf16[4,2,48,1536]{3,2,1,0:T(8,128)(2,1)}, u32[]{:S(2)}, u32[]{:S(2)}) collective-permute-start(bf16[4,2,48,1536]{3,2,1,0:T(8,128)(2,1)} %dynamic-slice_bitcast_fusion), channel_id=1, source_target_pairs={{0,2},{1,3},{2,0},{3,1},{4,6},{5,7},{6,4},{7,5},{8,10},{9,11},{10,... | collective-permute-start | bytes 3538952 | tf_op jit(solution)/shard_map/ppermute | solution.py:570
  262.4 29.9 %collective-permute-start.18 = (bf16[4,48,1536]{2,1,0:T(8,128)(2,1)}, bf16[4,48,1536]{2,1,0:T(8,128)(2,1)}, u32[]{:S(2)}, u32[]{:S(2)}) collective-permute-start(bf16[4,48,1536]{2,1,0:T(8,128)(2,1)} %fusion.4), channel_id=1, source_target_pairs={{0,4},{1,5},{2,6},{3,7},{4,0},{5,1},{6,2},{7,3},{8,12},{9,13},{10,... | collective-permute-start | bytes 1769480 | tf_op jit(solution)/shard_map/ppermute | solution.py:570
  266.4 25.9 %collective-permute-start.19 = (bf16[48,1536]{1,0:T(8,128)(2,1)}, bf16[48,1536]{1,0:T(8,128)(2,1)}, u32[]{:S(2)}, u32[]{:S(2)}) collective-permute-start(bf16[48,1536]{1,0:T(8,128)(2,1)} %get-tuple-element.365), channel_id=1, source_target_pairs={{0,8},{1,9},{2,10},{3,11},{4,12},{5,13},{6,14},{7,15},{8,16},{9,17... | collective-permute-start | bytes 442376 | tf_op jit(solution)/shard_map/ppermute | solution.py:570
  267.9 24.4 %collective-permute-start.20 = (bf16[48,1536]{1,0:T(8,128)(2,1)}, bf16[48,1536]{1,0:T(8,128)(2,1)}, u32[]{:S(2)}, u32[]{:S(2)}) collective-permute-start(bf16[48,1536]{1,0:T(8,128)(2,1)} %get-tuple-element.364), channel_id=1, source_target_pairs={{0,16},{1,17},{2,18},{3,19},{4,20},{5,21},{6,22},{7,23},{8,24},{9,... | collective-permute-start | bytes 442376 | tf_op jit(solution)/shard_map/ppermute | solution.py:570
  270.3 22.0 %collective-permute-start.21 = (bf16[48,1536]{1,0:T(8,128)(2,1)}, bf16[48,1536]{1,0:T(8,128)(2,1)}, u32[]{:S(2)}, u32[]{:S(2)}) collective-permute-start(bf16[48,1536]{1,0:T(8,128)(2,1)} %get-tuple-element.363), channel_id=1, source_target_pairs={{0,24},{1,25},{2,26},{3,27},{4,28},{5,29},{6,30},{7,31},{8,0},{9,1... | collective-permute-start | bytes 442376 | tf_op jit(solution)/shard_map/ppermute | solution.py:570
  293.6 12.9 %collective-permute-start.25 = (bf16[48,1536]{1,0:T(8,128)(2,1)S(1)}, bf16[48,1536]{1,0:T(8,128)(2,1)S(1)}, u32[]{:S(2)}, u32[]{:S(2)}) collective-permute-start(bf16[48,1536]{1,0:T(8,128)(2,1)S(1)} %fusion.15), channel_id=1, source_target_pairs={{0,1},{1,0},{2,3},{3,2},{4,5},{5,4},{6,7},{7,6},{8,9},{9,8},{10,11... | collective-permute-start | bytes 442376 | tf_op jit(solution)/shard_map/ppermute | solution.py:570
  296.6 12.0 %collective-permute-start.22 = (bf16[48,1536]{1,0:T(8,128)(2,1)S(1)}, bf16[48,1536]{1,0:T(8,128)(2,1)S(1)}, u32[]{:S(2)}, u32[]{:S(2)}) collective-permute-start(bf16[48,1536]{1,0:T(8,128)(2,1)S(1)} %get-tuple-element.362), channel_id=1, source_target_pairs={{0,8},{1,9},{2,10},{3,11},{4,12},{5,13},{6,14},{7,15},{8,16},{9,17... | collective-permute-start | bytes 442376 | tf_op jit(solution)/shard_map/ppermute | solution.py:570
  304.1 9.8 %collective-permute-start.23 = (bf16[48,1536]{1,0:T(8,128)(2,1)S(1)}, bf16[48,1536]{1,0:T(8,128)(2,1)S(1)}, u32[]{:S(2)}, u32[]{:S(2)}) collective-permute-start(bf16[48,1536]{1,0:T(8,128)(2,1)S(1)} %get-tuple-element.361), channel_id=1, source_target_pairs={{0,16},{1,17},{2,18},{3,19},{4,20},{5,21},{6,22},{7,23},{8,24},{9,... | collective-permute-start | bytes 442376 | tf_op jit(solution)/shard_map/ppermute | solution.py:570
  304.8 9.1 %collective-permute-start.24 = (bf16[48,1536]{1,0:T(8,128)(2,1)S(1)}, bf16[48,1536]{1,0:T(8,128)(2,1)S(1)}, u32[]{:S(2)}, u32[]{:S(2)}) collective-permute-start(bf16[48,1536]{1,0:T(8,128)(2,1)S(1)} %get-tuple-element.360), channel_id=1, source_target_pairs={{0,24},{1,25},{2,26},{3,27},{4,28},{5,29},{6,30},{7,31},{8,0},{9,1... | collective-permute-start | bytes 442376 | tf_op jit(solution)/shard_map/ppermute | solution.py:570
  316.6 6.8 %collective-permute-start.26 = (bf16[48,1536]{1,0:T(8,128)(2,1)S(1)}, bf16[48,1536]{1,0:T(8,128)(2,1)S(1)}, u32[]{:S(2)}, u32[]{:S(2)}) collective-permute-start(bf16[48,1536]{1,0:T(8,128)(2,1)S(1)} %fusion.22), channel_id=1, source_target_pairs={{0,1},{1,0},{2,3},{3,2},{4,5},{5,4},{6,7},{7,6},{8,9},{9,8},{10,11... | collective-permute-start | bytes 442376 | tf_op jit(solution)/shard_map/ppermute | solution.py:570
  318.0 10.6 %collective-permute-start.27 = (bf16[192,768]{1,0:T(8,128)(2,1)S(1)}, bf16[192,768]{1,0:T(8,128)(2,1)S(1)}, u32[]{:S(2)}, u32[]{:S(2)}) collective-permute-start(bf16[192,768]{1,0:T(8,128)(2,1)S(1)} %dynamic-slice_bitcast_fusion.2), channel_id=1, source_target_pairs={{0,1},{1,0},{2,3},{3,2},{4,5},{5,4},{6,7},{7,6},{8,9},{9,8},{10,11... | collective-permute-start | bytes 884744 | tf_op jit(solution)/shard_map/ppermute | solution.py:570
  331.4 4.3 %collective-permute-start.29 = (f32[120,128]{1,0:T(8,128)S(1)}, f32[120,128]{1,0:T(8,128)S(1)}, u32[]{:S(2)}, u32[]{:S(2)}) collective-permute-start(f32[120,128]{1,0:T(8,128)S(1)} %bitcast_add_fusion), channel_id=1, source_target_pairs={{0,1},{1,0},{2,3},{3,2},{4,5},{5,4},{6,7},{7,6},{8,9},{9,8},{10,11... | collective-permute-start | bytes 184328 | tf_op jit(solution)/shard_map/ppermute | solution.py:570
  335.7 4.3 %collective-permute-start.30 = (f32[120,128]{1,0:T(8,128)S(1)}, f32[120,128]{1,0:T(8,128)S(1)}, u32[]{:S(2)}, u32[]{:S(2)}) collective-permute-start(f32[120,128]{1,0:T(8,128)S(1)} %fusion.91), channel_id=1, source_target_pairs={{0,4},{1,5},{2,6},{3,7},{4,0},{5,1},{6,2},{7,3},{8,12},{9,13},{10,... | collective-permute-start | bytes 184328 | tf_op jit(solution)/shard_map/ppermute | solution.py:570
  340.0 5.4 %collective-permute-start.31 = (f32[120,128]{1,0:T(8,128)S(1)}, f32[120,128]{1,0:T(8,128)S(1)}, u32[]{:S(2)}, u32[]{:S(2)}) collective-permute-start(f32[120,128]{1,0:T(8,128)S(1)} %add.556), channel_id=1, source_target_pairs={{0,8},{1,9},{2,10},{3,11},{4,12},{5,13},{6,14},{7,15},{8,0},{9,1},... | collective-permute-start | bytes 184328 | tf_op jit(solution)/shard_map/ppermute | solution.py:570
  345.4 5.2 %collective-permute-start.32 = (f32[120,128]{1,0:T(8,128)S(1)}, f32[120,128]{1,0:T(8,128)S(1)}, u32[]{:S(2)}, u32[]{:S(2)}) collective-permute-start(f32[120,128]{1,0:T(8,128)S(1)} %add.557), channel_id=1, source_target_pairs={{0,16},{1,17},{2,18},{3,19},{4,20},{5,21},{6,22},{7,23},{8,24},{9,... | collective-permute-start | bytes 184328 | tf_op jit(solution)/shard_map/ppermute | solution.py:570
  (63 other events, 327.4 us)
Sparse Core Ops, SparseCore 0:
  27.3 94.4 all-gather.2
  179.5 122.1 reduce-scatter.1

commit v4 on v3

--- a/solution.py
+++ b/solution.py
@@ -66,37 +66,6 @@
         compiler_params=pltpu.CompilerParams(vmem_limit_bytes=VMEM),
         cost_estimate=cost(8),
     )(offr.reshape(n, 1, w))
-
-
-def assemble_kernel(at_ref, mine_ref, peer_ref, out_ref, sem, *, zs, rows, cols):
-    z0, y0, c0 = at_ref[0], at_ref[1], at_ref[2]
-    copies = []
-    for c, src in enumerate((mine_ref, peer_ref)):
-        for y in range(2):
-            for z in range(zs):
-                block = (lax.rem(z0 + z, zs) * 2 + lax.rem(y0 + y, 2)) * 2 + lax.rem(c0 + c, 2)
-                first = pl.multiple_of(block * rows, rows)
-                for k in range(3):
-                    there = out_ref.at[pl.ds(first, rows), pl.ds(k * cols, cols)]
-                    copies.append(pltpu.make_async_copy(src.at[y, z, 3 + k], there, sem.at[len(copies)]))
-    for copy in copies:
-        copy.start()
-    for copy in copies:
-        copy.wait()
-
-
-def assemble(at, mine, peer):
-    _, zs, _, rows, cols = mine.shape
-    hbm = pl.BlockSpec(memory_space=pl.ANY)
-    return pl.pallas_call(
-        functools.partial(assemble_kernel, zs=zs, rows=rows, cols=cols),
-        in_specs=[pl.BlockSpec(memory_space=pltpu.SMEM), hbm, hbm],
-        out_specs=pl.BlockSpec(memory_space=pltpu.VMEM),
-        scratch_shapes=[pltpu.SemaphoreType.DMA((12 * zs,))],
-        out_shape=jax.ShapeDtypeStruct((D, D), jnp.bfloat16),
-        compiler_params=pltpu.CompilerParams(vmem_limit_bytes=VMEM),
-        cost_estimate=cost(2),
-    )(at, mine, peer)
 
 
 def fwd_kernel(len_ref, at_ref, x_ref, mine_ref, peer_ref, bias_ref, t_ref, g_ref, *rest, seq, ib, zs, rows, kept):
@@ -218,6 +187,8 @@
     q = q_ref[0]
     base = seq - 128
     a_ref[...] = jnp.zeros_like(a_ref)
+    dv = dot(p_ref[0], dc)
+    d_ref[2] = jnp.where(inh, dv.astype(jnp.bfloat16), d_ref[2])
     for i0 in range(0, seq, ib):
         gate = g_ref[0, :, i0 : i0 + ib]
         dcb = dca[i0 : i0 + ib]
@@ -233,8 +204,6 @@
         d_ref[0, i0 : i0 + ib, :] = jnp.where(inh[i0 : i0 + ib], dqt.astype(jnp.bfloat16), d_ref[0, i0 : i0 + ib, :])
     dk = dot(ds_ref[...], q)
     d_ref[1] = jnp.where(inh, dk.astype(jnp.bfloat16), d_ref[1])
-    dv = dot(p_ref[0], dc)
-    d_ref[2] = jnp.where(inh, dv.astype(jnp.bfloat16), d_ref[2])
     a = a_ref[...]
     w = a.shape[1]
     r = 64
@@ -400,16 +369,36 @@
     ]
 
 
-def middle_kernel(len_ref, c_ref, wa_ref, x_ref, mask_ref, w_ref, b_ref, cot_ref, rl_ref, small_ref,
+def middle_kernel(len_ref, at_ref, c_ref, mine_ref, peer_ref, x_ref, mask_ref, w_ref, b_ref, cot_ref, rl_ref, small_ref,
                   low_ref, act_ref, dh_ref, dlow_ref, out_ref, dr1_ref, da_ref, dc_ref, gb_ref, red_ref,
-                  wi_ref, wo_ref, slope_ref, sem, *, block):
+                  wi_ref, wo_ref, slope_ref, sem, wa_ref, wa_sem, *, block):
     i = pl.program_id(0)
     f32, b16 = jnp.float32, jnp.bfloat16
 
+    _, zs, _, rows, cols = mine_ref.shape
+
+    def projection_copies():
+        z0, y0, c0 = at_ref[0], at_ref[1], at_ref[2]
+        copies = []
+        for c, src in enumerate((mine_ref, peer_ref)):
+            for y in range(2):
+                for z in range(zs):
+                    owner = (lax.rem(z0 + z, zs) * 2 + lax.rem(y0 + y, 2)) * 2 + lax.rem(c0 + c, 2)
+                    first = pl.multiple_of(owner * rows, rows)
+                    for k in range(3):
+                        there = wa_ref.at[pl.ds(first, rows), pl.ds(k * cols, cols)]
+                        copies.append(pltpu.make_async_copy(src.at[y, z, 3 + k], there, wa_sem.at[len(copies)]))
+        return copies
+
     @pl.when(i == 0)
     def _():
+        copies = projection_copies()
+        for copy in copies:
+            copy.start()
         red_ref[...] = jnp.zeros_like(red_ref)
         gb_ref[...] = jnp.zeros_like(gb_ref)
+        for copy in copies:
+            copy.wait()
 
     def body(per, chunks, wait):
         def weights(ref, c):
@@ -457,11 +446,13 @@
     by_step(w_ref, wi_ref, wo_ref, sem, body)
 
 
-def middle(length, ctx, w_attn, rounded, mask, w_all, bias, cot, rl, small, block=256):
+def middle(length, at, ctx, mine, peer, rounded, mask, w_all, bias, cot, rl, small, block=256):
     seq = ctx.shape[0]
-    wide = pl.BlockSpec((block, D), lambda i, n: (i, 0))
-    hidden = pl.BlockSpec((block, FF), lambda i, n: (i, 0))
-    one = pl.BlockSpec((1, FF), lambda i, n: (0, 0))
+    wide = pl.BlockSpec((block, D), lambda i, n, a: (i, 0))
+    hidden = pl.BlockSpec((block, FF), lambda i, n, a: (i, 0))
+    one = pl.BlockSpec((1, FF), lambda i, n, a: (0, 0))
+    hbm = pl.BlockSpec(memory_space=pl.ANY)
+    zs = mine.shape[1]
     f32, b16 = jnp.float32, jnp.bfloat16
 
     def shape(cols, kind, rows=seq):
@@ -470,18 +461,19 @@
     return pl.pallas_call(
         functools.partial(middle_kernel, block=block),
         grid_spec=pltpu.PrefetchScalarGridSpec(
-            num_scalar_prefetch=1,
+            num_scalar_prefetch=2,
             grid=(seq // block,),
-            in_specs=[wide, pl.BlockSpec((D, D), lambda i, n: (0, 0)), wide, pl.BlockSpec((block, 1), lambda i, n: (i, 0)),
-                      pl.BlockSpec(memory_space=pl.ANY), one, wide, wide, pl.BlockSpec((9, D), lambda i, n: (0, 0))],
-            out_specs=[wide, hidden, hidden, wide, wide, wide, wide, wide, one, pl.BlockSpec((8, D), lambda i, n: (0, 0))],
-            scratch_shapes=ffn_scratch(w_all, block),
+            in_specs=[wide, hbm, hbm, wide, pl.BlockSpec((block, 1), lambda i, n, a: (i, 0)),
+                      pl.BlockSpec(memory_space=pl.ANY), one, wide, wide, pl.BlockSpec((9, D), lambda i, n, a: (0, 0))],
+            out_specs=[wide, hidden, hidden, wide, wide, wide, wide, wide, one, pl.BlockSpec((8, D), lambda i, n, a: (0, 0))],
+            scratch_shapes=ffn_scratch(w_all, block)
+            + [pltpu.VMEM((D, D), b16), pltpu.SemaphoreType.DMA((12 * zs,))],
         ),
         out_shape=[shape(D, b16), shape(FF, b16), shape(FF, b16), shape(D, b16), shape(D, f32), shape(D, f32),
                    shape(D, b16), shape(D, b16), shape(FF, f32, 1), shape(D, f32, 8)],
         compiler_params=pltpu.CompilerParams(vmem_limit_bytes=VMEM),
         cost_estimate=cost(40),
-    )(length, ctx, w_attn, rounded, mask, w_all, bias, cot, rl, small)
+    )(length, at, ctx, mine, peer, rounded, mask, w_all, bias, cot, rl, small)
 
 
 def input_kernel(dr_ref, d0_ref, d1_ref, d2_ref, w0_ref, w1_ref, w2_ref, z_ref, wg_ref, mask_ref,
@@ -607,13 +599,6 @@
     for dim, axis in dims:
         v = jnp.roll(v, sign * net.at[axis], dim)
     return v
-
-
-def natural(net, places, mine, peer):
-    if mine.shape[3] % 16 == 0:
-        return assemble(places, mine, peer)
-    v = rolled(net, jnp.stack([mine, peer])[:, :, :, 3:], ((0, "c"), (1, "y"), (2, "z")), 1)
-    return v.transpose(2, 1, 0, 4, 3, 5).reshape(D, D)
 
 
 def wide_rows(net, places, mine, peer):
@@ -705,13 +690,13 @@
     probs1, *kept, q1, w1 = attend(1, y1, p1, kept)
     y2, probs1, q1, w1, *kept = bar((y2, probs1, q1, w1, *kept))
     p2 = net.shift(y2, "c", 1)
-    w_attn = natural(net, places, y2, p2)
     probs2, context, context_f, inv_sum, q2, w2 = attend(2, y2, p2, kept)
     qkv, w_qkv, probs = (q0, q1, q2), (w0, w1, w2), (probs0, probs1, probs2)
 
+    at2, mine2, peer2 = wide_rows(net, places, y2, p2)
     bias_in = w_all[:, 2 * own, :own].reshape(1, -1).astype(f32)
     low, act, d_hidden, d_branch, layer_out, d_res1, d_attention, d_context, g_bias_in, red = middle(
-        lengths, context, w_attn, rounded, mask, w_all_k, bias_in, cotangent[0], inv_sum, small_params)
+        lengths, at2, context, mine2, peer2, rounded, mask, w_all_k, bias_in, cotangent[0], inv_sum, small_params)
 
     def attend_back(g):
         return attn_bwd(qkv[g], d_context, context_f, probs[g], table, gates, g * group_heads, group_heads)
@@ -732,40 +717,47 @@
     d2, dg2, do2 = attend_back(2)
     got_1, d2, dg2, do2 = bar((got_1, d2, dg2, do2))
     m2 = by_owner(weight_grads(rounded_t, d1, d2, jnp.zeros((8, 128), f32)))
+    m2, dg0, dg1, dg2, do0, do1, do2 = bar((m2, dg0, dg1, dg2, do0, do1, do2))
     stay_2, got_2 = net.scatter([m2], "c", 2)
-
     dgate = jnp.concatenate([dg0, dg1, dg2], axis=0).reshape(H, seq)
-    doff = jnp.concatenate([do0, do1, do2], axis=0).reshape(H, 2 * seq)
     d_a = dgate * (gate_b * const - 1.0) * gate_a * (1.0 - gate_a)
     d_b = dgate * gate_a * const * gate_b * (1.0 - gate_b)
-    d_const = jnp.sum(dgate * gate_a * gate_b, axis=1)
+    d_const = jnp.sum(dgate * gate_a * gate_b, axis=1, keepdims=True)
     dz = jnp.concatenate([d_a, d_b], axis=0)
     dz_hi = dz.astype(b16)
     dz_lo = (dz - dz_hi.astype(f32)).astype(b16)
-    g_z2 = dot(jnp.concatenate([dz_hi, dz_lo], axis=0), rounded).reshape(2, 2, H, H, HD)
-    g_z = jnp.sum((g_z2[0] + g_z2[1]) * eye, axis=(1, 2))
-    g_zb = jnp.sum(dz.reshape(2, H * seq), axis=1)
-    g_gate_local = jnp.repeat(jnp.concatenate([g_z, g_zb[:, None]], axis=1).T, 4, axis=1)
-    pos3 = dot(onehot, jnp.concatenate(split3(doff), axis=0), NT).reshape(NB, 3, H)
-    pos_local = jnp.concatenate([jnp.sum(pos3, axis=1), d_const[None, :]], axis=0)
-    got_2, got_1, dz_hi, dz_lo, pos_local, g_gate_local, d_res1 = bar(
-        (got_2, got_1, dz_hi, dz_lo, pos_local, g_gate_local, d_res1))
+    got_2, got_1, dz, dz_hi, dz_lo, d_const, d_res1 = bar((got_2, got_1, dz, dz_hi, dz_lo, d_const, d_res1))
+
     stay_2, got_2 = net.scatter(stay_2 + got_2, "y", 1)
     stay_1, got_1 = net.scatter(stay_1 + got_1, "z", 0)
     feature_grad, red0 = input_grad(
         d_res1, (d0, d1, d2), w_qkv, jnp.concatenate([dz_hi, dz_lo, dz_hi], axis=0),
         jnp.concatenate([wg3[0], wg3[0], wg3[1]], axis=0), mask)
     small_local = jnp.concatenate([red0[:2], red[:6], red0[2:3]], axis=0)
-
-    parts = [small_local, pos_local, g_gate_local, g_bias_in]
-    counts = [p.size for p in parts]
-    pad = -(sum(counts) + 1) % 1024
-    packed = jnp.concatenate([p.reshape(-1) for p in parts])
-    got_2, got_1, feature_grad, packed = bar((got_2, got_1, feature_grad, packed))
+    got_2, got_1, feature_grad, small_local, do0, do1, do2, dz = bar(
+        (got_2, got_1, feature_grad, small_local, do0, do1, do2, dz))
     stay_2, got_2 = net.scatter(stay_2 + got_2, "z", 0)
     m1 = added(stay_1 + got_1).astype(b16)
     m1 = tree_sum([m1.astype(f32)] + [net.shift(m1, "x", k).astype(f32) for k in range(1, t_size)])
-    got_2, m1, g_ffn = bar((got_2, m1, g_ffn))
+    exact = lax.Precision.HIGHEST
+    g_z2 = dot(jnp.concatenate([dz_hi, dz_lo], axis=0), rounded)
+    of_head = jnp.arange(D)[None, :] // HD == jnp.arange(2 * H)[:, None] % H
+    g_z = jnp.where(of_head, g_z2[: 2 * H] + g_z2[2 * H :], 0.0)
+    kind = (jnp.arange(2 * H)[None, :] // H == jnp.arange(2)[:, None]).astype(f32)
+    fold = (jnp.arange(D)[:, None] % HD == jnp.arange(HD)[None, :]).astype(f32)
+    g_z = jnp.dot(jnp.dot(kind, g_z, precision=exact), fold, precision=exact)
+    g_zb = jnp.dot(kind, jnp.sum(dz, axis=1, keepdims=True), precision=exact)
+    doff = jnp.concatenate([do0, do1, do2], axis=0).reshape(H, 2 * seq)
+    pos3 = dot(jnp.concatenate(split3(doff), axis=0), onehot, NT)
+    pos_t = jnp.concatenate([pos3[:H] + pos3[H : 2 * H] + pos3[2 * H :], d_const], axis=1)
+
+    wide = 384
+    packed = jnp.concatenate(
+        [small_local[:, :wide], small_local[:, wide:]]
+        + [g_bias_in[:, k * wide : (k + 1) * wide] for k in range(FF // wide)]
+        + [jnp.pad(pos_t, ((0, 0), (0, wide - NB - 1))),
+           jnp.pad(jnp.concatenate([g_z, g_zb], axis=1), ((0, 0), (0, wide - HD - 1)))], axis=0)
+    got_2, m1, packed, g_ffn = bar((got_2, m1, packed, g_ffn))
     m2 = added(stay_2 + got_2).astype(b16)
     m2 = tree_sum([m2.astype(f32)] + [net.shift(m2, "x", k).astype(f32) for k in range(1, t_size)])
     stay_f, got_f = net.scatter([g_ffn], "x", 0)
@@ -774,19 +766,20 @@
     g_in_t = g_ffn[:own].T
     g_outw = g_ffn[own:]
     own_sum = jnp.sum(jnp.square(m2)) * (1.0 / t_size) + own_ffn
-    flat = jnp.concatenate([packed, own_sum.reshape(1), jnp.zeros((pad,), f32)]).reshape(-1, 128)
-    flat = net.total(flat).reshape(-1)
-    own_sum = flat[sum(counts)]
-    shared = jnp.sum(jnp.where(jnp.arange(flat.size) < sum(counts), flat * flat, 0.0))
+    used = packed.shape[0]
+    flat = jnp.concatenate([packed, jnp.full((48 - used, wide), own_sum)], axis=0)
+    flat = net.total(flat)
+    own_sum = flat[used, 0]
+    flat = flat[:used]
+    shared = jnp.sum(jnp.square(flat)) + 3.0 * jnp.sum(jnp.square(flat[38:40]))
     m1 = m1.reshape(rows, 2, 3, cols)
     m2 = m2.reshape(rows, 2, 3, cols)
     g_qkv = jnp.stack([m1[:, 0], m2[:, 0], m2[:, 1]], axis=2).transpose(1, 0, 2, 3).reshape(3, rows, D)
     g_out = m1[:, 1].reshape(rows, D)
-    pieces, at = [], 0
-    for p, count in zip(parts, counts):
-        pieces.append(flat[at : at + count].reshape(p.shape))
-        at += count
-    g_small, g_pos, g_gate, g_bias = pieces
+    g_small = jnp.concatenate([flat[:9], flat[9:18]], axis=1)
+    g_bias = flat[18:26].reshape(-1, own)
+    g_pos = flat[26:38, : NB + 1].T
+    g_gate = jnp.repeat(flat[38:40, : HD + 1].T, 4, axis=1)
     grad_norm = jnp.sqrt(own_sum + shared)
     clip = jnp.minimum(1.0, CLIP_NORM / (grad_norm + 1e-06))
     count = step_count[0].astype(f32)

time: 377 us -> 365 us (0.968)
  waiting for transfers between devices: 38.5 us -> 52.5 us
  local copies, waits for them, and re-layouts: 37.8 us -> 25.4 us
  other arithmetic: 43.9 us -> 38.8 us
  Pallas kernels: 179 us -> 175 us
  starting transfers between devices: 46.9 us -> 43.1 us
    ppermute x33, waiting for transfers between devices: 38.4 us -> 50.1 us  [shift(): return lax.ppermute(v, ('dp', 'tensor'), pairs)]
    reshape x5 -> x1, local copies, waits for them, and re-layouts: 5.49 us -> 0.07 us  [local(): g_bias = flat[18:26].reshape(-1, own)]
    ppermute x33, starting transfers between devices: 46.8 us -> 43.1 us  [shift(): return lax.ppermute(v, ('dp', 'tensor'), pairs)]
  transfers between devices with their start and end apart: 35 -> 35, of which waited for: 15 -> 17; matrix products, arithmetic and copies ran while one was open for 18% -> 13% of each run, Pallas kernels for 34% -> 33%
where the time goes in v4:
time: 365 us; the launch traced here: 360 us
  Pallas kernels  175 us (48%)
  waiting for transfers between devices  52.5 us (14%)
  starting transfers between devices  43.1 us (12%)
  other arithmetic  38.8 us (11%)
  local copies, waits for them, and re-layouts  25.4 us (7%)
  between operations  22 us (6%)
    ppermute x33, waiting for transfers between devices, shift(): return lax.ppermute(v, ('dp', 'tensor'), pairs)  50.1 us
    pallas_call x3, Pallas kernels, attn_fwd(): pl.pallas_call(functools.partial(fwd_kernel, seq=seq, ib=ib, zs=zs, rows=...  47.9 us
    ppermute x33, starting transfers between devices, shift(): return lax.ppermute(v, ('dp', 'tensor'), pairs)  43.1 us
    pallas_call x1, Pallas kernels, middle(): pl.pallas_call(functools.partial(middle_kernel, block=block), grid_spec=p...  41.2 us
    pallas_call x3, Pallas kernels, attn_bwd(): pl.pallas_call(functools.partial(bwd_kernel, seq=seq, ib=ib), grid=(heads...  40.2 us
    pallas_call x1, Pallas kernels, ffn_grads(): pl.pallas_call(ffn_grad_kernel, grid=(FF // cols,), in_specs=[hidden, hid...  15 us
    pallas_call x2, Pallas kernels, weight_grads(): pl.pallas_call(functools.partial(wgrad_kernel, pair=pair), grid=(D // blo...  13.7 us
    pallas_call x1, Pallas kernels, input_grad(): pl.pallas_call(input_kernel, grid=(seq // block,), in_specs=[wide, part,...  9.37 us
  transfers between devices with their start and end apart: 35, of which 17 were waited for; matrix products, arithmetic and copies ran while one was open for 13% of the time, Pallas kernels for 33%

profile of v4, /device:TPU:0, one launch (start us, length us, event | category | flops | bytes accessed | tf_op | source)
XLA Modules:
  0.0 359.7 jit_solution(8829089884073253134)
XLA Ops:
  9.0 5.0 %collective-permute-start = (bf16[1,1,3,48,256]{4,3,2,1,0:T(8,128)(2,1)S(1)}, bf16[1,1,3,48,256]{4,3,2,1,0:T(8,128)(2,1)S(1)}, u32[]{:S(2)}, u32[]{:S(2)}) collective-permute-start(bf16[1,1,3,48,256]{4,3,2,1,0:T(8,128)(2,1)S(1)} %get-tuple-element.314), channel_id=1, source_target_pairs={{0,24},{1,25},{2,26},{3,27},{4,28},{5,29},{6,30},{7,31},{8,0},{9,1... | collective-permute-start | bytes 221192 | tf_op jit(solution)/shard_map/ppermute | solution.py:562
  18.5 7.7 %shard_map.482.t_ref = f32[12,128,2048]{2,1,0:T(8,128)} custom-call(f32[12,1,2048]{2,1,0:T(1,128)} %add.534.off_ref), custom_call_target="tpu_custom_call" | custom-call | bytes 24000000 | tf_op jit(solution)/shard_map/pallas_call | solution.py:60
  29.8 2.9 collective-permute-start.4
  58.4 15.8 %shard_map.483 = (bf16[4,1024,1024]{2,1,0:T(8,128)(2,1)}, bf16[1024,768]{1,0:T(8,128)(2,1)}, f32[1024,768]{1,0:T(8,128)}, f32[1024,768]{1,0:T(8,128)}, bf16[3,10...) custom-call(s32[1]{0:T(128)S(6)} %copy.172.len_ref, s32[4]{0:T(128)} %pad_add_fusion.1.at_ref, ...), custom_call_target="tpu_custom_call" | custom-call | bytes 44400000 | tf_op jit(solution)/shard_map/pallas_call | solution.py:145
  79.4 16.0 %shard_map.484 = (bf16[4,1024,1024]{2,1,0:T(8,128)(2,1)}, bf16[1024,768]{1,0:T(8,128)(2,1)}, f32[1024,768]{1,0:T(8,128)}, f32[1024,768]{1,0:T(8,128)}, bf16[3,10...) custom-call(s32[1]{0:T(128)S(6)} %copy.172.len_ref, ...), custom_call_target="tpu_custom_call", output_to_operand_aliasing={{1}: (8, {}), {2}: (9, {}), {3}: (10, {})} | custom-call | bytes 44400000 | tf_op jit(solution)/shard_map/pallas_call | solution.py:145
  95.4 4.1 %collective-permute-done.12 = bf16[1,4,6,48,256]{4,3,2,1,0:T(8,128)(2,1)} collective-permute-done((bf16[1,4,6,48,256]{4,3,2,1,0:T(8,128)(2,1)S(1)}, bf16[1,4,6,48,256]{4,3,2,1,0:T(8,128)(2,1)}, u32[]{:S(2)}, u32[]{:S(2)}) %collective-permute-start.12) | collective-permute-done | bytes 589856 | tf_op jit(solution)/shard_map/ppermute | solution.py:562
  103.8 16.1 %shard_map.485 = (bf16[4,1024,1024]{2,1,0:T(8,128)(2,1)}, bf16[1024,768]{1,0:T(8,128)(2,1)}, f32[1024,768]{1,0:T(8,128)}, f32[1024,768]{1,0:T(8,128)}, bf16[3,10...) custom-call(s32[1]{0:T(128)S(6)} %copy.172.len_ref, ...), custom_call_target="tpu_custom_call", output_to_operand_aliasing={{1}: (8, {}), {2}: (9, {}), {3}: (10, {})} | custom-call | bytes 44400000 | tf_op jit(solution)/shard_map/pallas_call | solution.py:145
  119.9 2.3 all-gather.3.cloned.1.call-done
  123.7 41.2 %shard_map.486 = (bf16[1024,768]{1,0:T(8,128)(2,1)}, bf16[1024,3072]{1,0:T(8,128)(2,1)}, bf16[1024,3072]{1,0:T(8,128)(2,1)}, bf16[1024,768]{1,0:T(8,128)(2,1)}, ...) custom-call(s32[1]{0:T(128)S(6)} %copy.172.len_ref, ...), custom_call_target="tpu_custom_call" | custom-call | bytes 120000000 | tf_op jit(solution)/shard_map/pallas_call | solution.py:461
  165.0 15.0 %shard_map.487 = bf16[32,192,768]{2,1,0:T(8,128)(2,1)} custom-call(bf16[1024,3072]{1,0:T(8,128)(2,1)} %get-tuple-element.186.dh_ref, bf16[1024,3072]{1,0:T(8,128)(2,1)} %get-tuple-element.187.act_ref, bf16[1024,768]{1,0:T(8,128)(2,1)} %get-tuple-element.188.low_ref, bf16[1024,768]{1,0:T(8,128)(2,1)} %get-tuple-element.189.dlow_ref), custom_call_target="tpu_custom_call" | custom-call | bytes 48000000 | tf_op jit(solution)/shard_map/pallas_call | solution.py:298
  180.0 13.5 %shard_map.488 = (bf16[3,1024,256]{2,1,0:T(8,128)(2,1)}, f32[4,1,1024]{2,1,0:T(1,128)}, f32[4,1,2048]{2,1,0:T(1,128)}) custom-call(bf16[3,1024,256]{2,1,0:T(8,128)(2,1)} %get-tuple-element.185.q_ref.k_ref.v_ref, bf16[3,1024,256]{2,1,0:T(8,128)(2,1)} %get-tuple-element.185.q_ref.k_ref.v_ref, bf16[3,1024,256]{2,1,0:T(8,128)(2,1)} %get-tuple-element.185.q_ref.k_ref.v_ref, ...), custom_call_target="tpu_custom_call" | custom-call | bytes 36000000 | tf_op jit(solution)/shard_map/pallas_call | solution.py:227
  193.5 7.2 %shard_map.489 = bf16[768,1536]{1,0:T(8,128)(2,1)} custom-call(bf16[768,1024]{1,0:T(8,128)(2,1)} %fusion.118.xt_ref, bf16[3,1024,256]{2,1,0:T(8,128)(2,1)} %get-tuple-element.229.d_ref.d0_ref, bf16[1024,768]{1,0:T(8,128)(2,1)} %get-tuple-element.180.c_ref.a_ref, bf16[1024,768]{1,0:T(8,128)(2,1)} %get-tuple-element.195.b_ref), custom_call_target="tpu_custom_call" | custom-call | bytes 15000000 | tf_op jit(solution)/shard_map/pallas_call | solution.py:273
  200.7 2.5 dynamic-slice_bitcast_fusion.1
  203.5 13.4 %shard_map.490 = (bf16[3,1024,256]{2,1,0:T(8,128)(2,1)}, f32[4,1,1024]{2,1,0:T(1,128)}, f32[4,1,2048]{2,1,0:T(1,128)}) custom-call(bf16[3,1024,256]{2,1,0:T(8,128)(2,1)} %get-tuple-element.199.q_ref.k_ref.v_ref, bf16[3,1024,256]{2,1,0:T(8,128)(2,1)} %get-tuple-element.199.q_ref.k_ref.v_ref, bf16[3,1024,256]{2,1,0:T(8,128)(2,1)} %get-tuple-element.199.q_ref.k_ref.v_ref, ...), custom_call_target="tpu_custom_call" | custom-call | bytes 36000000 | tf_op jit(solution)/shard_map/pallas_call | solution.py:227
  216.8 2.5 fusion.5
  220.8 13.4 %shard_map.491 = (bf16[3,1024,256]{2,1,0:T(8,128)(2,1)}, f32[4,1,1024]{2,1,0:T(1,128)}, f32[4,1,2048]{2,1,0:T(1,128)}) custom-call(bf16[3,1024,256]{2,1,0:T(8,128)(2,1)} %get-tuple-element.207.q_ref.k_ref.v_ref, bf16[3,1024,256]{2,1,0:T(8,128)(2,1)} %get-tuple-element.207.q_ref.k_ref.v_ref, bf16[3,1024,256]{2,1,0:T(8,128)(2,1)} %get-tuple-element.207.q_ref.k_ref.v_ref, ...), custom_call_target="tpu_custom_call" | custom-call | bytes 36000000 | tf_op jit(solution)/shard_map/pallas_call | solution.py:227
  234.2 4.6 %collective-permute-done.16 = bf16[4,48,1536]{2,1,0:T(8,128)(2,1)} collective-permute-done((bf16[4,48,1536]{2,1,0:T(8,128)(2,1)}, bf16[4,48,1536]{2,1,0:T(8,128)(2,1)}, u32[]{:S(2)}, u32[]{:S(2)}) %collective-permute-start.16) | collective-permute-done | bytes 589856 | tf_op jit(solution)/shard_map/ppermute | solution.py:562
  239.4 6.4 %shard_map.492 = bf16[768,1536]{1,0:T(8,128)(2,1)} custom-call(bf16[768,1024]{1,0:T(8,128)(2,1)} %fusion.118.xt_ref, bf16[3,1024,256]{2,1,0:T(8,128)(2,1)} %get-tuple-element.205.d_ref.d1_ref, bf16[3,1024,256]{2,1,0:T(8,128)(2,1)} %get-tuple-element.213.a_ref.d2_ref, f32[8,128]{1,0:T(8,128)} %broadcast_in_dim.69.b_ref), custom_call_target="tpu_custom_call" | custom-call | bytes 15000000 | tf_op jit(solution)/shard_map/pallas_call | solution.py:273
  245.9 2.4 dynamic-slice_bitcast_fusion
  251.7 2.3 fusion.24
  255.7 2.2 collective-permute-start.20
  263.7 9.4 %shard_map.493 = (f32[1024,768]{1,0:T(8,128)}, f32[8,768]{1,0:T(8,128)}) custom-call(f32[1024,768]{1,0:T(8,128)} %get-tuple-element.228.dr_ref, bf16[3,1024,256]{2,1,0:T(8,128)(2,1)} %get-tuple-element.229.d_ref.d0_ref, bf16[3,1024,256]{2,1,0:T(8,128)(2,1)} %get-tuple-element.205.d_ref.d1_ref, bf16[3,1024,256]{2,1,0:T(8,128)(2,1)} %get-tuple-element.213.a_ref.d2_ref, ...), custom_call_target="tpu_custom_call" | custom-call | bytes 24000000 | tf_op jit(solution)/shard_map/pallas_call | solution.py:510
  274.7 8.3 %collective-permute-done.18 = bf16[4,48,1536]{2,1,0:T(8,128)(2,1)} collective-permute-done((bf16[4,48,1536]{2,1,0:T(8,128)(2,1)}, bf16[4,48,1536]{2,1,0:T(8,128)(2,1)}, u32[]{:S(2)}, u32[]{:S(2)}) %collective-permute-start.18) | collective-permute-done | bytes 589856 | tf_op jit(solution)/shard_map/ppermute | solution.py:562
  288.3 3.3 collective-permute-start.24
  292.9 4.2 %collective-permute-done.22 = bf16[48,1536]{1,0:T(8,128)(2,1)S(1)} collective-permute-done((bf16[48,1536]{1,0:T(8,128)(2,1)S(1)}, bf16[48,1536]{1,0:T(8,128)(2,1)S(1)}, u32[]{:S(2)}, u32[]{:S(2)}) %collective-permute-start.22) | collective-permute-done | bytes 147488 | tf_op jit(solution)/shard_map/ppermute | solution.py:562
  297.1 5.4 %collective-permute-done.23 = bf16[48,1536]{1,0:T(8,128)(2,1)S(1)} collective-permute-done((bf16[48,1536]{1,0:T(8,128)(2,1)S(1)}, bf16[48,1536]{1,0:T(8,128)(2,1)S(1)}, u32[]{:S(2)}, u32[]{:S(2)}) %collective-permute-start.23) | collective-permute-done | bytes 147488 | tf_op jit(solution)/shard_map/ppermute | solution.py:562
  312.9 3.7 %collective-permute-done.27 = bf16[192,768]{1,0:T(8,128)(2,1)S(1)} collective-permute-done((bf16[192,768]{1,0:T(8,128)(2,1)S(1)}, bf16[192,768]{1,0:T(8,128)(2,1)S(1)}, u32[]{:S(2)}, u32[]{:S(2)}) %collective-permute-start.27) | collective-permute-done | bytes 294944 | tf_op jit(solution)/shard_map/ppermute | solution.py:562
  320.6 3.2 collective-permute-done.29
  324.6 3.7 %collective-permute-done.30 = f32[48,384]{1,0:T(8,128)S(1)} collective-permute-done((f32[48,384]{1,0:T(8,128)S(1)}, f32[48,384]{1,0:T(8,128)S(1)}, u32[]{:S(2)}, u32[]{:S(2)}) %collective-permute-start.30) | collective-permute-done | bytes 73760 | tf_op jit(solution)/shard_map/ppermute | solution.py:562
  328.3 2.8 collective-permute-start.31
  333.4 3.1 collective-permute-start.32
  336.6 2.3 collective-permute-done.32
  (306 shorter events, 91.8 us)
Async XLA Ops:
  7.2 114.9 %all-gather.3.cloned.1.call-start = ((), (), s32[]{:S(2)}) async-start(), calls=%async_computation.2 | async-start | bytes 10137600 | tf_op jit(solution)/shard_map/all_gather | solution.py:644
  9.0 18.1 %collective-permute-start = (bf16[1,1,3,48,256]{4,3,2,1,0:T(8,128)(2,1)S(1)}, bf16[1,1,3,48,256]{4,3,2,1,0:T(8,128)(2,1)S(1)}, u32[]{:S(2)}, u32[]{:S(2)}) collective-permute-start(bf16[1,1,3,48,256]{4,3,2,1,0:T(8,128)(2,1)S(1)} %get-tuple-element.314), channel_id=1, source_target_pairs={{0,24},{1,25},{2,26},{3,27},{4,28},{5,29},{6,30},{7,31},{8,0},{9,1... | collective-permute-start | bytes 221192 | tf_op jit(solution)/shard_map/ppermute | solution.py:562
  14.0 13.1 %collective-permute-start.1 = (bf16[1,1,3,48,256]{4,3,2,1,0:T(8,128)(2,1)S(1)}, bf16[1,1,3,48,256]{4,3,2,1,0:T(8,128)(2,1)S(1)}, u32[]{:S(2)}, u32[]{:S(2)}) collective-permute-start(bf16[1,1,3,48,256]{4,3,2,1,0:T(8,128)(2,1)S(1)} %get-tuple-element.314), channel_id=1, source_target_pairs={{0,16},{1,17},{2,18},{3,19},{4,20},{5,21},{6,22},{7,23},{8,24},{9,... | collective-permute-start | bytes 221192 | tf_op jit(solution)/shard_map/ppermute | solution.py:562
  14.0 13.1 %collective-permute-start.2 = (bf16[1,1,3,48,256]{4,3,2,1,0:T(8,128)(2,1)S(1)}, bf16[1,1,3,48,256]{4,3,2,1,0:T(8,128)(2,1)S(1)}, u32[]{:S(2)}, u32[]{:S(2)}) collective-permute-start(bf16[1,1,3,48,256]{4,3,2,1,0:T(8,128)(2,1)S(1)} %get-tuple-element.314), channel_id=1, source_target_pairs={{0,8},{1,9},{2,10},{3,11},{4,12},{5,13},{6,14},{7,15},{8,16},{9,17... | collective-permute-start | bytes 221192 | tf_op jit(solution)/shard_map/ppermute | solution.py:562
  27.9 275.9 %reduce-scatter.2.cloned.1.call-start = ((), (), s32[]{:S(2)}) async-start(), calls=%async_computation.1 | async-start | bytes 10027008 | tf_op jit(solution)/shard_map/reduce_scatter | solution.py:709
  29.8 11.8 %collective-permute-start.4 = (bf16[1,1,3,48,256]{4,3,2,1,0:T(8,128)(2,1)}, bf16[1,1,3,48,256]{4,3,2,1,0:T(8,128)(2,1)}, u32[]{:S(2)}, u32[]{:S(2)}) collective-permute-start(bf16[1,1,3,48,256]{4,3,2,1,0:T(8,128)(2,1)} %get-tuple-element.146), channel_id=1, source_target_pairs={{0,24},{1,25},{2,26},{3,27},{4,28},{5,29},{6,30},{7,31},{8,0},{9,1... | collective-permute-start | bytes 221192 | tf_op jit(solution)/shard_map/ppermute | solution.py:562
  32.7 9.0 %collective-permute-start.5 = (bf16[1,1,3,48,256]{4,3,2,1,0:T(8,128)(2,1)}, bf16[1,1,3,48,256]{4,3,2,1,0:T(8,128)(2,1)}, u32[]{:S(2)}, u32[]{:S(2)}) collective-permute-start(bf16[1,1,3,48,256]{4,3,2,1,0:T(8,128)(2,1)} %get-tuple-element.146), channel_id=1, source_target_pairs={{0,16},{1,17},{2,18},{3,19},{4,20},{5,21},{6,22},{7,23},{8,24},{9,... | collective-permute-start | bytes 221192 | tf_op jit(solution)/shard_map/ppermute | solution.py:562
  33.8 7.8 %collective-permute-start.6 = (bf16[1,1,3,48,256]{4,3,2,1,0:T(8,128)(2,1)}, bf16[1,1,3,48,256]{4,3,2,1,0:T(8,128)(2,1)}, u32[]{:S(2)}, u32[]{:S(2)}) collective-permute-start(bf16[1,1,3,48,256]{4,3,2,1,0:T(8,128)(2,1)} %get-tuple-element.146), channel_id=1, source_target_pairs={{0,8},{1,9},{2,10},{3,11},{4,12},{5,13},{6,14},{7,15},{8,16},{9,17... | collective-permute-start | bytes 221192 | tf_op jit(solution)/shard_map/ppermute | solution.py:562
  34.7 9.8 %collective-permute-start.3 = (bf16[1,4,3,48,256]{4,3,2,1,0:T(8,128)(2,1)}, bf16[1,4,3,48,256]{4,3,2,1,0:T(8,128)(2,1)S(1)}, u32[]{:S(2)}, u32[]{:S(2)}) collective-permute-start(bf16[1,4,3,48,256]{4,3,2,1,0:T(8,128)(2,1)} %pad_maximum_fusion.4), channel_id=1, source_target_pairs={{0,4},{1,5},{2,6},{3,7},{4,0},{5,1},{6,2},{7,3},{8,12},{9,13},{10,... | collective-permute-start | bytes 884744 | tf_op jit(solution)/shard_map/ppermute | solution.py:562
  46.7 27.5 %collective-permute-start.10 = (bf16[1,1,6,48,256]{4,3,2,1,0:T(8,128)(2,1)}, bf16[1,1,6,48,256]{4,3,2,1,0:T(8,128)(2,1)}, u32[]{:S(2)}, u32[]{:S(2)}) collective-permute-start(bf16[1,1,6,48,256]{4,3,2,1,0:T(8,128)(2,1)} %pad_maximum_fusion.6), channel_id=1, source_target_pairs={{0,16},{1,17},{2,18},{3,19},{4,20},{5,21},{6,22},{7,23},{8,24},{9,... | collective-permute-start | bytes 442376 | tf_op jit(solution)/shard_map/ppermute | solution.py:562
  48.8 25.5 %collective-permute-start.11 = (bf16[1,1,6,48,256]{4,3,2,1,0:T(8,128)(2,1)}, bf16[1,1,6,48,256]{4,3,2,1,0:T(8,128)(2,1)}, u32[]{:S(2)}, u32[]{:S(2)}) collective-permute-start(bf16[1,1,6,48,256]{4,3,2,1,0:T(8,128)(2,1)} %pad_maximum_fusion.6), channel_id=1, source_target_pairs={{0,8},{1,9},{2,10},{3,11},{4,12},{5,13},{6,14},{7,15},{8,16},{9,17... | collective-permute-start | bytes 442376 | tf_op jit(solution)/shard_map/ppermute | solution.py:562
  50.8 23.5 %collective-permute-start.9 = (bf16[1,1,6,48,256]{4,3,2,1,0:T(8,128)(2,1)}, bf16[1,1,6,48,256]{4,3,2,1,0:T(8,128)(2,1)}, u32[]{:S(2)}, u32[]{:S(2)}) collective-permute-start(bf16[1,1,6,48,256]{4,3,2,1,0:T(8,128)(2,1)} %pad_maximum_fusion.6), channel_id=1, source_target_pairs={{0,24},{1,25},{2,26},{3,27},{4,28},{5,29},{6,30},{7,31},{8,0},{9,1... | collective-permute-start | bytes 442376 | tf_op jit(solution)/shard_map/ppermute | solution.py:562
  52.8 22.7 %collective-permute-start.8 = (bf16[1,4,3,48,256]{4,3,2,1,0:T(8,128)(2,1)S(1)}, bf16[1,4,3,48,256]{4,3,2,1,0:T(8,128)(2,1)}, u32[]{:S(2)}, u32[]{:S(2)}) collective-permute-start(bf16[1,4,3,48,256]{4,3,2,1,0:T(8,128)(2,1)S(1)} %pad_maximum_fusion.5), channel_id=1, source_target_pairs={{0,4},{1,5},{2,6},{3,7},{4,0},{5,1},{6,2},{7,3},{8,12},{9,13},{10,... | collective-permute-start | bytes 884744 | tf_op jit(solution)/shard_map/ppermute | solution.py:562
  76.6 22.9 %collective-permute-start.12 = (bf16[1,4,6,48,256]{4,3,2,1,0:T(8,128)(2,1)S(1)}, bf16[1,4,6,48,256]{4,3,2,1,0:T(8,128)(2,1)}, u32[]{:S(2)}, u32[]{:S(2)}) collective-permute-start(bf16[1,4,6,48,256]{4,3,2,1,0:T(8,128)(2,1)S(1)} %pad_maximum_fusion.3), channel_id=1, source_target_pairs={{0,4},{1,5},{2,6},{3,7},{4,0},{5,1},{6,2},{7,3},{8,12},{9,13},{10,... | collective-permute-start | bytes 1769480 | tf_op jit(solution)/shard_map/ppermute | solution.py:562
  100.7 3.0 collective-permute-start.14
  203.2 13.6 %collective-permute-start.15 = (bf16[4,2,48,1536]{3,2,1,0:T(8,128)(2,1)}, bf16[4,2,48,1536]{3,2,1,0:T(8,128)(2,1)S(1)}, u32[]{:S(2)}, u32[]{:S(2)}) collective-permute-start(bf16[4,2,48,1536]{3,2,1,0:T(8,128)(2,1)} %dynamic-slice_bitcast_fusion.1), channel_id=1, source_target_pairs={{0,2},{1,3},{2,0},{3,1},{4,6},{5,7},{6,4},{7,5},{8,10},{9,11},{10,... | collective-permute-start | bytes 3538952 | tf_op jit(solution)/shard_map/ppermute | solution.py:562
  219.3 19.5 %collective-permute-start.16 = (bf16[4,48,1536]{2,1,0:T(8,128)(2,1)}, bf16[4,48,1536]{2,1,0:T(8,128)(2,1)}, u32[]{:S(2)}, u32[]{:S(2)}) collective-permute-start(bf16[4,48,1536]{2,1,0:T(8,128)(2,1)} %fusion.5), channel_id=1, source_target_pairs={{0,4},{1,5},{2,6},{3,7},{4,0},{5,1},{6,2},{7,3},{8,12},{9,13},{10,... | collective-permute-start | bytes 1769480 | tf_op jit(solution)/shard_map/ppermute | solution.py:562
  248.3 3.4 collective-permute-start.17
  253.9 20.7 %collective-permute-start.19 = (bf16[48,1536]{1,0:T(8,128)(2,1)}, bf16[48,1536]{1,0:T(8,128)(2,1)}, u32[]{:S(2)}, u32[]{:S(2)}) collective-permute-start(bf16[48,1536]{1,0:T(8,128)(2,1)} %get-tuple-element.304), channel_id=1, source_target_pairs={{0,8},{1,9},{2,10},{3,11},{4,12},{5,13},{6,14},{7,15},{8,16},{9,17... | collective-permute-start | bytes 442376 | tf_op jit(solution)/shard_map/ppermute | solution.py:562
  255.7 19.0 %collective-permute-start.20 = (bf16[48,1536]{1,0:T(8,128)(2,1)}, bf16[48,1536]{1,0:T(8,128)(2,1)}, u32[]{:S(2)}, u32[]{:S(2)}) collective-permute-start(bf16[48,1536]{1,0:T(8,128)(2,1)} %get-tuple-element.303), channel_id=1, source_target_pairs={{0,16},{1,17},{2,18},{3,19},{4,20},{5,21},{6,22},{7,23},{8,24},{9,... | collective-permute-start | bytes 442376 | tf_op jit(solution)/shard_map/ppermute | solution.py:562
  257.9 16.8 %collective-permute-start.21 = (bf16[48,1536]{1,0:T(8,128)(2,1)S(1)}, bf16[48,1536]{1,0:T(8,128)(2,1)}, u32[]{:S(2)}, u32[]{:S(2)}) collective-permute-start(bf16[48,1536]{1,0:T(8,128)(2,1)S(1)} %get-tuple-element.302), channel_id=1, source_target_pairs={{0,24},{1,25},{2,26},{3,27},{4,28},{5,29},{6,30},{7,31},{8,0},{9,1... | collective-permute-start | bytes 442376 | tf_op jit(solution)/shard_map/ppermute | solution.py:562
  261.4 21.6 %collective-permute-start.18 = (bf16[4,48,1536]{2,1,0:T(8,128)(2,1)}, bf16[4,48,1536]{2,1,0:T(8,128)(2,1)}, u32[]{:S(2)}, u32[]{:S(2)}) collective-permute-start(bf16[4,48,1536]{2,1,0:T(8,128)(2,1)} %fusion.4), channel_id=1, source_target_pairs={{0,4},{1,5},{2,6},{3,7},{4,0},{5,1},{6,2},{7,3},{8,12},{9,13},{10,... | collective-permute-start | bytes 1769480 | tf_op jit(solution)/shard_map/ppermute | solution.py:562
  284.8 8.1 %collective-permute-start.25 = (bf16[48,1536]{1,0:T(8,128)(2,1)S(1)}, bf16[48,1536]{1,0:T(8,128)(2,1)S(1)}, u32[]{:S(2)}, u32[]{:S(2)}) collective-permute-start(bf16[48,1536]{1,0:T(8,128)(2,1)S(1)} %fusion.20), channel_id=1, source_target_pairs={{0,1},{1,0},{2,3},{3,2},{4,5},{5,4},{6,7},{7,6},{8,9},{9,8},{10,11... | collective-permute-start | bytes 442376 | tf_op jit(solution)/shard_map/ppermute | solution.py:562
  287.7 9.4 %collective-permute-start.22 = (bf16[48,1536]{1,0:T(8,128)(2,1)S(1)}, bf16[48,1536]{1,0:T(8,128)(2,1)S(1)}, u32[]{:S(2)}, u32[]{:S(2)}) collective-permute-start(bf16[48,1536]{1,0:T(8,128)(2,1)S(1)} %get-tuple-element.301), channel_id=1, source_target_pairs={{0,8},{1,9},{2,10},{3,11},{4,12},{5,13},{6,14},{7,15},{8,16},{9,17... | collective-permute-start | bytes 442376 | tf_op jit(solution)/shard_map/ppermute | solution.py:562
  288.3 14.2 %collective-permute-start.23 = (bf16[48,1536]{1,0:T(8,128)(2,1)S(1)}, bf16[48,1536]{1,0:T(8,128)(2,1)S(1)}, u32[]{:S(2)}, u32[]{:S(2)}) collective-permute-start(bf16[48,1536]{1,0:T(8,128)(2,1)S(1)} %get-tuple-element.300), channel_id=1, source_target_pairs={{0,16},{1,17},{2,18},{3,19},{4,20},{5,21},{6,22},{7,23},{8,24},{9,... | collective-permute-start | bytes 442376 | tf_op jit(solution)/shard_map/ppermute | solution.py:562
  288.3 14.2 %collective-permute-start.24 = (bf16[48,1536]{1,0:T(8,128)(2,1)S(1)}, bf16[48,1536]{1,0:T(8,128)(2,1)S(1)}, u32[]{:S(2)}, u32[]{:S(2)}) collective-permute-start(bf16[48,1536]{1,0:T(8,128)(2,1)S(1)} %get-tuple-element.299), channel_id=1, source_target_pairs={{0,24},{1,25},{2,26},{3,27},{4,28},{5,29},{6,30},{7,31},{8,0},{9,1... | collective-permute-start | bytes 442376 | tf_op jit(solution)/shard_map/ppermute | solution.py:562
  305.1 6.5 %collective-permute-start.26 = (bf16[48,1536]{1,0:T(8,128)(2,1)S(1)}, bf16[48,1536]{1,0:T(8,128)(2,1)S(1)}, u32[]{:S(2)}, u32[]{:S(2)}) collective-permute-start(bf16[48,1536]{1,0:T(8,128)(2,1)S(1)} %fusion.16), channel_id=1, source_target_pairs={{0,1},{1,0},{2,3},{3,2},{4,5},{5,4},{6,7},{7,6},{8,9},{9,8},{10,11... | collective-permute-start | bytes 442376 | tf_op jit(solution)/shard_map/ppermute | solution.py:562
  307.7 9.0 %collective-permute-start.27 = (bf16[192,768]{1,0:T(8,128)(2,1)S(1)}, bf16[192,768]{1,0:T(8,128)(2,1)S(1)}, u32[]{:S(2)}, u32[]{:S(2)}) collective-permute-start(bf16[192,768]{1,0:T(8,128)(2,1)S(1)} %dynamic-slice_bitcast_fusion.2), channel_id=1, source_target_pairs={{0,1},{1,0},{2,3},{3,2},{4,5},{5,4},{6,7},{7,6},{8,9},{9,8},{10,11... | collective-permute-start | bytes 884744 | tf_op jit(solution)/shard_map/ppermute | solution.py:562
  319.4 4.4 %collective-permute-start.29 = (f32[48,384]{1,0:T(8,128)S(1)}, f32[48,384]{1,0:T(8,128)S(1)}, u32[]{:S(2)}, u32[]{:S(2)}) collective-permute-start(f32[48,384]{1,0:T(8,128)S(1)} %pad_add_fusion), channel_id=1, source_target_pairs={{0,1},{1,0},{2,3},{3,2},{4,5},{5,4},{6,7},{7,6},{8,9},{9,8},{10,11... | collective-permute-start | bytes 221192 | tf_op jit(solution)/shard_map/ppermute | solution.py:562
  323.9 4.4 %collective-permute-start.30 = (f32[48,384]{1,0:T(8,128)S(1)}, f32[48,384]{1,0:T(8,128)S(1)}, u32[]{:S(2)}, u32[]{:S(2)}) collective-permute-start(f32[48,384]{1,0:T(8,128)S(1)} %add.603), channel_id=1, source_target_pairs={{0,4},{1,5},{2,6},{3,7},{4,0},{5,1},{6,2},{7,3},{8,12},{9,13},{10,... | collective-permute-start | bytes 221192 | tf_op jit(solution)/shard_map/ppermute | solution.py:562
  328.3 5.1 %collective-permute-start.31 = (f32[48,384]{1,0:T(8,128)S(1)}, f32[48,384]{1,0:T(8,128)S(1)}, u32[]{:S(2)}, u32[]{:S(2)}) collective-permute-start(f32[48,384]{1,0:T(8,128)S(1)} %add.604), channel_id=1, source_target_pairs={{0,8},{1,9},{2,10},{3,11},{4,12},{5,13},{6,14},{7,15},{8,0},{9,1},... | collective-permute-start | bytes 221192 | tf_op jit(solution)/shard_map/ppermute | solution.py:562
  333.4 5.5 %collective-permute-start.32 = (f32[48,384]{1,0:T(8,128)S(1)}, f32[48,384]{1,0:T(8,128)S(1)}, u32[]{:S(2)}, u32[]{:S(2)}) collective-permute-start(f32[48,384]{1,0:T(8,128)S(1)} %add.605), channel_id=1, source_target_pairs={{0,16},{1,17},{2,18},{3,19},{4,20},{5,21},{6,22},{7,23},{8,24},{9,... | collective-permute-start | bytes 221192 | tf_op jit(solution)/shard_map/ppermute | solution.py:562
  (64 other events, 350.6 us)
Sparse Core Ops, SparseCore 0:
  28.0 94.1 all-gather.2
  180.1 121.2 reduce-scatter.1

commit v5 on v4

--- a/solution.py
+++ b/solution.py
@@ -556,7 +556,8 @@
                     for x in range(sz["x"]):
                         src = {"z": z, "y": y, "c": c, "x": x}
                         dst = dict(src)
-                        dst[axis] = src[axis] ^ k if swap else (src[axis] - k) % sz[axis]
+                        for one in axis:
+                            dst[one] = src[one] ^ k if swap else (src[one] - k) % sz[one]
                         flat = [((q["z"] * 2 + q["y"]) * 2 + q["c"]) * sz["x"] + q["x"] for q in (src, dst)]
                         pairs.append(tuple(flat))
         return lax.ppermute(v, ("dp", "tensor"), pairs)
@@ -587,6 +588,11 @@
         return out
 
     def total(self, v, axes=("c", "x", "y", "z")):
+        if self.t == 2:
+            v = v + self.shift(v, "c", 1, True)
+            near = [self.shift(v, axis, 1, True) for axis in ("x", "y", "xy")]
+            v = (v + near[0]) + (near[1] + near[2])
+            axes = ("z",)
         for axis in axes:
             bit = 1
             while bit < self.sizes[axis]:

time: 365 us -> 364 us (level)
    ppermute x33 -> x34, waiting for transfers between devices: 50.1 us -> 47.4 us  [shift(): return lax.ppermute(v, ('dp', 'tensor'), pairs)]
    ppermute x33 -> x34, starting transfers between devices: 43.1 us -> 44.3 us  [shift(): return lax.ppermute(v, ('dp', 'tensor'), pairs)]
  transfers between devices with their start and end apart: 35 -> 36, of which waited for: 17 -> 18; matrix products, arithmetic and copies ran while one was open for 13% -> 13% of each run, Pallas kernels for 33% -> 33%
where the time goes in v5:
time: 364 us; the launch traced here: 358 us
  Pallas kernels  175 us (48%)
  waiting for transfers between devices  49.8 us (14%)
  starting transfers between devices  44.4 us (12%)
  other arithmetic  38.8 us (11%)
  local copies, waits for them, and re-layouts  25.4 us (7%)
  between operations  22 us (6%)
    pallas_call x3, Pallas kernels, attn_fwd(): pl.pallas_call(functools.partial(fwd_kernel, seq=seq, ib=ib, zs=zs, rows=...  47.9 us
    ppermute x34, waiting for transfers between devices, shift(): return lax.ppermute(v, ('dp', 'tensor'), pairs)  47.4 us
    ppermute x34, starting transfers between devices, shift(): return lax.ppermute(v, ('dp', 'tensor'), pairs)  44.3 us
    pallas_call x1, Pallas kernels, middle(): pl.pallas_call(functools.partial(middle_kernel, block=block), grid_spec=p...  41.2 us
    pallas_call x3, Pallas kernels, attn_bwd(): pl.pallas_call(functools.partial(bwd_kernel, seq=seq, ib=ib), grid=(heads...  40.2 us
    pallas_call x1, Pallas kernels, ffn_grads(): pl.pallas_call(ffn_grad_kernel, grid=(FF // cols,), in_specs=[hidden, hid...  15 us
    pallas_call x2, Pallas kernels, weight_grads(): pl.pallas_call(functools.partial(wgrad_kernel, pair=pair), grid=(D // blo...  13.7 us
    pallas_call x1, Pallas kernels, input_grad(): pl.pallas_call(input_kernel, grid=(seq // block,), in_specs=[wide, part,...  9.35 us
  transfers between devices with their start and end apart: 36, of which 18 were waited for; matrix products, arithmetic and copies ran while one was open for 13% of the time, Pallas kernels for 33%

profile of v5, /device:TPU:0, one launch (start us, length us, event | category | flops | bytes accessed | tf_op | source)
XLA Modules:
  0.0 358.2 jit_solution(12442164736150772948)
XLA Ops:
  9.0 5.0 %collective-permute-start = (bf16[1,1,3,48,256]{4,3,2,1,0:T(8,128)(2,1)S(1)}, bf16[1,1,3,48,256]{4,3,2,1,0:T(8,128)(2,1)S(1)}, u32[]{:S(2)}, u32[]{:S(2)}) collective-permute-start(bf16[1,1,3,48,256]{4,3,2,1,0:T(8,128)(2,1)S(1)} %get-tuple-element.314), channel_id=1, source_target_pairs={{0,24},{1,25},{2,26},{3,27},{4,28},{5,29},{6,30},{7,31},{8,0},{9,1... | collective-permute-start | bytes 221192 | tf_op jit(solution)/shard_map/ppermute | solution.py:563
  18.5 7.7 %shard_map.482.t_ref = f32[12,128,2048]{2,1,0:T(8,128)} custom-call(f32[12,1,2048]{2,1,0:T(1,128)} %add.537.off_ref), custom_call_target="tpu_custom_call" | custom-call | bytes 24000000 | tf_op jit(solution)/shard_map/pallas_call | solution.py:60
  29.8 2.9 collective-permute-start.4
  46.7 2.1 collective-permute-start.10
  58.4 15.9 %shard_map.483 = (bf16[4,1024,1024]{2,1,0:T(8,128)(2,1)}, bf16[1024,768]{1,0:T(8,128)(2,1)}, f32[1024,768]{1,0:T(8,128)}, f32[1024,768]{1,0:T(8,128)}, bf16[3,10...) custom-call(s32[1]{0:T(128)S(6)} %copy.172.len_ref, s32[4]{0:T(128)} %pad_add_fusion.1.at_ref, ...), custom_call_target="tpu_custom_call" | custom-call | bytes 44400000 | tf_op jit(solution)/shard_map/pallas_call | solution.py:145
  79.4 16.0 %shard_map.484 = (bf16[4,1024,1024]{2,1,0:T(8,128)(2,1)}, bf16[1024,768]{1,0:T(8,128)(2,1)}, f32[1024,768]{1,0:T(8,128)}, f32[1024,768]{1,0:T(8,128)}, bf16[3,10...) custom-call(s32[1]{0:T(128)S(6)} %copy.172.len_ref, ...), custom_call_target="tpu_custom_call", output_to_operand_aliasing={{1}: (8, {}), {2}: (9, {}), {3}: (10, {})} | custom-call | bytes 44400000 | tf_op jit(solution)/shard_map/pallas_call | solution.py:145
  95.4 4.2 %collective-permute-done.12 = bf16[1,4,6,48,256]{4,3,2,1,0:T(8,128)(2,1)} collective-permute-done((bf16[1,4,6,48,256]{4,3,2,1,0:T(8,128)(2,1)S(1)}, bf16[1,4,6,48,256]{4,3,2,1,0:T(8,128)(2,1)}, u32[]{:S(2)}, u32[]{:S(2)}) %collective-permute-start.12) | collective-permute-done | bytes 589856 | tf_op jit(solution)/shard_map/ppermute | solution.py:563
  103.8 16.0 %shard_map.485 = (bf16[4,1024,1024]{2,1,0:T(8,128)(2,1)}, bf16[1024,768]{1,0:T(8,128)(2,1)}, f32[1024,768]{1,0:T(8,128)}, f32[1024,768]{1,0:T(8,128)}, bf16[3,10...) custom-call(s32[1]{0:T(128)S(6)} %copy.172.len_ref, ...), custom_call_target="tpu_custom_call", output_to_operand_aliasing={{1}: (8, {}), {2}: (9, {}), {3}: (10, {})} | custom-call | bytes 44400000 | tf_op jit(solution)/shard_map/pallas_call | solution.py:145
  119.9 2.3 all-gather.3.cloned.1.call-done
  123.8 41.2 %shard_map.486 = (bf16[1024,768]{1,0:T(8,128)(2,1)}, bf16[1024,3072]{1,0:T(8,128)(2,1)}, bf16[1024,3072]{1,0:T(8,128)(2,1)}, bf16[1024,768]{1,0:T(8,128)(2,1)}, ...) custom-call(s32[1]{0:T(128)S(6)} %copy.172.len_ref, ...), custom_call_target="tpu_custom_call" | custom-call | bytes 120000000 | tf_op jit(solution)/shard_map/pallas_call | solution.py:461
  165.0 15.0 %shard_map.487 = bf16[32,192,768]{2,1,0:T(8,128)(2,1)} custom-call(bf16[1024,3072]{1,0:T(8,128)(2,1)} %get-tuple-element.186.dh_ref, bf16[1024,3072]{1,0:T(8,128)(2,1)} %get-tuple-element.187.act_ref, bf16[1024,768]{1,0:T(8,128)(2,1)} %get-tuple-element.188.low_ref, bf16[1024,768]{1,0:T(8,128)(2,1)} %get-tuple-element.189.dlow_ref), custom_call_target="tpu_custom_call" | custom-call | bytes 48000000 | tf_op jit(solution)/shard_map/pallas_call | solution.py:298
  180.1 13.5 %shard_map.488 = (bf16[3,1024,256]{2,1,0:T(8,128)(2,1)}, f32[4,1,1024]{2,1,0:T(1,128)}, f32[4,1,2048]{2,1,0:T(1,128)}) custom-call(bf16[3,1024,256]{2,1,0:T(8,128)(2,1)} %get-tuple-element.185.q_ref.k_ref.v_ref, bf16[3,1024,256]{2,1,0:T(8,128)(2,1)} %get-tuple-element.185.q_ref.k_ref.v_ref, bf16[3,1024,256]{2,1,0:T(8,128)(2,1)} %get-tuple-element.185.q_ref.k_ref.v_ref, ...), custom_call_target="tpu_custom_call" | custom-call | bytes 36000000 | tf_op jit(solution)/shard_map/pallas_call | solution.py:227
  193.5 7.2 %shard_map.489 = bf16[768,1536]{1,0:T(8,128)(2,1)} custom-call(bf16[768,1024]{1,0:T(8,128)(2,1)} %fusion.118.xt_ref, bf16[3,1024,256]{2,1,0:T(8,128)(2,1)} %get-tuple-element.229.d_ref.d0_ref, bf16[1024,768]{1,0:T(8,128)(2,1)} %get-tuple-element.180.c_ref.a_ref, bf16[1024,768]{1,0:T(8,128)(2,1)} %get-tuple-element.195.b_ref), custom_call_target="tpu_custom_call" | custom-call | bytes 15000000 | tf_op jit(solution)/shard_map/pallas_call | solution.py:273
  200.8 2.5 dynamic-slice_bitcast_fusion.1
  203.5 13.3 %shard_map.490 = (bf16[3,1024,256]{2,1,0:T(8,128)(2,1)}, f32[4,1,1024]{2,1,0:T(1,128)}, f32[4,1,2048]{2,1,0:T(1,128)}) custom-call(bf16[3,1024,256]{2,1,0:T(8,128)(2,1)} %get-tuple-element.199.q_ref.k_ref.v_ref, bf16[3,1024,256]{2,1,0:T(8,128)(2,1)} %get-tuple-element.199.q_ref.k_ref.v_ref, bf16[3,1024,256]{2,1,0:T(8,128)(2,1)} %get-tuple-element.199.q_ref.k_ref.v_ref, ...), custom_call_target="tpu_custom_call" | custom-call | bytes 36000000 | tf_op jit(solution)/shard_map/pallas_call | solution.py:227
  216.9 2.5 fusion.5
  220.8 13.4 %shard_map.491 = (bf16[3,1024,256]{2,1,0:T(8,128)(2,1)}, f32[4,1,1024]{2,1,0:T(1,128)}, f32[4,1,2048]{2,1,0:T(1,128)}) custom-call(bf16[3,1024,256]{2,1,0:T(8,128)(2,1)} %get-tuple-element.207.q_ref.k_ref.v_ref, bf16[3,1024,256]{2,1,0:T(8,128)(2,1)} %get-tuple-element.207.q_ref.k_ref.v_ref, bf16[3,1024,256]{2,1,0:T(8,128)(2,1)} %get-tuple-element.207.q_ref.k_ref.v_ref, ...), custom_call_target="tpu_custom_call" | custom-call | bytes 36000000 | tf_op jit(solution)/shard_map/pallas_call | solution.py:227
  234.2 4.7 %collective-permute-done.16 = bf16[4,48,1536]{2,1,0:T(8,128)(2,1)} collective-permute-done((bf16[4,48,1536]{2,1,0:T(8,128)(2,1)}, bf16[4,48,1536]{2,1,0:T(8,128)(2,1)}, u32[]{:S(2)}, u32[]{:S(2)}) %collective-permute-start.16) | collective-permute-done | bytes 589856 | tf_op jit(solution)/shard_map/ppermute | solution.py:563
  239.5 6.4 %shard_map.492 = bf16[768,1536]{1,0:T(8,128)(2,1)} custom-call(bf16[768,1024]{1,0:T(8,128)(2,1)} %fusion.118.xt_ref, bf16[3,1024,256]{2,1,0:T(8,128)(2,1)} %get-tuple-element.205.d_ref.d1_ref, bf16[3,1024,256]{2,1,0:T(8,128)(2,1)} %get-tuple-element.213.a_ref.d2_ref, f32[8,128]{1,0:T(8,128)} %broadcast_in_dim.69.b_ref), custom_call_target="tpu_custom_call" | custom-call | bytes 15000000 | tf_op jit(solution)/shard_map/pallas_call | solution.py:273
  246.0 2.4 dynamic-slice_bitcast_fusion
  251.7 2.3 fusion.24
  255.7 2.2 collective-permute-start.20
  263.8 9.4 %shard_map.493 = (f32[1024,768]{1,0:T(8,128)}, f32[8,768]{1,0:T(8,128)}) custom-call(f32[1024,768]{1,0:T(8,128)} %get-tuple-element.228.dr_ref, bf16[3,1024,256]{2,1,0:T(8,128)(2,1)} %get-tuple-element.229.d_ref.d0_ref, bf16[3,1024,256]{2,1,0:T(8,128)(2,1)} %get-tuple-element.205.d_ref.d1_ref, bf16[3,1024,256]{2,1,0:T(8,128)(2,1)} %get-tuple-element.213.a_ref.d2_ref, ...), custom_call_target="tpu_custom_call" | custom-call | bytes 24000000 | tf_op jit(solution)/shard_map/pallas_call | solution.py:510
  274.8 8.3 %collective-permute-done.18 = bf16[4,48,1536]{2,1,0:T(8,128)(2,1)} collective-permute-done((bf16[4,48,1536]{2,1,0:T(8,128)(2,1)}, bf16[4,48,1536]{2,1,0:T(8,128)(2,1)}, u32[]{:S(2)}, u32[]{:S(2)}) %collective-permute-start.18) | collective-permute-done | bytes 589856 | tf_op jit(solution)/shard_map/ppermute | solution.py:563
  288.4 3.3 collective-permute-start.24
  293.0 4.1 %collective-permute-done.22 = bf16[48,1536]{1,0:T(8,128)(2,1)S(1)} collective-permute-done((bf16[48,1536]{1,0:T(8,128)(2,1)S(1)}, bf16[48,1536]{1,0:T(8,128)(2,1)S(1)}, u32[]{:S(2)}, u32[]{:S(2)}) %collective-permute-start.22) | collective-permute-done | bytes 147488 | tf_op jit(solution)/shard_map/ppermute | solution.py:563
  297.2 5.4 %collective-permute-done.23 = bf16[48,1536]{1,0:T(8,128)(2,1)S(1)} collective-permute-done((bf16[48,1536]{1,0:T(8,128)(2,1)S(1)}, bf16[48,1536]{1,0:T(8,128)(2,1)S(1)}, u32[]{:S(2)}, u32[]{:S(2)}) %collective-permute-start.23) | collective-permute-done | bytes 147488 | tf_op jit(solution)/shard_map/ppermute | solution.py:563
  313.0 3.7 %collective-permute-done.27 = bf16[192,768]{1,0:T(8,128)(2,1)S(1)} collective-permute-done((bf16[192,768]{1,0:T(8,128)(2,1)S(1)}, bf16[192,768]{1,0:T(8,128)(2,1)S(1)}, u32[]{:S(2)}, u32[]{:S(2)}) %collective-permute-start.27) | collective-permute-done | bytes 294944 | tf_op jit(solution)/shard_map/ppermute | solution.py:563
  326.7 3.1 collective-permute-start.32
  332.1 2.4 collective-permute-start.33
  334.6 2.8 collective-permute-done.33
  343.7 2.2 fusion.100
  (307 shorter events, 92.8 us)
Async XLA Ops:
  7.2 115.0 %all-gather.3.cloned.1.call-start = ((), (), s32[]{:S(2)}) async-start(), calls=%async_computation.2 | async-start | bytes 10137600 | tf_op jit(solution)/shard_map/all_gather | solution.py:650
  9.0 18.1 %collective-permute-start = (bf16[1,1,3,48,256]{4,3,2,1,0:T(8,128)(2,1)S(1)}, bf16[1,1,3,48,256]{4,3,2,1,0:T(8,128)(2,1)S(1)}, u32[]{:S(2)}, u32[]{:S(2)}) collective-permute-start(bf16[1,1,3,48,256]{4,3,2,1,0:T(8,128)(2,1)S(1)} %get-tuple-element.314), channel_id=1, source_target_pairs={{0,24},{1,25},{2,26},{3,27},{4,28},{5,29},{6,30},{7,31},{8,0},{9,1... | collective-permute-start | bytes 221192 | tf_op jit(solution)/shard_map/ppermute | solution.py:563
  14.0 13.1 %collective-permute-start.1 = (bf16[1,1,3,48,256]{4,3,2,1,0:T(8,128)(2,1)S(1)}, bf16[1,1,3,48,256]{4,3,2,1,0:T(8,128)(2,1)S(1)}, u32[]{:S(2)}, u32[]{:S(2)}) collective-permute-start(bf16[1,1,3,48,256]{4,3,2,1,0:T(8,128)(2,1)S(1)} %get-tuple-element.314), channel_id=1, source_target_pairs={{0,16},{1,17},{2,18},{3,19},{4,20},{5,21},{6,22},{7,23},{8,24},{9,... | collective-permute-start | bytes 221192 | tf_op jit(solution)/shard_map/ppermute | solution.py:563
  14.0 13.1 %collective-permute-start.2 = (bf16[1,1,3,48,256]{4,3,2,1,0:T(8,128)(2,1)S(1)}, bf16[1,1,3,48,256]{4,3,2,1,0:T(8,128)(2,1)S(1)}, u32[]{:S(2)}, u32[]{:S(2)}) collective-permute-start(bf16[1,1,3,48,256]{4,3,2,1,0:T(8,128)(2,1)S(1)} %get-tuple-element.314), channel_id=1, source_target_pairs={{0,8},{1,9},{2,10},{3,11},{4,12},{5,13},{6,14},{7,15},{8,16},{9,17... | collective-permute-start | bytes 221192 | tf_op jit(solution)/shard_map/ppermute | solution.py:563
  27.9 276.0 %reduce-scatter.2.cloned.1.call-start = ((), (), s32[]{:S(2)}) async-start(), calls=%async_computation.1 | async-start | bytes 10027008 | tf_op jit(solution)/shard_map/reduce_scatter | solution.py:715
  29.8 11.8 %collective-permute-start.4 = (bf16[1,1,3,48,256]{4,3,2,1,0:T(8,128)(2,1)}, bf16[1,1,3,48,256]{4,3,2,1,0:T(8,128)(2,1)}, u32[]{:S(2)}, u32[]{:S(2)}) collective-permute-start(bf16[1,1,3,48,256]{4,3,2,1,0:T(8,128)(2,1)} %get-tuple-element.146), channel_id=1, source_target_pairs={{0,24},{1,25},{2,26},{3,27},{4,28},{5,29},{6,30},{7,31},{8,0},{9,1... | collective-permute-start | bytes 221192 | tf_op jit(solution)/shard_map/ppermute | solution.py:563
  32.7 9.0 %collective-permute-start.5 = (bf16[1,1,3,48,256]{4,3,2,1,0:T(8,128)(2,1)}, bf16[1,1,3,48,256]{4,3,2,1,0:T(8,128)(2,1)}, u32[]{:S(2)}, u32[]{:S(2)}) collective-permute-start(bf16[1,1,3,48,256]{4,3,2,1,0:T(8,128)(2,1)} %get-tuple-element.146), channel_id=1, source_target_pairs={{0,16},{1,17},{2,18},{3,19},{4,20},{5,21},{6,22},{7,23},{8,24},{9,... | collective-permute-start | bytes 221192 | tf_op jit(solution)/shard_map/ppermute | solution.py:563
  33.8 7.9 %collective-permute-start.6 = (bf16[1,1,3,48,256]{4,3,2,1,0:T(8,128)(2,1)}, bf16[1,1,3,48,256]{4,3,2,1,0:T(8,128)(2,1)}, u32[]{:S(2)}, u32[]{:S(2)}) collective-permute-start(bf16[1,1,3,48,256]{4,3,2,1,0:T(8,128)(2,1)} %get-tuple-element.146), channel_id=1, source_target_pairs={{0,8},{1,9},{2,10},{3,11},{4,12},{5,13},{6,14},{7,15},{8,16},{9,17... | collective-permute-start | bytes 221192 | tf_op jit(solution)/shard_map/ppermute | solution.py:563
  34.7 9.8 %collective-permute-start.3 = (bf16[1,4,3,48,256]{4,3,2,1,0:T(8,128)(2,1)}, bf16[1,4,3,48,256]{4,3,2,1,0:T(8,128)(2,1)S(1)}, u32[]{:S(2)}, u32[]{:S(2)}) collective-permute-start(bf16[1,4,3,48,256]{4,3,2,1,0:T(8,128)(2,1)} %pad_maximum_fusion.4), channel_id=1, source_target_pairs={{0,4},{1,5},{2,6},{3,7},{4,0},{5,1},{6,2},{7,3},{8,12},{9,13},{10,... | collective-permute-start | bytes 884744 | tf_op jit(solution)/shard_map/ppermute | solution.py:563
  46.7 27.6 %collective-permute-start.10 = (bf16[1,1,6,48,256]{4,3,2,1,0:T(8,128)(2,1)}, bf16[1,1,6,48,256]{4,3,2,1,0:T(8,128)(2,1)}, u32[]{:S(2)}, u32[]{:S(2)}) collective-permute-start(bf16[1,1,6,48,256]{4,3,2,1,0:T(8,128)(2,1)} %pad_maximum_fusion.6), channel_id=1, source_target_pairs={{0,16},{1,17},{2,18},{3,19},{4,20},{5,21},{6,22},{7,23},{8,24},{9,... | collective-permute-start | bytes 442376 | tf_op jit(solution)/shard_map/ppermute | solution.py:563
  48.8 25.5 %collective-permute-start.11 = (bf16[1,1,6,48,256]{4,3,2,1,0:T(8,128)(2,1)}, bf16[1,1,6,48,256]{4,3,2,1,0:T(8,128)(2,1)}, u32[]{:S(2)}, u32[]{:S(2)}) collective-permute-start(bf16[1,1,6,48,256]{4,3,2,1,0:T(8,128)(2,1)} %pad_maximum_fusion.6), channel_id=1, source_target_pairs={{0,8},{1,9},{2,10},{3,11},{4,12},{5,13},{6,14},{7,15},{8,16},{9,17... | collective-permute-start | bytes 442376 | tf_op jit(solution)/shard_map/ppermute | solution.py:563
  50.8 23.5 %collective-permute-start.9 = (bf16[1,1,6,48,256]{4,3,2,1,0:T(8,128)(2,1)}, bf16[1,1,6,48,256]{4,3,2,1,0:T(8,128)(2,1)}, u32[]{:S(2)}, u32[]{:S(2)}) collective-permute-start(bf16[1,1,6,48,256]{4,3,2,1,0:T(8,128)(2,1)} %pad_maximum_fusion.6), channel_id=1, source_target_pairs={{0,24},{1,25},{2,26},{3,27},{4,28},{5,29},{6,30},{7,31},{8,0},{9,1... | collective-permute-start | bytes 442376 | tf_op jit(solution)/shard_map/ppermute | solution.py:563
  52.8 22.7 %collective-permute-start.8 = (bf16[1,4,3,48,256]{4,3,2,1,0:T(8,128)(2,1)S(1)}, bf16[1,4,3,48,256]{4,3,2,1,0:T(8,128)(2,1)}, u32[]{:S(2)}, u32[]{:S(2)}) collective-permute-start(bf16[1,4,3,48,256]{4,3,2,1,0:T(8,128)(2,1)S(1)} %pad_maximum_fusion.5), channel_id=1, source_target_pairs={{0,4},{1,5},{2,6},{3,7},{4,0},{5,1},{6,2},{7,3},{8,12},{9,13},{10,... | collective-permute-start | bytes 884744 | tf_op jit(solution)/shard_map/ppermute | solution.py:563
  76.6 23.0 %collective-permute-start.12 = (bf16[1,4,6,48,256]{4,3,2,1,0:T(8,128)(2,1)S(1)}, bf16[1,4,6,48,256]{4,3,2,1,0:T(8,128)(2,1)}, u32[]{:S(2)}, u32[]{:S(2)}) collective-permute-start(bf16[1,4,6,48,256]{4,3,2,1,0:T(8,128)(2,1)S(1)} %pad_maximum_fusion.3), channel_id=1, source_target_pairs={{0,4},{1,5},{2,6},{3,7},{4,0},{5,1},{6,2},{7,3},{8,12},{9,13},{10,... | collective-permute-start | bytes 1769480 | tf_op jit(solution)/shard_map/ppermute | solution.py:563
  203.3 13.6 %collective-permute-start.15 = (bf16[4,2,48,1536]{3,2,1,0:T(8,128)(2,1)}, bf16[4,2,48,1536]{3,2,1,0:T(8,128)(2,1)S(1)}, u32[]{:S(2)}, u32[]{:S(2)}) collective-permute-start(bf16[4,2,48,1536]{3,2,1,0:T(8,128)(2,1)} %dynamic-slice_bitcast_fusion.1), channel_id=1, source_target_pairs={{0,2},{1,3},{2,0},{3,1},{4,6},{5,7},{6,4},{7,5},{8,10},{9,11},{10,... | collective-permute-start | bytes 3538952 | tf_op jit(solution)/shard_map/ppermute | solution.py:563
  219.4 19.5 %collective-permute-start.16 = (bf16[4,48,1536]{2,1,0:T(8,128)(2,1)}, bf16[4,48,1536]{2,1,0:T(8,128)(2,1)}, u32[]{:S(2)}, u32[]{:S(2)}) collective-permute-start(bf16[4,48,1536]{2,1,0:T(8,128)(2,1)} %fusion.5), channel_id=1, source_target_pairs={{0,4},{1,5},{2,6},{3,7},{4,0},{5,1},{6,2},{7,3},{8,12},{9,13},{10,... | collective-permute-start | bytes 1769480 | tf_op jit(solution)/shard_map/ppermute | solution.py:563
  248.4 3.4 collective-permute-start.17
  254.0 20.7 %collective-permute-start.19 = (bf16[48,1536]{1,0:T(8,128)(2,1)}, bf16[48,1536]{1,0:T(8,128)(2,1)}, u32[]{:S(2)}, u32[]{:S(2)}) collective-permute-start(bf16[48,1536]{1,0:T(8,128)(2,1)} %get-tuple-element.304), channel_id=1, source_target_pairs={{0,8},{1,9},{2,10},{3,11},{4,12},{5,13},{6,14},{7,15},{8,16},{9,17... | collective-permute-start | bytes 442376 | tf_op jit(solution)/shard_map/ppermute | solution.py:563
  255.7 19.0 %collective-permute-start.20 = (bf16[48,1536]{1,0:T(8,128)(2,1)}, bf16[48,1536]{1,0:T(8,128)(2,1)}, u32[]{:S(2)}, u32[]{:S(2)}) collective-permute-start(bf16[48,1536]{1,0:T(8,128)(2,1)} %get-tuple-element.303), channel_id=1, source_target_pairs={{0,16},{1,17},{2,18},{3,19},{4,20},{5,21},{6,22},{7,23},{8,24},{9,... | collective-permute-start | bytes 442376 | tf_op jit(solution)/shard_map/ppermute | solution.py:563
  258.0 16.8 %collective-permute-start.21 = (bf16[48,1536]{1,0:T(8,128)(2,1)S(1)}, bf16[48,1536]{1,0:T(8,128)(2,1)}, u32[]{:S(2)}, u32[]{:S(2)}) collective-permute-start(bf16[48,1536]{1,0:T(8,128)(2,1)S(1)} %get-tuple-element.302), channel_id=1, source_target_pairs={{0,24},{1,25},{2,26},{3,27},{4,28},{5,29},{6,30},{7,31},{8,0},{9,1... | collective-permute-start | bytes 442376 | tf_op jit(solution)/shard_map/ppermute | solution.py:563
  261.5 21.6 %collective-permute-start.18 = (bf16[4,48,1536]{2,1,0:T(8,128)(2,1)}, bf16[4,48,1536]{2,1,0:T(8,128)(2,1)}, u32[]{:S(2)}, u32[]{:S(2)}) collective-permute-start(bf16[4,48,1536]{2,1,0:T(8,128)(2,1)} %fusion.4), channel_id=1, source_target_pairs={{0,4},{1,5},{2,6},{3,7},{4,0},{5,1},{6,2},{7,3},{8,12},{9,13},{10,... | collective-permute-start | bytes 1769480 | tf_op jit(solution)/shard_map/ppermute | solution.py:563
  284.9 8.1 %collective-permute-start.25 = (bf16[48,1536]{1,0:T(8,128)(2,1)S(1)}, bf16[48,1536]{1,0:T(8,128)(2,1)S(1)}, u32[]{:S(2)}, u32[]{:S(2)}) collective-permute-start(bf16[48,1536]{1,0:T(8,128)(2,1)S(1)} %fusion.20), channel_id=1, source_target_pairs={{0,1},{1,0},{2,3},{3,2},{4,5},{5,4},{6,7},{7,6},{8,9},{9,8},{10,11... | collective-permute-start | bytes 442376 | tf_op jit(solution)/shard_map/ppermute | solution.py:563
  287.8 9.4 %collective-permute-start.22 = (bf16[48,1536]{1,0:T(8,128)(2,1)S(1)}, bf16[48,1536]{1,0:T(8,128)(2,1)S(1)}, u32[]{:S(2)}, u32[]{:S(2)}) collective-permute-start(bf16[48,1536]{1,0:T(8,128)(2,1)S(1)} %get-tuple-element.301), channel_id=1, source_target_pairs={{0,8},{1,9},{2,10},{3,11},{4,12},{5,13},{6,14},{7,15},{8,16},{9,17... | collective-permute-start | bytes 442376 | tf_op jit(solution)/shard_map/ppermute | solution.py:563
  288.4 14.2 %collective-permute-start.23 = (bf16[48,1536]{1,0:T(8,128)(2,1)S(1)}, bf16[48,1536]{1,0:T(8,128)(2,1)S(1)}, u32[]{:S(2)}, u32[]{:S(2)}) collective-permute-start(bf16[48,1536]{1,0:T(8,128)(2,1)S(1)} %get-tuple-element.300), channel_id=1, source_target_pairs={{0,16},{1,17},{2,18},{3,19},{4,20},{5,21},{6,22},{7,23},{8,24},{9,... | collective-permute-start | bytes 442376 | tf_op jit(solution)/shard_map/ppermute | solution.py:563
  288.4 14.2 %collective-permute-start.24 = (bf16[48,1536]{1,0:T(8,128)(2,1)S(1)}, bf16[48,1536]{1,0:T(8,128)(2,1)S(1)}, u32[]{:S(2)}, u32[]{:S(2)}) collective-permute-start(bf16[48,1536]{1,0:T(8,128)(2,1)S(1)} %get-tuple-element.299), channel_id=1, source_target_pairs={{0,24},{1,25},{2,26},{3,27},{4,28},{5,29},{6,30},{7,31},{8,0},{9,1... | collective-permute-start | bytes 442376 | tf_op jit(solution)/shard_map/ppermute | solution.py:563
  305.2 6.5 %collective-permute-start.26 = (bf16[48,1536]{1,0:T(8,128)(2,1)S(1)}, bf16[48,1536]{1,0:T(8,128)(2,1)S(1)}, u32[]{:S(2)}, u32[]{:S(2)}) collective-permute-start(bf16[48,1536]{1,0:T(8,128)(2,1)S(1)} %fusion.16), channel_id=1, source_target_pairs={{0,1},{1,0},{2,3},{3,2},{4,5},{5,4},{6,7},{7,6},{8,9},{9,8},{10,11... | collective-permute-start | bytes 442376 | tf_op jit(solution)/shard_map/ppermute | solution.py:563
  307.7 9.0 %collective-permute-start.27 = (bf16[192,768]{1,0:T(8,128)(2,1)S(1)}, bf16[192,768]{1,0:T(8,128)(2,1)S(1)}, u32[]{:S(2)}, u32[]{:S(2)}) collective-permute-start(bf16[192,768]{1,0:T(8,128)(2,1)S(1)} %dynamic-slice_bitcast_fusion.2), channel_id=1, source_target_pairs={{0,1},{1,0},{2,3},{3,2},{4,5},{5,4},{6,7},{7,6},{8,9},{9,8},{10,11... | collective-permute-start | bytes 884744 | tf_op jit(solution)/shard_map/ppermute | solution.py:563
  319.5 4.4 %collective-permute-start.29 = (f32[48,384]{1,0:T(8,128)S(1)}, f32[48,384]{1,0:T(8,128)S(1)}, u32[]{:S(2)}, u32[]{:S(2)}) collective-permute-start(f32[48,384]{1,0:T(8,128)S(1)} %pad_add_fusion), channel_id=1, source_target_pairs={{0,1},{1,0},{2,3},{3,2},{4,5},{5,4},{6,7},{7,6},{8,9},{9,8},{10,11... | collective-permute-start | bytes 221192 | tf_op jit(solution)/shard_map/ppermute | solution.py:563
  320.7 5.2 %collective-permute-start.30 = (f32[48,384]{1,0:T(8,128)S(1)}, f32[48,384]{1,0:T(8,128)S(1)}, u32[]{:S(2)}, u32[]{:S(2)}) collective-permute-start(f32[48,384]{1,0:T(8,128)S(1)} %pad_add_fusion), channel_id=1, source_target_pairs={{0,4},{1,5},{2,6},{3,7},{4,0},{5,1},{6,2},{7,3},{8,12},{9,13},{10,... | collective-permute-start | bytes 221192 | tf_op jit(solution)/shard_map/ppermute | solution.py:563
  321.3 5.3 %collective-permute-start.31 = (f32[48,384]{1,0:T(8,128)S(1)}, f32[48,384]{1,0:T(8,128)S(1)}, u32[]{:S(2)}, u32[]{:S(2)}) collective-permute-start(f32[48,384]{1,0:T(8,128)S(1)} %pad_add_fusion), channel_id=1, source_target_pairs={{0,5},{1,4},{2,7},{3,6},{4,1},{5,0},{6,3},{7,2},{8,13},{9,12},{10,... | collective-permute-start | bytes 221192 | tf_op jit(solution)/shard_map/ppermute | solution.py:563
  326.7 5.5 %collective-permute-start.32 = (f32[48,384]{1,0:T(8,128)S(1)}, f32[48,384]{1,0:T(8,128)S(1)}, u32[]{:S(2)}, u32[]{:S(2)}) collective-permute-start(f32[48,384]{1,0:T(8,128)S(1)} %add_add_fusion), channel_id=1, source_target_pairs={{0,8},{1,9},{2,10},{3,11},{4,12},{5,13},{6,14},{7,15},{8,0},{9,1},... | collective-permute-start | bytes 221192 | tf_op jit(solution)/shard_map/ppermute | solution.py:563
  332.1 5.3 %collective-permute-start.33 = (f32[48,384]{1,0:T(8,128)S(1)}, f32[48,384]{1,0:T(8,128)S(1)}, u32[]{:S(2)}, u32[]{:S(2)}) collective-permute-start(f32[48,384]{1,0:T(8,128)S(1)} %add.609), channel_id=1, source_target_pairs={{0,16},{1,17},{2,18},{3,19},{4,20},{5,21},{6,22},{7,23},{8,24},{9,... | collective-permute-start | bytes 221192 | tf_op jit(solution)/shard_map/ppermute | solution.py:563
  (65 other events, 353.6 us)
Sparse Core Ops, SparseCore 0:
  28.0 94.1 all-gather.2
  180.2 121.1 reduce-scatter.1
